TPU v7x, 32 devices: a whole 2x2x4 slice. The times are simulated.
32 devices in a mesh: ctx: 4 (over y, core), exp: 8 (over z, x).
Axes of the slice: x: 2, y: 2, z: 4, core: 2. Of those that a mesh axis runs over, the one named last changes fastest.
Arguments:
- hits: bfloat16 [4096, 2048], P(('ctx', 'exp')), may hold values from -6 to 6
- cotangent: bfloat16 [4096, 2048], P(('ctx', 'exp')), may hold values from -6 to 6
- combine: float32 [4096, 2], P(('ctx', 'exp')), may hold values from 0.1 to 1
- expert_ids: int32 [4096, 2], P(('ctx', 'exp')), may hold values from 0 to 7, all different within a row; in each aligned block of 128 rows (0 to 127, 128 to 255, ...) at most 48 rows name the same one
- gate_weight: bfloat16 [8, 2048, 768], P('exp'), may hold values from -0.125 to 0.125
- up_weight: bfloat16 [8, 2048, 768], P('exp'), may hold values from -0.125 to 0.125
- down_weight: bfloat16 [8, 2048, 768], P('exp'), may hold values from -0.21875 to 0.21875
Outputs:
- mixed: bfloat16 [4096, 2048], P(('ctx', 'exp'))
- input_grads: bfloat16 [4096, 2048], P(('ctx', 'exp'))
- combine_grads: float32 [4096, 2], P(('ctx', 'exp'))
- gate_grads: bfloat16 [8, 2048, 768], P('exp', 'ctx')
- up_grads: bfloat16 [8, 2048, 768], P('exp', 'ctx')
- down_grads: bfloat16 [8, 2048, 768], P('exp', 'ctx')
Inputs may be any that keep to these rules, and one draw needn't show every extreme that they name: `expert_ids`: the two ids of a hit differ. Among the 128 hits of one device no expert is named more than 48 times, and in every draw some device names some expert exactly 48 times.
All inputs are finite; a program needn't handle non-finite values.
Results may differ from a plain program's by a relative error of at most 0.017.
Values may be sent and summed in bfloat16 or wider, within the bound.
No kernel may reach another device: no remote copies, remote signals or barrier semaphores. Data moves between devices by JAX's collectives and lax.ppermute only.
A program may use at most 128 MiB of HBM per device.

v0:
```python
import jax
import jax.numpy as jnp
from jax import lax
from jax.sharding import PartitionSpec as P

grad_scale = 0.0625


def expert_pass(slot_hits, slot_cot, w_gate, w_up, w_down):
    contract_hidden = (((1,), (1,)), ((), ()))
    gate_value = jnp.dot(slot_hits, w_gate, preferred_element_type=jnp.float32)
    up_value = jnp.dot(slot_hits, w_up, preferred_element_type=jnp.float32)
    sigmoid_gate = jax.nn.sigmoid(gate_value)
    active = gate_value * sigmoid_gate
    hidden = (active * up_value).astype(jnp.bfloat16)
    outputs = lax.dot_general(
        hidden, w_down, contract_hidden, preferred_element_type=jnp.float32
    ).astype(jnp.bfloat16)
    grad_hidden = jnp.dot(slot_cot, w_down, preferred_element_type=jnp.float32)
    grad_up = (grad_hidden * active).astype(jnp.bfloat16)
    grad_gate = (
        grad_hidden * up_value * sigmoid_gate * (1.0 + gate_value * (1.0 - sigmoid_gate))
    ).astype(jnp.bfloat16)
    grad_input = lax.dot_general(
        grad_gate, w_gate, contract_hidden, preferred_element_type=jnp.float32
    )
    grad_input = grad_input + lax.dot_general(
        grad_up, w_up, contract_hidden, preferred_element_type=jnp.float32
    )
    return (outputs, grad_input.astype(jnp.bfloat16), hidden, grad_gate, grad_up)


def local(hits, cotangent, combine, expert_ids, gate_weight, up_weight, down_weight):
    tokens_here = hits.shape[0]
    model_width = hits.shape[1]
    experts = lax.axis_size("exp")
    capacity = 3 * tokens_here // experts
    routed = expert_ids.reshape(-1)
    owners = jnp.arange(2 * tokens_here, dtype=jnp.int32) // 2
    one_hot = (routed[:, None] == jnp.arange(experts, dtype=jnp.int32)[None, :]).astype(jnp.int32)
    before = jnp.cumsum(one_hot, axis=0) - one_hot
    slot_rank = jnp.sum(before * one_hot, axis=1)
    slot_index = routed * capacity + slot_rank
    scaled = (combine.reshape(-1)[:, None] * cotangent[owners].astype(jnp.float32)).astype(
        jnp.bfloat16
    )
    buffer_shape = (experts * capacity, model_width)
    send_hits = jnp.zeros(buffer_shape, jnp.bfloat16).at[slot_index].set(hits[owners])
    send_hits = send_hits.reshape(experts, capacity, model_width)
    send_cot = jnp.zeros(buffer_shape, jnp.bfloat16).at[slot_index].set(scaled)
    send_cot = send_cot.reshape(experts, capacity, model_width)
    w_gate = gate_weight[0]
    w_up = up_weight[0]
    w_down = down_weight[0]
    hidden_width = w_gate.shape[1]
    recv_hits = lax.all_to_all(send_hits, "exp", split_axis=0, concat_axis=0, tiled=True)
    recv_cot = lax.all_to_all(send_cot, "exp", split_axis=0, concat_axis=0, tiled=True)
    sources = recv_hits.shape[0]
    count_here = recv_hits.shape[1]
    flat_hits = recv_hits.reshape(sources * count_here, model_width)
    flat_cot = recv_cot.reshape(sources * count_here, model_width)
    outputs, grad_input, hidden, grad_gate, grad_up = expert_pass(
        flat_hits, flat_cot, w_gate, w_up, w_down
    )
    block_shape = (sources, count_here, model_width)
    back_out = lax.all_to_all(
        outputs.reshape(block_shape), "exp", split_axis=0, concat_axis=0, tiled=True
    )
    back_grad = lax.all_to_all(
        grad_input.reshape(block_shape), "exp", split_axis=0, concat_axis=0, tiled=True
    )
    inner_shape = (sources, count_here, hidden_width)
    back_out, back_grad, kept_hits, kept_cot, kept_hidden, kept_gate, kept_up = (
        back_out,
        back_grad,
        recv_hits,
        recv_cot,
        hidden.reshape(inner_shape),
        grad_gate.reshape(inner_shape),
        grad_up.reshape(inner_shape),
    )
    expert_out = (
        back_out.reshape(buffer_shape)[slot_index]
        .reshape(tokens_here, 2, model_width)
        .astype(jnp.float32)
    )
    mixed = jnp.sum(combine[:, :, None] * expert_out, axis=1).astype(jnp.bfloat16)
    combine_grads = jnp.sum(cotangent[:, None, :].astype(jnp.float32) * expert_out, axis=2)
    pair_grads = back_grad.reshape(buffer_shape)[slot_index].reshape(tokens_here, 2, model_width)
    input_grads = jnp.sum(pair_grads.astype(jnp.float32), axis=1).astype(jnp.bfloat16)
    row_total = kept_hits.shape[0] * kept_hits.shape[1]
    slot_rows = kept_hits.reshape(row_total, model_width)
    cot_rows = kept_cot.reshape(row_total, model_width)
    hidden_rows = kept_hidden.reshape(row_total, hidden_width)
    gate_rows = kept_gate.reshape(row_total, hidden_width)
    up_rows = kept_up.reshape(row_total, hidden_width)
    row_share = model_width // lax.axis_size("ctx")
    gate_term = jnp.einsum("rd,rf->df", slot_rows, gate_rows, preferred_element_type=jnp.float32)
    up_term = jnp.einsum("rd,rf->df", slot_rows, up_rows, preferred_element_type=jnp.float32)
    down_term = jnp.einsum("rd,rf->df", cot_rows, hidden_rows, preferred_element_type=jnp.float32)
    summed = lax.psum_scatter(
        jnp.concatenate([gate_term, up_term, down_term], axis=1).astype(jnp.bfloat16),
        "ctx",
        scatter_dimension=0,
        tiled=True,
    ).astype(jnp.float32)
    grad_parts = (
        summed[:, :hidden_width],
        summed[:, hidden_width : 2 * hidden_width],
        summed[:, 2 * hidden_width :],
    )
    gate_grads = (
        (grad_parts[0] * grad_scale).astype(jnp.bfloat16).reshape(1, row_share, hidden_width)
    )
    up_grads = (grad_parts[1] * grad_scale).astype(jnp.bfloat16).reshape(1, row_share, hidden_width)
    down_grads = (
        (grad_parts[2] * grad_scale).astype(jnp.bfloat16).reshape(1, row_share, hidden_width)
    )
    return (mixed, input_grads, combine_grads, gate_grads, up_grads, down_grads)


def solution(mesh):
    placed = (
        P(("ctx", "exp"), None),
        P(("ctx", "exp"), None),
        P(("ctx", "exp"), None),
        P(("ctx", "exp"), None),
        P("exp", None, None),
        P("exp", None, None),
        P("exp", None, None),
    )
    return jax.shard_map(
        local,
        mesh=mesh,
        in_specs=placed,
        out_specs=(
            P(("ctx", "exp"), None),
            P(("ctx", "exp"), None),
            P(("ctx", "exp"), None),
            P("exp", "ctx", None),
            P("exp", "ctx", None),
            P("exp", "ctx", None),
        ),
        check_vma=False,
    )
```

profile of v0, /device:TPU:0, one launch (start us, length us, event | category | flops | bytes accessed | tf_op | source)
XLA Modules:
  0.0 249.0 jit_solution(9460393541381594804)
XLA Ops:
  11.4 7.0 %scatter_custom_fusion.1 = bf16[384,2048]{1,0:T(8,128)(2,1)} fusion(s32[256]{0:T(256)S(1)} %bitcast.62, f32[256]{0:T(256)S(1)} %mul.87, bf16[]{:T(256)} %constant.27.clone.1, bf16[128,2048]{1,0:T(8,128)(2,1)} %param.8, s32[1024]{0:T(1024)S(1)} %pad_clamp_fusion.1), kind=kCustom, calls=%fused_computation.38 | custom fusion | flops 1572864 | bytes 2102274 | tf_op jit(solution)/shard_map/scatter | solution.py:50
  18.3 7.3 %all-to-all-start.2 = ((bf16[8,48,2048]{2,1,0:T(8,128)(2,1)}), bf16[8,48,2048]{2,1,0:T(8,128)(2,1)}, u32[]{:S(2)}, u32[]{:S(2)}) async-start(bf16[8,48,2048]{2,1,0:T(8,128)(2,1)} %bitcast.59), calls=%async_computation.2 | async-start | bytes 3145728 | tf_op jit(solution)/shard_map/all_to_all | solution.py:57
  25.6 6.9 %scatter_custom_fusion = bf16[384,2048]{1,0:T(8,128)(2,1)} fusion(s32[256]{0:T(256)S(1)} %bitcast.63, bf16[128,2048]{1,0:T(8,128)(2,1)} %param.7, s32[1024]{0:T(1024)S(1)} %pad_clamp_fusion.1, bf16[]{:T(256)} %constant.27.clone.1), kind=kCustom, calls=%fused_computation.39 | custom fusion | bytes 1573376 | tf_op jit(solution)/shard_map/scatter | solution.py:48
  32.5 30.2 %all-to-all-done.2 = bf16[8,48,2048]{2,1,0:T(8,128)(2,1)} async-done(((bf16[8,48,2048]{2,1,0:T(8,128)(2,1)}), bf16[8,48,2048]{2,1,0:T(8,128)(2,1)}, u32[]{:S(2)}, u32[]{:S(2)}) %all-to-all-start.2) | async-done | bytes 1572896 | tf_op jit(solution)/shard_map/all_to_all | solution.py:57
  62.7 4.3 %all-to-all-start = ((bf16[8,48,2048]{2,1,0:T(8,128)(2,1)}), bf16[8,48,2048]{2,1,0:T(8,128)(2,1)}, u32[]{:S(2)}, u32[]{:S(2)}) async-start(bf16[8,48,2048]{2,1,0:T(8,128)(2,1)} %bitcast.58), calls=%async_computation | async-start | bytes 3145728 | tf_op jit(solution)/shard_map/all_to_all | solution.py:56
  67.2 4.8 %fusion = f32[384,768]{1,0:T(8,128)} fusion(bf16[384,2048]{1,0:T(8,128)(2,1)} %bitcast.13, bf16[1,2048,768]{2,1,0:T(8,128)(2,1)} %param.13), kind=kOutput, calls=%fused_computation.10 | convolution fusion | flops 1207959552 | bytes 5898240 | tf_op jit(solution)/shard_map/dot_general | solution.py:19
  72.0 31.6 %all-to-all-done = bf16[8,48,2048]{2,1,0:T(8,128)(2,1)} async-done(((bf16[8,48,2048]{2,1,0:T(8,128)(2,1)}), bf16[8,48,2048]{2,1,0:T(8,128)(2,1)}, u32[]{:S(2)}, u32[]{:S(2)}) %all-to-all-start) | async-done | bytes 1572896 | tf_op jit(solution)/shard_map/all_to_all | solution.py:56
  103.6 3.8 %fusion.6 = f32[384,768]{1,0:T(8,128)S(1)} fusion(bf16[384,2048]{1,0:T(8,128)(2,1)} %bitcast.6, bf16[1,2048,768]{2,1,0:T(8,128)(2,1)} %param.12), kind=kOutput, calls=%fused_computation.16 | convolution fusion | flops 1207959552 | bytes 5898240 | tf_op jit(solution)/shard_map/dot_general | solution.py:12
  107.5 3.2 %multiply_convert_fusion.2 = (bf16[384,768]{1,0:T(8,128)(2,1)S(1)}, bf16[384,768]{1,0:T(8,128)(2,1)S(1)}, bf16[384,768]{1,0:T(8,128)(2,1)S(1)}) fusion(f32[384,768]{1,0:T(8,128)S(1)} %copy-done.5, f32[384,768]{1,0:T(8,128)S(1)} %fusion.6, bf16[384,2048]{1,0:T(8,128)(2,1)} %bitcast.6, bf16[1,2048,768]{2,1,0:T(8,128)(2,1)S(1)} %copy-done), kind=kOutput, calls=%fused_computation.34 | convolution fusion | flops 1212383232 | bytes 8847360 | tf_op jit(solution)/shard_map/dot_general | solution.py:11
  110.7 3.9 %convolution_convert_fusion = bf16[2048,768]{0,1:T(8,128)(2,1)S(1)} fusion(bf16[384,2048]{1,0:T(8,128)(2,1)} %bitcast.13, bf16[384,768]{1,0:T(8,128)(2,1)S(1)} %get-tuple-element.31), kind=kOutput, calls=%fused_computation.7 | convolution fusion | flops 1209532416 | bytes 5308416 | tf_op jit(solution)/shard_map/rd,rf->df/dot_general | solution.py:100
  114.6 3.3 %convolution_convert_fusion.1 = bf16[2048,768]{0,1:T(8,128)(2,1)S(1)} fusion(bf16[384,2048]{1,0:T(8,128)(2,1)} %bitcast.6, bf16[384,768]{1,0:T(8,128)(2,1)S(1)} %get-tuple-element.30), kind=kOutput, calls=%fused_computation.8 | convolution fusion | flops 1209532416 | bytes 5308416 | tf_op jit(solution)/shard_map/rd,rf->df/dot_general | solution.py:99
  117.9 3.3 %convolution_convert_fusion.2 = bf16[2048,768]{0,1:T(8,128)(2,1)S(1)} fusion(bf16[384,2048]{1,0:T(8,128)(2,1)} %bitcast.6, bf16[384,768]{1,0:T(8,128)(2,1)S(1)} %get-tuple-element.29), kind=kOutput, calls=%fused_computation.9 | convolution fusion | flops 1209532416 | bytes 5308416 | tf_op jit(solution)/shard_map/rd,rf->df/dot_general | solution.py:98
  121.2 4.5 %pad_maximum_fusion = bf16[2048,2304]{0,1:T(8,128)(2,1)} fusion(bf16[2048,768]{0,1:T(8,128)(2,1)S(1)} %convolution_convert_fusion, bf16[2048,768]{0,1:T(8,128)(2,1)S(1)} %convolution_convert_fusion.1, bf16[2048,768]{0,1:T(8,128)(2,1)S(1)} %convolution_convert_fusion.2), kind=kLoop, calls=%fused_computation.6 | loop fusion | flops 28311552 | bytes 18874368 | tf_op jit(solution)/shard_map/concatenate | solution.py:102
  125.7 4.7 %fusion.14 = bf16[384,2048]{1,0:T(8,128)(2,1)} fusion(bf16[384,768]{1,0:T(8,128)(2,1)} %copy-done.4, bf16[1,2048,768]{2,1,0:T(8,128)(2,1)} %param.13), kind=kOutput, calls=%fused_computation.23 | convolution fusion | flops 1208745984 | bytes 5308416 | tf_op jit(solution)/shard_map/dot_general | solution.py:16
  130.3 4.4 %all-to-all-start.1 = ((bf16[8,48,2048]{2,1,0:T(8,128)(2,1)}), bf16[8,48,2048]{2,1,0:T(8,128)(2,1)}, u32[]{:S(2)}, u32[]{:S(2)}) async-start(bf16[8,48,2048]{2,1,0:T(8,128)(2,1)} %bitcast.61), calls=%async_computation.1 | async-start | bytes 3145728 | tf_op jit(solution)/shard_map/all_to_all | solution.py:66
  134.8 4.4 %fusion.4 = f32[384,2048]{1,0:T(8,128)S(1)} fusion(bf16[384,768]{1,0:T(8,128)(2,1)} %copy-done.3, bf16[1,2048,768]{2,1,0:T(8,128)(2,1)} %param.12), kind=kOutput, calls=%fused_computation.14 | convolution fusion | flops 1207959552 | bytes 6881280 | tf_op jit(solution)/shard_map/dot_general | solution.py:27
  141.8 29.5 %all-to-all-done.1 = bf16[8,48,2048]{2,1,0:T(8,128)(2,1)} async-done(((bf16[8,48,2048]{2,1,0:T(8,128)(2,1)}), bf16[8,48,2048]{2,1,0:T(8,128)(2,1)}, u32[]{:S(2)}, u32[]{:S(2)}) %all-to-all-start.1) | async-done | bytes 1572896 | tf_op jit(solution)/shard_map/all_to_all | solution.py:66
  171.3 4.5 %all-to-all-start.3 = ((bf16[8,48,2048]{2,1,0:T(8,128)(2,1)}), bf16[8,48,2048]{2,1,0:T(8,128)(2,1)}, u32[]{:S(2)}, u32[]{:S(2)}) async-start(bf16[8,48,2048]{2,1,0:T(8,128)(2,1)} %bitcast.60), calls=%async_computation.3 | async-start | bytes 3145728 | tf_op jit(solution)/shard_map/all_to_all | solution.py:69
  177.9 5.1 %gather_fusion = bf16[256,2048]{1,0:T(8,128)(2,1)} fusion(bf16[384,2048]{1,0:T(8,128)(2,1)} %bitcast.11, s32[1024]{0:T(1024)S(1)} %pad_clamp_fusion), kind=kCustom, calls=%fused_computation.1 | custom fusion | bytes 2098176 | tf_op jit(solution)/shard_map/gather | solution.py:83
  183.0 3.4 %reshape.169 = f32[128,2,2048]{2,1,0:T(2,128)} reshape(bf16[256,2048]{1,0:T(8,128)(2,1)} %gather_fusion) | data formatting | bytes 3145728 | tf_op jit(solution)/shard_map/convert_element_type | solution.py:85
  186.4 25.8 %all-to-all-done.3 = bf16[8,48,2048]{2,1,0:T(8,128)(2,1)} async-done(((bf16[8,48,2048]{2,1,0:T(8,128)(2,1)}), bf16[8,48,2048]{2,1,0:T(8,128)(2,1)}, u32[]{:S(2)}, u32[]{:S(2)}) %all-to-all-start.3) | async-done | bytes 1572896 | tf_op jit(solution)/shard_map/all_to_all | solution.py:69
  212.2 5.0 %gather_fusion.1 = bf16[256,2048]{1,0:T(8,128)(2,1)} fusion(bf16[384,2048]{1,0:T(8,128)(2,1)} %bitcast.15, s32[1024]{0:T(1024)S(1)} %pad_clamp_fusion), kind=kCustom, calls=%fused_computation.3 | custom fusion | bytes 2098176 | tf_op jit(solution)/shard_map/gather | solution.py:89
  219.7 4.6 %reduce_sum.44 = bf16[128,2048]{1,0:T(8,128)(2,1)} reduce(bf16[128,2,2048]{2,1,0:T(2,128)(2,1)} %reshape.165, bf16[]{:T(256)} %constant.27.clone.1), dimensions={1}, to_apply=%region_6.7 | reduce | flops 262144 | bytes 1572866 | tf_op jit(solution)/shard_map/reduce_sum | solution.py:90
  224.3 6.3 %multiply_reduce_fusion = (f32[128,2]{1,0:T(8,128)S(1)}, bf16[128,2048]{1,0:T(8,128)(2,1)}) fusion(f32[128,2,2048]{2,1,0:T(2,128)} %reshape.169, f32[128,2048]{1,0:T(8,128)} %convert_element_type.72, f32[128,2]{1,0:T(8,128)S(1)} %copy.25), kind=kLoop, calls=%fused_computation.24 | loop fusion | flops 1834752 | bytes 3672064 | tf_op jit(solution)/shard_map/reduce_sum | solution.py:88
  (42 shorter events, 23.2 us)
Async XLA Ops:
  7.2 100.3 %copy-start = (bf16[1,2048,768]{2,1,0:T(8,128)(2,1)S(1)}, bf16[1,2048,768]{2,1,0:T(8,128)(2,1)}, u32[]{:S(2)}) copy-start(bf16[1,2048,768]{2,1,0:T(8,128)(2,1)} %param.11) | copy-start | bytes 9437188
  18.3 44.4 %all-to-all-start.2 = ((bf16[8,48,2048]{2,1,0:T(8,128)(2,1)}), bf16[8,48,2048]{2,1,0:T(8,128)(2,1)}, u32[]{:S(2)}, u32[]{:S(2)}) async-start(bf16[8,48,2048]{2,1,0:T(8,128)(2,1)} %bitcast.59), calls=%async_computation.2 | async-start | bytes 3145728 | tf_op jit(solution)/shard_map/all_to_all | solution.py:57
  62.7 40.9 %all-to-all-start = ((bf16[8,48,2048]{2,1,0:T(8,128)(2,1)}), bf16[8,48,2048]{2,1,0:T(8,128)(2,1)}, u32[]{:S(2)}, u32[]{:S(2)}) async-start(bf16[8,48,2048]{2,1,0:T(8,128)(2,1)} %bitcast.58), calls=%async_computation | async-start | bytes 3145728 | tf_op jit(solution)/shard_map/all_to_all | solution.py:56
  67.0 164.2 %reduce-scatter.2.cloned.1.call-start = ((), (), s32[]{:S(2)}) async-start(), calls=%async_computation.5 | async-start | bytes 11796480 | tf_op jit(solution)/shard_map/reduce_scatter | solution.py:101
  103.6 3.9 %copy-start.5 = (f32[384,768]{1,0:T(8,128)S(1)}, f32[384,768]{1,0:T(8,128)}, u32[]{:S(2)}) copy-start(f32[384,768]{1,0:T(8,128)} %fusion) | copy-start | bytes 3538948
  110.7 3.9 %copy-start.4 = (bf16[384,768]{1,0:T(8,128)(2,1)}, bf16[384,768]{1,0:T(8,128)(2,1)S(1)}, u32[]{:S(2)}) copy-start(bf16[384,768]{1,0:T(8,128)(2,1)S(1)} %get-tuple-element.31) | copy-start | bytes 1769476
  110.7 3.9 %copy-start.3 = (bf16[384,768]{1,0:T(8,128)(2,1)}, bf16[384,768]{1,0:T(8,128)(2,1)S(1)}, u32[]{:S(2)}) copy-start(bf16[384,768]{1,0:T(8,128)(2,1)S(1)} %get-tuple-element.30) | copy-start | bytes 1769476
  110.7 7.2 %copy-start.1 = (bf16[384,768]{1,0:T(8,128)(2,1)}, bf16[384,768]{1,0:T(8,128)(2,1)S(1)}, u32[]{:S(2)}) copy-start(bf16[384,768]{1,0:T(8,128)(2,1)S(1)} %get-tuple-element.29) | copy-start | bytes 1769476
  130.3 41.0 %all-to-all-start.1 = ((bf16[8,48,2048]{2,1,0:T(8,128)(2,1)}), bf16[8,48,2048]{2,1,0:T(8,128)(2,1)}, u32[]{:S(2)}, u32[]{:S(2)}) async-start(bf16[8,48,2048]{2,1,0:T(8,128)(2,1)} %bitcast.61), calls=%async_computation.1 | async-start | bytes 3145728 | tf_op jit(solution)/shard_map/all_to_all | solution.py:66
  134.8 4.5 %copy-start.2 = (bf16[384,768]{1,0:T(8,128)(2,1)S(1)}, bf16[384,768]{1,0:T(8,128)(2,1)}, u32[]{:S(2)}) copy-start(bf16[384,768]{1,0:T(8,128)(2,1)} %copy-done.1) | copy-start | bytes 1769476
  171.3 40.9 %all-to-all-start.3 = ((bf16[8,48,2048]{2,1,0:T(8,128)(2,1)}), bf16[8,48,2048]{2,1,0:T(8,128)(2,1)}, u32[]{:S(2)}, u32[]{:S(2)}) async-start(bf16[8,48,2048]{2,1,0:T(8,128)(2,1)} %bitcast.60), calls=%async_computation.3 | async-start | bytes 3145728 | tf_op jit(solution)/shard_map/all_to_all | solution.py:69
Sparse Core Ops, SparseCore 0:
  125.8 77.5 reduce-scatter.1
where the time goes:
time: 250 us; the launch traced here: 249 us
  waiting for transfers between devices  117 us (47%)
  matrix products  33.9 us (14%)
  local copies, waits for them, and re-layouts  32.9 us (13%)
  other arithmetic  30.1 us (12%)
  starting transfers between devices  20.7 us (8%)
  between operations  14.2 us (6%)
    all_to_all x1, waiting for transfers between devices, local(): lax.all_to_all(send_hits, 'exp', split_axis=0, concat_axis=0, tiled=True)  31.6 us
    all_to_all x1, waiting for transfers between devices, local(): lax.all_to_all(send_cot, 'exp', split_axis=0, concat_axis=0, tiled=True)  30.2 us
    all_to_all x1, waiting for transfers between devices, local(): lax.all_to_all(outputs.reshape(block_shape), 'exp', split_axis=0, concat_...  29.5 us
    all_to_all x1, waiting for transfers between devices, local(): lax.all_to_all(grad_input.reshape(block_shape), 'exp', split_axis=0, conc...  25.8 us
    unnamed x18, local copies, waits for them, and re-layouts  9.23 us
    all_to_all x1, starting transfers between devices, local(): lax.all_to_all(send_cot, 'exp', split_axis=0, concat_axis=0, tiled=True)  7.25 us
    scatter x1, other arithmetic, local(): send_cot = jnp.zeros(buffer_shape, jnp.bfloat16).at[slot_index].set(scaled)  6.96 us
    scatter x1, local copies, waits for them, and re-layouts, local(): jnp.zeros(buffer_shape, jnp.bfloat16).at[slot_index].set(hits[owners])  6.87 us
  transfers between devices with their start and end apart: 5, of which 4 were waited for; matrix products, arithmetic and copies ran while one was open for 21% of the time, Pallas kernels for 0%

commit v1 on v0

v1 whole, which is shorter than its diff:
```python
import jax
import jax.numpy as jnp
from jax import lax
from jax.sharding import PartitionSpec as P

grad_scale = 0.0625
f32 = jnp.float32
bf16 = jnp.bfloat16


def dot(a, b, dims=((1,), (0,))):
    return lax.dot_general(a, b, (dims, ((), ())), preferred_element_type=f32)


def exchange(x, axis, bit):
    size = lax.axis_size(axis)
    return lax.ppermute(x, axis, [(i, i ^ bit) for i in range(size)])


def within_half(blocks):
    return [blocks[0]] + [exchange(blocks[s], "exp", s) for s in range(1, len(blocks))]


def slot_plan(meta, half_experts, capacity):
    tokens = meta.shape[1]
    named = meta[:2, None, :] == half_experts.astype(f32)[None, :, None]
    either = (named[0] | named[1]).astype(bf16)
    place = jnp.arange(tokens)
    earlier = (place[:, None] < place[None, :]).astype(bf16)
    rank = dot(either, earlier)
    here = rank[:, None, :] == jnp.arange(capacity, dtype=f32)[None, :, None]
    return [(named[k][:, None, :] & here).astype(bf16).reshape(-1, tokens) for k in range(2)]


def gate_parts(gate, up):
    s = jax.nn.sigmoid(gate)
    active = gate * s
    return active, up * s * (1.0 + gate * (1.0 - s))


def scatter_sum(left, right):
    rows, width = left.shape
    size = lax.axis_size("ctx")
    me = lax.axis_index("ctx")
    share = width // size
    cols = left.reshape(rows, size // 2, 2, share)
    low = me % 2
    send_cols = lax.dynamic_index_in_dim(cols, 1 - low, 2, keepdims=False).reshape(rows, width // 2)
    keep_cols = lax.dynamic_index_in_dim(cols, low, 2, keepdims=False).reshape(rows, width // 2)
    send = dot(send_cols, right, ((0,), (0,))).astype(bf16)
    got = exchange(send, "ctx", 1)
    total = dot(keep_cols, right, ((0,), (0,))) + got.astype(f32)
    bit = 2
    while bit < size:
        groups = total.shape[0] // share
        parts = total.reshape(groups // 2, 2, share, -1)
        side = (me // bit) % 2
        send = lax.dynamic_index_in_dim(parts, 1 - side, 1, keepdims=False).reshape(groups // 2 * share, -1)
        keep = lax.dynamic_index_in_dim(parts, side, 1, keepdims=False).reshape(groups // 2 * share, -1)
        total = keep + exchange(send.astype(bf16), "ctx", bit).astype(f32)
        bit *= 2
    return total


def local(hits, cotangent, combine, expert_ids, gate_weight, up_weight, down_weight):
    tokens, width = hits.shape
    experts = lax.axis_size("exp")
    half = experts // 2
    capacity = 3 * tokens // experts
    me = lax.axis_index("exp")
    place = me % half
    half_experts = me - place + (place ^ jnp.arange(half, dtype=jnp.int32))
    w_gate, w_up, w_down = gate_weight[0], up_weight[0], down_weight[0]

    meta = jnp.concatenate([expert_ids.T.astype(f32), combine.T], axis=0)
    far_meta = exchange(meta, "exp", half)
    far_hits = exchange(hits, "exp", half)
    far_cot = exchange(cotangent, "exp", half)

    def weights_of(plan, m):
        return jnp.sum(plan[0].astype(f32) * m[2][None, :] + plan[1].astype(f32) * m[3][None, :], axis=1)

    def hit_slots(plan, x):
        return dot(plan[0] + plan[1], x).astype(bf16)

    def cot_slots(plan, m, x):
        return (weights_of(plan, m)[:, None] * dot(plan[0] + plan[1], x)).astype(bf16)

    def blocks_of(x):
        return [x[s * capacity : (s + 1) * capacity] for s in range(half)]

    def sum_out(plan, m, rows, cot):
        mixed, grads = 0.0, []
        for k in range(2):
            pair = dot(plan[k], rows, ((0,), (0,)))
            mixed = mixed + m[2 + k][:, None] * pair
            grads.append(jnp.sum(cot.astype(f32) * pair, axis=1))
        return mixed, jnp.stack(grads)

    own_plan = slot_plan(meta, half_experts, capacity)
    far_plan = slot_plan(far_meta, half_experts, capacity)

    own_send = jnp.concatenate([hit_slots(own_plan, hits), cot_slots(own_plan, meta, cotangent)], axis=1)
    own_rows = jnp.concatenate(within_half(blocks_of(own_send)), axis=0)
    x0, c0 = own_rows[:, :width], own_rows[:, width:]
    x1 = jnp.concatenate(within_half(blocks_of(hit_slots(far_plan, far_hits))), axis=0)
    c1 = jnp.concatenate(within_half(blocks_of(cot_slots(far_plan, far_meta, far_cot))), axis=0)

    def forward(x):
        gate, up = dot(x, w_gate), dot(x, w_up)
        active, slope = gate_parts(gate, up)
        hidden = (active * up).astype(bf16)
        return dot(hidden, w_down, ((1,), (1,))).astype(bf16), hidden, active, slope

    def backward(c, active, slope):
        grad_hidden = dot(c, w_down)
        grad_up = (grad_hidden * active).astype(bf16)
        grad_gate = (grad_hidden * slope).astype(bf16)
        grad_input = dot(grad_gate, w_gate, ((1,), (1,))) + dot(grad_up, w_up, ((1,), (1,)))
        return grad_input.astype(bf16), grad_gate, grad_up

    out0, hidden0, active0, slope0 = forward(x0)
    gin0, gg0, gu0 = backward(c0, active0, slope0)
    out1, hidden1, active1, slope1 = forward(x1)
    gin1, gg1, gu1 = backward(c1, active1, slope1)

    back_out1 = jnp.concatenate(within_half(blocks_of(out1)), axis=0)
    far_mixed, far_cg = sum_out(far_plan, far_meta, back_out1, far_cot)
    got_mixed = exchange(far_mixed.astype(bf16), "exp", half)
    got_cg = exchange(far_cg, "exp", half)
    back_gin1 = jnp.concatenate(within_half(blocks_of(gin1)), axis=0)
    far_gin = dot(far_plan[0] + far_plan[1], back_gin1, ((0,), (0,)))
    got_gin = exchange(far_gin.astype(bf16), "exp", half)

    back0 = jnp.concatenate(within_half(blocks_of(jnp.concatenate([out0, gin0], axis=1))), axis=0)
    own_mixed, own_cg = sum_out(own_plan, meta, back0[:, :width], cotangent)
    own_gin = dot(own_plan[0] + own_plan[1], back0[:, width:], ((0,), (0,)))

    mixed = (own_mixed + got_mixed.astype(f32)).astype(bf16)
    input_grads = (own_gin + got_gin.astype(f32)).astype(bf16)
    combine_grads = (own_cg + got_cg).T

    x = jnp.concatenate([x0, x1], axis=0)
    c = jnp.concatenate([c0, c1], axis=0)
    cat = lambda a, b: jnp.concatenate([a, b], axis=0)
    out = []
    for left, right in ((c, cat(hidden0, hidden1)), (x, cat(gg0, gg1)), (x, cat(gu0, gu1))):
        out.append((scatter_sum(left, right) * grad_scale).astype(bf16)[None])
    down_grads, gate_grads, up_grads = out
    return (mixed, input_grads, combine_grads, gate_grads, up_grads, down_grads)


def solution(mesh):
    rows = P(("ctx", "exp"), None)
    weight = P("exp", None, None)
    grads = P("exp", "ctx", None)
    return jax.shard_map(
        local,
        mesh=mesh,
        in_specs=(rows, rows, rows, rows, weight, weight, weight),
        out_specs=(rows, rows, rows, grads, grads, grads),
        check_vma=False,
    )
```

time: 250 us -> 250 us (level)
  other arithmetic: 30.1 us -> 11.4 us
  local copies, waits for them, and re-layouts: 32.9 us -> 48.7 us
  between operations: 14.2 us -> 1.39 us
  matrix products: 33.9 us -> 46.3 us
  starting transfers between devices: 20.7 us -> 30.9 us
  waiting for transfers between devices: 117 us -> 111 us
    all_to_all x4 -> x0, waiting for transfers between devices: 117 us -> none  [the longest x1 31.6 us: local(): lax.all_to_all(send_hits, 'exp', split_axis=0, concat_axis=0, tiled=True)]
    ppermute x0 -> x30, waiting for transfers between devices: none -> 111 us  [exchange(): return lax.ppermute(x, axis, [(i, i ^ bit) for i in range(size)])]
    ppermute x0 -> x30, starting transfers between devices: none -> 30.9 us  [exchange(): return lax.ppermute(x, axis, [(i, i ^ bit) for i in range(size)])]
    all_to_all x4 -> x0, starting transfers between devices: 20.5 us -> none  [the longest x1 7.25 us: local(): lax.all_to_all(send_cot, 'exp', split_axis=0, concat_axis=0, tiled=True)]
    unnamed x18 -> x113, local copies, waits for them, and re-layouts: 9.23 us -> 25.7 us
    dot_general x9 -> x30, matrix products: 33.9 us -> 46.3 us  [dot(): return lax.dot_general(a, b, (dims, ((), ())), preferred_element_type=f32)]
    dynamic_slice x0 -> x2, local copies, waits for them, and re-layouts: none -> 11.3 us  [scatter_sum(): lax.dynamic_index_in_dim(cols, low, 2, keepdims=False)]
    reduce_sum x3 -> x2, other arithmetic: 10.9 us -> 0.24 us  [weights_of(): jnp.sum(plan[0].astype(f32) * m[2][None, :] + plan[1].astype(f32) * m[3][...]
  transfers between devices with their start and end apart: 5 -> 30, of which waited for: 4 -> 17; matrix products, arithmetic and copies ran while one was open for 21% -> 38% of each run, Pallas kernels for 0% -> 0%
where the time goes in v1:
time: 250 us; the launch traced here: 249 us
  waiting for transfers between devices  111 us (44%)
  local copies, waits for them, and re-layouts  48.7 us (19%)
  matrix products  46.3 us (19%)
  starting transfers between devices  30.9 us (12%)
  other arithmetic  11.4 us (5%)
    ppermute x30, waiting for transfers between devices, exchange(): return lax.ppermute(x, axis, [(i, i ^ bit) for i in range(size)])  111 us
    dot_general x30, matrix products, dot(): return lax.dot_general(a, b, (dims, ((), ())), preferred_element_type=f32)  46.3 us
    ppermute x30, starting transfers between devices, exchange(): return lax.ppermute(x, axis, [(i, i ^ bit) for i in range(size)])  30.9 us
    unnamed x113, local copies, waits for them, and re-layouts  25.7 us
    dynamic_slice x2, local copies, waits for them, and re-layouts, scatter_sum(): lax.dynamic_index_in_dim(cols, low, 2, keepdims=False)  11.3 us
    reshape x2, local copies, waits for them, and re-layouts, scatter_sum(): cols = left.reshape(rows, size // 2, 2, share)  6.71 us
  transfers between devices with their start and end apart: 30, of which 17 were waited for; matrix products, arithmetic and copies ran while one was open for 38% of the time, Pallas kernels for 0%

profile of v1, /device:TPU:0, one launch (start us, length us, event | category | flops | bytes accessed | tf_op | source)
XLA Modules:
  0.0 249.3 jit_solution(5781732989386033468)
XLA Ops:
  2.3 4.0 %collective-permute-start.6 = (f32[4,128]{1,0:T(4,128)S(1)}, f32[4,128]{1,0:T(4,128)S(1)}, u32[]{:S(2)}, u32[]{:S(2)}) collective-permute-start(f32[4,128]{1,0:T(4,128)S(1)} %pad_maximum_fusion.25), channel_id=1, source_target_pairs={{0,4},{1,5},{2,6},{3,7},{4,0},{5,1},{6,2},{7,3},{8,12},{9,13},{10,... | collective-permute-start | bytes 6152 | tf_op jit(solution)/shard_map/ppermute | solution.py:17
  17.0 2.9 %collective-permute-start.15 = (bf16[128,2048]{1,0:T(8,128)(2,1)}, bf16[128,2048]{1,0:T(8,128)(2,1)}, u32[]{:S(2)}, u32[]{:S(2)}) collective-permute-start(bf16[128,2048]{1,0:T(8,128)(2,1)} %param.8), channel_id=1, source_target_pairs={{0,4},{1,5},{2,6},{3,7},{4,0},{5,1},{6,2},{7,3},{8,12},{9,13},{10,... | collective-permute-start | bytes 1572872 | tf_op jit(solution)/shard_map/ppermute | solution.py:17
  20.7 3.1 %collective-permute-done = bf16[48,4096]{1,0:T(8,128)(2,1)} collective-permute-done((bf16[48,4096]{1,0:T(8,128)(2,1)}, bf16[48,4096]{1,0:T(8,128)(2,1)}, u32[]{:S(2)}, u32[]{:S(2)}) %collective-permute-start) | collective-permute-done | bytes 393248 | tf_op jit(solution)/shard_map/ppermute | solution.py:17
  23.8 20.4 %collective-permute-done.1 = bf16[48,4096]{1,0:T(8,128)(2,1)} collective-permute-done((bf16[48,4096]{1,0:T(8,128)(2,1)}, bf16[48,4096]{1,0:T(8,128)(2,1)}, u32[]{:S(2)}, u32[]{:S(2)}) %collective-permute-start.1) | collective-permute-done | bytes 393248 | tf_op jit(solution)/shard_map/ppermute | solution.py:17
  44.1 4.9 %collective-permute-done.2 = bf16[48,4096]{1,0:T(8,128)(2,1)} collective-permute-done((bf16[48,4096]{1,0:T(8,128)(2,1)}, bf16[48,4096]{1,0:T(8,128)(2,1)}, u32[]{:S(2)}, u32[]{:S(2)}) %collective-permute-start.2) | collective-permute-done | bytes 393248 | tf_op jit(solution)/shard_map/ppermute | solution.py:17
  74.2 4.4 %collective-permute-done.17 = bf16[48,2048]{1,0:T(8,128)(2,1)S(1)} collective-permute-done((bf16[48,2048]{1,0:T(8,128)(2,1)S(1)}, bf16[48,2048]{1,0:T(8,128)(2,1)S(1)}, u32[]{:S(2)}, u32[]{:S(2)}) %collective-permute-start.17) | collective-permute-done | bytes 196640 | tf_op jit(solution)/shard_map/ppermute | solution.py:17
  79.3 3.0 %collective-permute-done.18 = bf16[48,2048]{1,0:T(8,128)(2,1)S(1)} collective-permute-done((bf16[48,2048]{1,0:T(8,128)(2,1)S(1)}, bf16[48,2048]{1,0:T(8,128)(2,1)S(1)}, u32[]{:S(2)}, u32[]{:S(2)}) %collective-permute-start.18) | collective-permute-done | bytes 196640 | tf_op jit(solution)/shard_map/ppermute | solution.py:17
  83.8 3.8 %reshape.166 = bf16[384,2,2,512]{3,2,1,0:T(2,128)(2,1)} reshape(bf16[384,2048]{1,0:T(8,128)(2,1)} %constant_dynamic-update-slice_fusion.4) | data formatting | bytes 3145728 | tf_op jit(solution)/shard_map/reshape | solution.py:46
  87.6 6.8 %constant_dynamic-slice_fusion.1 = (bf16[384,2,1,512]{3,2,1,0:T(2,128)(2,1)}, bf16[384,2,1,512]{3,2,1,0:T(2,128)(2,1)}) fusion(bf16[384,2,2,512]{3,2,1,0:T(2,128)(2,1)} %reshape.166, s32[]{:T(128)S(6)} %select_n.53, s32[]{:T(128)S(6)} %select_n.54), kind=kLoop, calls=%fused_computation.171 | loop fusion | bytes 3145736 | tf_op jit(solution)/shard_map/jit(dynamic_index_in_dim)/dynamic_slice | solution.py:49
  94.4 4.7 %copy.24 = bf16[384,2,1,512]{0,3,1,2:T(8,128)(2,1)} copy(bf16[384,2,1,512]{3,2,1,0:T(2,128)(2,1)} %get-tuple-element.13) | data formatting | bytes 1572864
  99.1 2.8 %collective-permute-start.5 = (bf16[48,4096]{1,0:T(8,128)(2,1)}, bf16[48,4096]{1,0:T(8,128)(2,1)}, u32[]{:S(2)}, u32[]{:S(2)}) collective-permute-start(bf16[48,4096]{1,0:T(8,128)(2,1)} %get-tuple-element.20), channel_id=1, source_target_pairs={{0,3},{1,2},{2,1},{3,0},{4,7},{5,6},{6,5},{7,4},{8,11},{9,10},{10,... | collective-permute-start | bytes 1179656 | tf_op jit(solution)/shard_map/ppermute | solution.py:17
  101.9 3.2 %fusion.10 = f32[192,768]{1,0:T(8,128)S(1)} fusion(bf16[1,2048,768]{2,1,0:T(8,128)(2,1)} %param.12, bf16[48,2048]{1,0:T(8,128)(2,1)} %collective-permute-done.10, bf16[48,2048]{1,0:T(8,128)(2,1)} %collective-permute-done.9, bf16[48,2048]{1,0:T(8,128)(2,1)} %collective-permute-done.8, bf16[48,2048]{1,0:T(8,128)(2,1)} %get-tuple-element.41), kind=kOutput, calls=%fused_computation.10 | convolution fusion | flops 607125504 | bytes 4521984 | tf_op jit(solution)/shard_map/dot_general | solution.py:12
  113.2 2.8 %copy.23 = bf16[384,2,1,512]{0,3,1,2:T(8,128)(2,1)} copy(bf16[384,2,1,512]{3,2,1,0:T(2,128)(2,1)S(1)} %copy-done.8) | data formatting | bytes 1572864
  120.8 2.9 %reshape.159 = bf16[384,2,2,512]{3,2,1,0:T(2,128)(2,1)S(1)} reshape(bf16[384,2048]{1,0:T(8,128)(2,1)} %constant_dynamic-update-slice_fusion) | data formatting | bytes 3145728 | tf_op jit(solution)/shard_map/reshape | solution.py:46
  123.7 4.4 %constant_dynamic-slice_fusion.3 = (bf16[384,2,1,512]{3,2,1,0:T(2,128)(2,1)S(1)}, bf16[384,2,1,512]{3,2,1,0:T(2,128)(2,1)}) fusion(bf16[384,2,2,512]{3,2,1,0:T(2,128)(2,1)S(1)} %reshape.159, s32[]{:T(128)S(6)} %select_n.53, s32[]{:T(128)S(6)} %select_n.54), kind=kLoop, calls=%fused_computation.173 | loop fusion | bytes 3145736 | tf_op jit(solution)/shard_map/jit(dynamic_index_in_dim)/dynamic_slice | solution.py:49
  128.1 3.8 %copy.22 = bf16[384,2,1,512]{0,3,1,2:T(8,128)(2,1)S(1)} copy(bf16[384,2,1,512]{3,2,1,0:T(2,128)(2,1)} %get-tuple-element.17) | data formatting | bytes 1572864
  132.0 4.6 %fusion.8 = f32[192,2048]{1,0:T(8,128)} fusion(bf16[192,768]{1,0:T(8,128)(2,1)S(1)} %copy-done.19, bf16[1,2048,768]{2,1,0:T(8,128)(2,1)} %param.12), kind=kOutput, calls=%fused_computation.8 | convolution fusion | flops 603979776 | bytes 5013504 | tf_op jit(solution)/shard_map/dot_general | solution.py:12
  139.2 2.7 %copy.21 = bf16[384,2,1,512]{0,3,1,2:T(8,128)(2,1)} copy(bf16[384,2,1,512]{3,2,1,0:T(2,128)(2,1)S(1)} %get-tuple-element.16) | data formatting | bytes 1572864
  149.1 2.8 %collective-permute-start.13 = (bf16[48,2048]{1,0:T(8,128)(2,1)S(1)}, bf16[48,2048]{1,0:T(8,128)(2,1)S(1)}, u32[]{:S(2)}, u32[]{:S(2)}) collective-permute-start(bf16[48,2048]{1,0:T(8,128)(2,1)S(1)} %get-tuple-element.47), channel_id=1, source_target_pairs={{0,3},{1,2},{2,1},{3,0},{4,7},{5,6},{6,5},{7,4},{8,11},{9,10},{10,... | collective-permute-start | bytes 589832 | tf_op jit(solution)/shard_map/ppermute | solution.py:17
  156.9 5.0 %collective-permute-done.13 = bf16[48,2048]{1,0:T(8,128)(2,1)S(1)} collective-permute-done((bf16[48,2048]{1,0:T(8,128)(2,1)S(1)}, bf16[48,2048]{1,0:T(8,128)(2,1)S(1)}, u32[]{:S(2)}, u32[]{:S(2)}) %collective-permute-start.13) | collective-permute-done | bytes 196640 | tf_op jit(solution)/shard_map/ppermute | solution.py:17
  171.1 19.3 %collective-permute-done.14 = bf16[128,2048]{1,0:T(8,128)(2,1)S(1)} collective-permute-done((bf16[128,2048]{1,0:T(8,128)(2,1)S(1)}, bf16[128,2048]{1,0:T(8,128)(2,1)S(1)}, u32[]{:S(2)}, u32[]{:S(2)}) %collective-permute-start.14) | collective-permute-done | bytes 524320 | tf_op jit(solution)/shard_map/ppermute | solution.py:17
  203.3 11.2 %collective-permute-done.22 = bf16[128,2048]{1,0:T(8,128)(2,1)S(1)} collective-permute-done((bf16[128,2048]{1,0:T(8,128)(2,1)S(1)}, bf16[128,2048]{1,0:T(8,128)(2,1)S(1)}, u32[]{:S(2)}, u32[]{:S(2)}) %collective-permute-start.22) | collective-permute-done | bytes 524320 | tf_op jit(solution)/shard_map/ppermute | solution.py:17
  217.6 15.8 %collective-permute-done.27 = bf16[512,768]{1,0:T(8,128)(2,1)S(1)} collective-permute-done((bf16[512,768]{1,0:T(8,128)(2,1)S(1)}, bf16[512,768]{1,0:T(8,128)(2,1)S(1)}, u32[]{:S(2)}, u32[]{:S(2)}) %collective-permute-start.27) | collective-permute-done | bytes 786464 | tf_op jit(solution)/shard_map/ppermute | solution.py:17
  234.4 13.8 %collective-permute-done.25 = bf16[512,768]{1,0:T(8,128)(2,1)S(1)} collective-permute-done((bf16[512,768]{1,0:T(8,128)(2,1)S(1)}, bf16[512,768]{1,0:T(8,128)(2,1)S(1)}, u32[]{:S(2)}, u32[]{:S(2)}) %collective-permute-start.25) | collective-permute-done | bytes 786464 | tf_op jit(solution)/shard_map/ppermute | solution.py:17
  (214 shorter events, 95.0 us)
Async XLA Ops:
  13.5 10.3 %collective-permute-start = (bf16[48,4096]{1,0:T(8,128)(2,1)}, bf16[48,4096]{1,0:T(8,128)(2,1)}, u32[]{:S(2)}, u32[]{:S(2)}) collective-permute-start(bf16[48,4096]{1,0:T(8,128)(2,1)} %get-tuple-element.23), channel_id=1, source_target_pairs={{0,1},{1,0},{2,3},{3,2},{4,5},{5,4},{6,7},{7,6},{8,9},{9,8},{10,11... | collective-permute-start | bytes 1179656 | tf_op jit(solution)/shard_map/ppermute | solution.py:17
  15.3 28.8 %collective-permute-start.1 = (bf16[48,4096]{1,0:T(8,128)(2,1)}, bf16[48,4096]{1,0:T(8,128)(2,1)}, u32[]{:S(2)}, u32[]{:S(2)}) collective-permute-start(bf16[48,4096]{1,0:T(8,128)(2,1)} %get-tuple-element.25), channel_id=1, source_target_pairs={{0,2},{1,3},{2,0},{3,1},{4,6},{5,7},{6,4},{7,5},{8,10},{9,11},{10,... | collective-permute-start | bytes 1179656 | tf_op jit(solution)/shard_map/ppermute | solution.py:17
  16.9 32.1 %collective-permute-start.2 = (bf16[48,4096]{1,0:T(8,128)(2,1)}, bf16[48,4096]{1,0:T(8,128)(2,1)}, u32[]{:S(2)}, u32[]{:S(2)}) collective-permute-start(bf16[48,4096]{1,0:T(8,128)(2,1)} %get-tuple-element.24), channel_id=1, source_target_pairs={{0,3},{1,2},{2,1},{3,0},{4,7},{5,6},{6,5},{7,4},{8,11},{9,10},{10,... | collective-permute-start | bytes 1179656 | tf_op jit(solution)/shard_map/ppermute | solution.py:17
  17.0 46.4 %collective-permute-start.15 = (bf16[128,2048]{1,0:T(8,128)(2,1)}, bf16[128,2048]{1,0:T(8,128)(2,1)}, u32[]{:S(2)}, u32[]{:S(2)}) collective-permute-start(bf16[128,2048]{1,0:T(8,128)(2,1)} %param.8), channel_id=1, source_target_pairs={{0,4},{1,5},{2,6},{3,7},{4,0},{5,1},{6,2},{7,3},{8,12},{9,13},{10,... | collective-permute-start | bytes 1572872 | tf_op jit(solution)/shard_map/ppermute | solution.py:17
  19.9 47.9 %collective-permute-start.7 = (bf16[128,2048]{1,0:T(8,128)(2,1)}, bf16[128,2048]{1,0:T(8,128)(2,1)}, u32[]{:S(2)}, u32[]{:S(2)}) collective-permute-start(bf16[128,2048]{1,0:T(8,128)(2,1)} %param.7), channel_id=1, source_target_pairs={{0,4},{1,5},{2,6},{3,7},{4,0},{5,1},{6,2},{7,3},{8,12},{9,13},{10,... | collective-permute-start | bytes 1572872 | tf_op jit(solution)/shard_map/ppermute | solution.py:17
  59.5 88.8 %collective-permute-start.3 = (bf16[48,4096]{1,0:T(8,128)(2,1)}, bf16[48,4096]{1,0:T(8,128)(2,1)}, u32[]{:S(2)}, u32[]{:S(2)}) collective-permute-start(bf16[48,4096]{1,0:T(8,128)(2,1)} %get-tuple-element.19), channel_id=1, source_target_pairs={{0,1},{1,0},{2,3},{3,2},{4,5},{5,4},{6,7},{7,6},{8,9},{9,8},{10,11... | collective-permute-start | bytes 1179656 | tf_op jit(solution)/shard_map/ppermute | solution.py:17
  62.1 86.4 %collective-permute-start.4 = (bf16[48,4096]{1,0:T(8,128)(2,1)}, bf16[48,4096]{1,0:T(8,128)(2,1)}, u32[]{:S(2)}, u32[]{:S(2)}) collective-permute-start(bf16[48,4096]{1,0:T(8,128)(2,1)} %get-tuple-element.21), channel_id=1, source_target_pairs={{0,2},{1,3},{2,0},{3,1},{4,6},{5,7},{6,4},{7,5},{8,10},{9,11},{10,... | collective-permute-start | bytes 1179656 | tf_op jit(solution)/shard_map/ppermute | solution.py:17
  65.7 12.8 %collective-permute-start.17 = (bf16[48,2048]{1,0:T(8,128)(2,1)S(1)}, bf16[48,2048]{1,0:T(8,128)(2,1)S(1)}, u32[]{:S(2)}, u32[]{:S(2)}) collective-permute-start(bf16[48,2048]{1,0:T(8,128)(2,1)S(1)} %get-tuple-element.34), channel_id=1, source_target_pairs={{0,2},{1,3},{2,0},{3,1},{4,6},{5,7},{6,4},{7,5},{8,10},{9,11},{10,... | collective-permute-start | bytes 589832 | tf_op jit(solution)/shard_map/ppermute | solution.py:17
  67.7 14.7 %collective-permute-start.18 = (bf16[48,2048]{1,0:T(8,128)(2,1)S(1)}, bf16[48,2048]{1,0:T(8,128)(2,1)S(1)}, u32[]{:S(2)}, u32[]{:S(2)}) collective-permute-start(bf16[48,2048]{1,0:T(8,128)(2,1)S(1)} %get-tuple-element.33), channel_id=1, source_target_pairs={{0,3},{1,2},{2,1},{3,0},{4,7},{5,6},{6,5},{7,4},{8,11},{9,10},{10,... | collective-permute-start | bytes 589832 | tf_op jit(solution)/shard_map/ppermute | solution.py:17
  73.5 25.6 %collective-permute-start.10 = (bf16[48,2048]{1,0:T(8,128)(2,1)}, bf16[48,2048]{1,0:T(8,128)(2,1)}, u32[]{:S(2)}, u32[]{:S(2)}) collective-permute-start(bf16[48,2048]{1,0:T(8,128)(2,1)} %get-tuple-element.38), channel_id=1, source_target_pairs={{0,3},{1,2},{2,1},{3,0},{4,7},{5,6},{6,5},{7,4},{8,11},{9,10},{10,... | collective-permute-start | bytes 589832 | tf_op jit(solution)/shard_map/ppermute | solution.py:17
  78.6 23.3 %collective-permute-start.8 = (bf16[48,2048]{1,0:T(8,128)(2,1)}, bf16[48,2048]{1,0:T(8,128)(2,1)}, u32[]{:S(2)}, u32[]{:S(2)}) collective-permute-start(bf16[48,2048]{1,0:T(8,128)(2,1)} %get-tuple-element.40), channel_id=1, source_target_pairs={{0,1},{1,0},{2,3},{3,2},{4,5},{5,4},{6,7},{7,6},{8,9},{9,8},{10,11... | collective-permute-start | bytes 589832 | tf_op jit(solution)/shard_map/ppermute | solution.py:17
  82.4 19.5 %collective-permute-start.9 = (bf16[48,2048]{1,0:T(8,128)(2,1)}, bf16[48,2048]{1,0:T(8,128)(2,1)}, u32[]{:S(2)}, u32[]{:S(2)}) collective-permute-start(bf16[48,2048]{1,0:T(8,128)(2,1)} %get-tuple-element.39), channel_id=1, source_target_pairs={{0,2},{1,3},{2,0},{3,1},{4,6},{5,7},{6,4},{7,5},{8,10},{9,11},{10,... | collective-permute-start | bytes 589832 | tf_op jit(solution)/shard_map/ppermute | solution.py:17
  99.1 50.0 %collective-permute-start.5 = (bf16[48,4096]{1,0:T(8,128)(2,1)}, bf16[48,4096]{1,0:T(8,128)(2,1)}, u32[]{:S(2)}, u32[]{:S(2)}) collective-permute-start(bf16[48,4096]{1,0:T(8,128)(2,1)} %get-tuple-element.20), channel_id=1, source_target_pairs={{0,3},{1,2},{2,1},{3,0},{4,7},{5,6},{6,5},{7,4},{8,11},{9,10},{10,... | collective-permute-start | bytes 1179656 | tf_op jit(solution)/shard_map/ppermute | solution.py:17
  113.2 80.3 %collective-permute-start.28 = (bf16[1024,768]{1,0:T(8,128)(2,1)}, bf16[1024,768]{1,0:T(8,128)(2,1)}, u32[]{:S(2)}, u32[]{:S(2)}) collective-permute-start(bf16[1024,768]{1,0:T(8,128)(2,1)} %convolution_convert_fusion.3), channel_id=1, source_target_pairs={{0,8},{8,0},{16,24},{24,16},{1,9},{9,1},{17,25},{25,17},{2,10},{10... | collective-permute-start | bytes 4718600 | tf_op jit(solution)/shard_map/ppermute | solution.py:17
  138.7 58.8 %collective-permute-start.26 = (bf16[1024,768]{1,0:T(8,128)(2,1)}, bf16[1024,768]{1,0:T(8,128)(2,1)}, u32[]{:S(2)}, u32[]{:S(2)}) collective-permute-start(bf16[1024,768]{1,0:T(8,128)(2,1)} %convolution_convert_fusion.4), channel_id=1, source_target_pairs={{0,8},{8,0},{16,24},{24,16},{1,9},{9,1},{17,25},{25,17},{2,10},{10... | collective-permute-start | bytes 4718600 | tf_op jit(solution)/shard_map/ppermute | solution.py:17
  149.1 12.8 %collective-permute-start.13 = (bf16[48,2048]{1,0:T(8,128)(2,1)S(1)}, bf16[48,2048]{1,0:T(8,128)(2,1)S(1)}, u32[]{:S(2)}, u32[]{:S(2)}) collective-permute-start(bf16[48,2048]{1,0:T(8,128)(2,1)S(1)} %get-tuple-element.47), channel_id=1, source_target_pairs={{0,3},{1,2},{2,1},{3,0},{4,7},{5,6},{6,5},{7,4},{8,11},{9,10},{10,... | collective-permute-start | bytes 589832 | tf_op jit(solution)/shard_map/ppermute | solution.py:17
  156.3 11.3 %collective-permute-start.20 = (bf16[48,2048]{1,0:T(8,128)(2,1)S(1)}, bf16[48,2048]{1,0:T(8,128)(2,1)S(1)}, u32[]{:S(2)}, u32[]{:S(2)}) collective-permute-start(bf16[48,2048]{1,0:T(8,128)(2,1)S(1)} %get-tuple-element.44), channel_id=1, source_target_pairs={{0,2},{1,3},{2,0},{3,1},{4,6},{5,7},{6,4},{7,5},{8,10},{9,11},{10,... | collective-permute-start | bytes 589832 | tf_op jit(solution)/shard_map/ppermute | solution.py:17
  165.3 25.1 %collective-permute-start.14 = (bf16[128,2048]{1,0:T(8,128)(2,1)S(1)}, bf16[128,2048]{1,0:T(8,128)(2,1)S(1)}, u32[]{:S(2)}, u32[]{:S(2)}) collective-permute-start(bf16[128,2048]{1,0:T(8,128)(2,1)S(1)} %get-tuple-element.11), channel_id=1, source_target_pairs={{0,4},{1,5},{2,6},{3,7},{4,0},{5,1},{6,2},{7,3},{8,12},{9,13},{10,... | collective-permute-start | bytes 1572872 | tf_op jit(solution)/shard_map/ppermute | solution.py:17
  167.6 33.6 %collective-permute-start.24 = (bf16[1024,768]{1,0:T(8,128)(2,1)S(1)}, bf16[1024,768]{1,0:T(8,128)(2,1)S(1)}, u32[]{:S(2)}, u32[]{:S(2)}) collective-permute-start(bf16[1024,768]{1,0:T(8,128)(2,1)S(1)} %convolution_convert_fusion.5), channel_id=1, source_target_pairs={{0,8},{8,0},{16,24},{24,16},{1,9},{9,1},{17,25},{25,17},{2,10},{10... | collective-permute-start | bytes 4718600 | tf_op jit(solution)/shard_map/ppermute | solution.py:17
  170.0 22.8 %collective-permute-start.23 = (f32[2,128]{1,0:T(2,128)S(1)}, f32[2,128]{1,0:T(2,128)S(1)}, u32[]{:S(2)}, u32[]{:S(2)}) collective-permute-start(f32[2,128]{1,0:T(2,128)S(1)} %pad_maximum_fusion.26), channel_id=1, source_target_pairs={{0,4},{1,5},{2,6},{3,7},{4,0},{5,1},{6,2},{7,3},{8,12},{9,13},{10,... | collective-permute-start | bytes 3080 | tf_op jit(solution)/shard_map/ppermute | solution.py:17
  190.4 24.1 %collective-permute-start.22 = (bf16[128,2048]{1,0:T(8,128)(2,1)S(1)}, bf16[128,2048]{1,0:T(8,128)(2,1)S(1)}, u32[]{:S(2)}, u32[]{:S(2)}) collective-permute-start(bf16[128,2048]{1,0:T(8,128)(2,1)S(1)} %convolution_convert_fusion.2), channel_id=1, source_target_pairs={{0,4},{1,5},{2,6},{3,7},{4,0},{5,1},{6,2},{7,3},{8,12},{9,13},{10,... | collective-permute-start | bytes 1572872 | tf_op jit(solution)/shard_map/ppermute | solution.py:17
  195.9 20.5 %collective-permute-start.29 = (bf16[512,768]{1,0:T(8,128)(2,1)S(1)}, bf16[512,768]{1,0:T(8,128)(2,1)S(1)}, u32[]{:S(2)}, u32[]{:S(2)}) collective-permute-start(bf16[512,768]{1,0:T(8,128)(2,1)S(1)} %fusion.57), channel_id=1, source_target_pairs={{0,16},{8,24},{16,0},{24,8},{1,17},{9,25},{17,1},{25,9},{2,18},{10... | collective-permute-start | bytes 2359304 | tf_op jit(solution)/shard_map/ppermute | solution.py:17
  200.1 33.3 %collective-permute-start.27 = (bf16[512,768]{1,0:T(8,128)(2,1)S(1)}, bf16[512,768]{1,0:T(8,128)(2,1)S(1)}, u32[]{:S(2)}, u32[]{:S(2)}) collective-permute-start(bf16[512,768]{1,0:T(8,128)(2,1)S(1)} %fusion.56), channel_id=1, source_target_pairs={{0,16},{8,24},{16,0},{24,8},{1,17},{9,25},{17,1},{25,9},{2,18},{10... | collective-permute-start | bytes 2359304 | tf_op jit(solution)/shard_map/ppermute | solution.py:17
  202.3 45.9 %collective-permute-start.25 = (bf16[512,768]{1,0:T(8,128)(2,1)S(1)}, bf16[512,768]{1,0:T(8,128)(2,1)S(1)}, u32[]{:S(2)}, u32[]{:S(2)}) collective-permute-start(bf16[512,768]{1,0:T(8,128)(2,1)S(1)} %fusion.55), channel_id=1, source_target_pairs={{0,16},{8,24},{16,0},{24,8},{1,17},{9,25},{17,1},{25,9},{2,18},{10... | collective-permute-start | bytes 2359304 | tf_op jit(solution)/shard_map/ppermute | solution.py:17
  (57 other events, 385.5 us)

commit v2 on v1

v2 whole, which is shorter than its diff:
```python
import functools

import jax
import jax.numpy as jnp
from jax import lax
from jax.experimental import pallas as pl
from jax.experimental.pallas import tpu as pltpu
from jax.sharding import PartitionSpec as P

grad_scale = 0.0625
f32 = jnp.float32
bf16 = jnp.bfloat16
VMEM = pl.BlockSpec(memory_space=pltpu.VMEM)


def dot(a, b, dims=((1,), (0,))):
    return lax.dot_general(a, b, (dims, ((), ())), preferred_element_type=f32)


def exchange(x, axis, bit):
    size = lax.axis_size(axis)
    return lax.ppermute(x, axis, [(i, i ^ bit) for i in range(size)])


def within_half(blocks):
    return [blocks[0]] + [exchange(blocks[s], "exp", s) for s in range(1, len(blocks))]


def in_hbm(arrays):
    return list(arrays)


def result(shape, dtype):
    return jax.ShapeDtypeStruct(tuple(shape), dtype)


def params(**kw):
    return pltpu.CompilerParams(vmem_limit_bytes=24 * 1024 * 1024, **kw)


def cost(flops, bytes_accessed):
    return pl.CostEstimate(flops=1, bytes_accessed=1, transcendentals=0)


def after(value, *earlier):
    return lax.optimization_barrier((value, earlier))[0]


class Blocks:
    def __init__(self, half, capacity):
        self.half, self.capacity = half, capacity
        self.split = capacity % 16 == 0
        self.count = half if self.split else 1
        self.rows = half * capacity
        self.height = self.rows // self.count

    def shapes(self, width):
        return [result((self.height, width), bf16)] * self.count

    def send(self, arrays):
        if self.split:
            return within_half(arrays)
        blocks = [arrays[0][s * self.capacity : (s + 1) * self.capacity] for s in range(self.half)]
        return [jnp.concatenate(within_half(blocks), axis=0)]


def join(refs, cols=slice(None)):
    parts = [r[:, cols] for r in refs]
    return parts[0] if len(parts) == 1 else jnp.concatenate(parts, axis=0)


def store(refs, cols, value):
    height = refs[0].shape[0]
    for i, r in enumerate(refs):
        r[:, cols] = value[i * height : (i + 1) * height].astype(r.dtype)


def slot_plan(rows, form):
    tokens = rows[0].shape[1]
    me = lax.axis_index("exp")
    place = me % form.half
    slot = lax.broadcasted_iota(jnp.int32, (form.rows, 1), 0)
    block = jnp.zeros_like(slot)
    for i in range(1, form.half):
        block = block + (slot >= i * form.capacity).astype(jnp.int32)
    expert = (me - place + (block ^ place)).astype(f32)
    rank_here = (slot - block * form.capacity).astype(f32)
    first = (rows[0] == expert).astype(f32)
    second = (rows[1] == expert).astype(f32)
    row = lax.broadcasted_iota(jnp.int32, (tokens, tokens), 0)
    col = lax.broadcasted_iota(jnp.int32, (tokens, tokens), 1)
    earlier = (row < col).astype(f32).astype(bf16)
    rank = dot((first + second).astype(bf16), earlier)
    here = (rank == rank_here).astype(f32)
    return first * here, second * here


def pack_meta(ids, combine):
    pieces = []
    rest = combine
    for _ in range(3):
        top = lax.reduce_precision(rest, 8, 7)
        pieces.append(top)
        rest = rest - top
    packed = jnp.concatenate([ids.astype(f32)] + pieces, axis=1)
    return jnp.pad(packed, ((0, 0), (0, 128 - packed.shape[1]))).astype(bf16)


def packed_columns(ref):
    x = ref[...].astype(f32)
    return [x[:, k : k + 1] for k in range(2)] + [
        x[:, 2 + k : 3 + k] + x[:, 4 + k : 5 + k] + x[:, 6 + k : 7 + k] for k in range(2)
    ]


def packed_rows(ref):
    x = jnp.transpose(ref[...].astype(f32))
    return [x[k : k + 1] for k in range(2)] + [x[2 + k : 3 + k] + x[4 + k : 5 + k] + x[6 + k : 7 + k] for k in range(2)]


def plain_rows(ids_ref, combine_ref):
    ids = ids_ref[...].astype(f32)
    return [ids[0:1], ids[1:2], combine_ref[0:1, :], combine_ref[1:2, :]]


def chunks(width, step=512):
    step = min(step, width)
    return [slice(i, i + step) for i in range(0, width, step)]


def gather_kernel(form, scaled, width, plain, *refs):
    meta, refs = (plain_rows(*refs[:2]), refs[2:]) if plain else (packed_rows(refs[0]), refs[1:])
    inputs, outs = refs[: len(scaled)], refs[len(scaled) :]
    first, second = slot_plan(meta, form)
    either = (first + second).astype(bf16)
    weight = jnp.sum(first * meta[2] + second * meta[3], axis=1, keepdims=True)
    offset = 0
    for x, by_weight in zip(inputs, scaled):
        for cols in chunks(width):
            rows = dot(either, x[:, cols])
            if by_weight:
                rows = rows * weight
            store(outs, slice(offset + cols.start, offset + cols.stop), rows)
        offset += width


def meta_specs(meta, width):
    if len(meta) == 2:
        return [pl.BlockSpec(m.shape, lambda i: (0, 0)) for m in meta]
    return [pl.BlockSpec((meta[0].shape[0], 128), lambda i: (0, width // 128))]


def whole_spec(shape):
    return pl.BlockSpec(shape, lambda i: (0, 0))


def gather(form, meta, arrays, scaled, width):
    tokens = arrays[0].shape[0]
    total = width * len(arrays)
    out = pl.pallas_call(
        functools.partial(gather_kernel, form, scaled, width, len(meta) == 2),
        grid=(1,),
        out_shape=form.shapes(total),
        in_specs=meta_specs(meta, width) + [whole_spec((tokens, width)) for _ in arrays],
        out_specs=[whole_spec((form.height, total))] * form.count,
        compiler_params=params(),
        cost_estimate=cost(2 * form.rows * tokens * total, 4 * form.rows * total),
        name="gather_slots",
    )(*meta, *in_hbm(arrays))
    return list(out)


def back_kernel(form, offsets, plain, more, *refs):
    count = form.count
    if plain:
        meta, weights = plain_rows(*refs[:2]), [refs[2][:, k : k + 1] for k in range(2)]
        refs = refs[3:]
    else:
        meta, weights = packed_rows(refs[0]), packed_columns(refs[0])[2:]
        refs = refs[1:]
    cot_ref, rows, refs = refs[0], refs[1 : 1 + count], refs[1 + count :]
    others, outs = (list(refs[:2]), list(refs[2:])) if more else ([], list(refs))
    plan = [p.astype(bf16) for p in slot_plan(meta, form)]
    out_at, grad_at = offsets
    width = cot_ref.shape[1]

    def put(i, cols, value):
        if more:
            value = value + others[i][:, cols].astype(f32)
        outs[i][:, cols] = value.astype(outs[i].dtype)

    def put_grad(cols, value):
        if more:
            value = value + others[1][:, cols].astype(f32)
        outs[-1][:, cols] = value.astype(bf16)

    def put_sums(sums):
        if more:
            tail = others[0][:, width:].astype(f32)
            for k in range(2):
                outs[1][:, k : k + 1] = sums[k] + tail[:, k : k + 1] + tail[:, 2 + k : 3 + k] + tail[:, 4 + k : 5 + k]
            return
        lane = lax.broadcasted_iota(jnp.int32, (sums[0].shape[0], 128), 1)
        tail = jnp.zeros(lane.shape, f32)
        for k in range(2):
            rest = sums[k]
            for piece in range(3):
                top = rest.astype(bf16).astype(f32)
                tail = jnp.where(lane == 2 * piece + k, top, tail)
                rest = rest - top
        outs[0][:, width:] = tail.astype(bf16)

    if out_at is not None:
        sums = [0.0, 0.0]
        for cols in chunks(width):
            block = join(rows, slice(out_at + cols.start, out_at + cols.stop))
            mixed = 0.0
            cot = cot_ref[:, cols].astype(f32)
            for k in range(2):
                pair = dot(plan[k], block, ((0,), (0,)))
                mixed = mixed + weights[k] * pair
                sums[k] = sums[k] + jnp.sum(cot * pair, axis=1, keepdims=True)
            put(0, cols, mixed)
        put_sums(sums)
    if grad_at is not None:
        either = plan[0] + plan[1]
        for cols in chunks(width):
            block = join(rows, slice(grad_at + cols.start, grad_at + cols.stop))
            put_grad(cols, dot(either, block, ((0,), (0,))))


def back(form, meta, cot, rows, offsets, combine=None, others=()):
    tokens, width = cot.shape
    shapes = []
    if offsets[0] is not None:
        shapes += [result((tokens, width + (0 if others else 128)), bf16)]
    if others:
        shapes += [result((tokens, 2), f32)]
    if offsets[1] is not None:
        shapes += [result((tokens, width), bf16)]
    own = [] if combine is None else [combine]
    arrays = own + [cot] + list(rows) + list(others)
    return pl.pallas_call(
        functools.partial(back_kernel, form, offsets, combine is not None, len(others) > 0),
        grid=(1,),
        out_shape=shapes,
        in_specs=meta_specs(meta, width) + [whole_spec(a.shape) for a in arrays],
        out_specs=[whole_spec(x.shape) for x in shapes],
        compiler_params=params(),
        cost_estimate=cost(4 * form.rows * tokens * width, 4 * form.rows * width),
        name="sum_slots",
    )(*meta, *in_hbm(arrays))


def load_kernel(*refs):
    number = len(refs) // 2
    sems = refs[-1]
    copies = [pltpu.make_async_copy(refs[i].at[0], refs[number + i], sems.at[i]) for i in range(number)]
    for c in copies:
        c.start()
    for c in copies:
        c.wait()


def load(arrays):
    return pl.pallas_call(
        load_kernel,
        out_shape=[pltpu.VMEM(a.shape[1:], a.dtype) for a in arrays],
        in_specs=[pl.BlockSpec(memory_space=pl.ANY)] * len(arrays),
        out_specs=[VMEM] * len(arrays),
        scratch_shapes=[pltpu.SemaphoreType.DMA((len(arrays),))],
        compiler_params=params(),
        cost_estimate=cost(1, 1),
        name="load_weights",
    )(*arrays)


def in_vmem(arrays):
    return [pltpu.with_memory_space_constraint(a, pltpu.VMEM) for a in arrays]


def tiles(ff):
    return chunks(ff, 256 if ff % 256 == 0 else ff)


def add_to(acc, first, cols, value):
    if first:
        acc[:, cols] = value
    else:
        acc[:, cols] += value


def forward_kernel(count, *refs):
    x_refs, (gate_ref, up_ref, down_ref) = refs[:count], refs[count : count + 3]
    out_refs = refs[count + 3 : 2 * count + 3]
    hidden_ref, active_ref, slope_ref, acc = refs[2 * count + 3 :]
    x = join(x_refs)
    for step, inner in enumerate(tiles(hidden_ref.shape[1])):
        gate, up = dot(x, gate_ref[:, inner]), dot(x, up_ref[:, inner])
        s = jax.nn.sigmoid(gate)
        active = gate * s
        hidden = (active * up).astype(bf16)
        hidden_ref[:, inner] = hidden
        active_ref[:, inner] = active
        slope_ref[:, inner] = up * s * (1.0 + gate * (1.0 - s))
        for cols in chunks(acc.shape[1]):
            add_to(acc, step == 0, cols, dot(hidden, down_ref[cols, inner], ((1,), (1,))))
    store(out_refs, slice(None), acc[...])


def expert_call(kernel, form, inputs, weights, more, out_width, inner_types, name):
    width, ff = weights[0].shape
    rows = form.rows
    out_shape = form.shapes(out_width) + [jax.ShapeDtypeStruct((rows, ff), t) for t in inner_types]
    operands = [*inputs, *more]
    out = pl.pallas_call(
        functools.partial(kernel, form.count),
        out_shape=out_shape,
        in_specs=[VMEM] * (len(operands) + 3),
        out_specs=[VMEM] * len(out_shape),
        scratch_shapes=[pltpu.VMEM((rows, out_width), f32)],
        compiler_params=params(),
        cost_estimate=cost(6 * rows * width * ff, 6 * width * ff),
        name=name,
    )(*operands, *in_vmem(weights))
    return list(out[: form.count]), *out[form.count :]


def forward(form, x, *weights):
    return expert_call(forward_kernel, form, x, weights, [], weights[0].shape[0], [bf16, f32, f32], "expert_forward")


def backward_kernel(count, *refs):
    c_refs, (active_ref, slope_ref, gate_ref, up_ref, down_ref) = refs[:count], refs[count : count + 5]
    in_refs = refs[count + 5 : 2 * count + 5]
    gg_ref, gu_ref, acc = refs[2 * count + 5 :]
    c = join(c_refs)
    for step, inner in enumerate(tiles(gg_ref.shape[1])):
        grad_hidden = dot(c, down_ref[:, inner])
        gu = (grad_hidden * active_ref[:, inner]).astype(bf16)
        gg = (grad_hidden * slope_ref[:, inner]).astype(bf16)
        gu_ref[:, inner] = gu
        gg_ref[:, inner] = gg
        for cols in chunks(acc.shape[1]):
            back = dot(gg, gate_ref[cols, inner], ((1,), (1,))) + dot(gu, up_ref[cols, inner], ((1,), (1,)))
            add_to(acc, step == 0, cols, back)
    store(in_refs, slice(None), acc[...])


def backward(form, c, active, slope, *weights):
    more = [active, slope]
    return expert_call(backward_kernel, form, c, weights, more, weights[0].shape[0], [bf16, bf16], "expert_backward")


def both_kernel(count, *refs):
    in_refs, (gate_ref, up_ref, down_ref) = refs[:count], refs[count : count + 3]
    out_refs = refs[count + 3 : 2 * count + 3]
    hidden_ref, gg_ref, gu_ref, acc = refs[2 * count + 3 :]
    width = acc.shape[1] // 2
    x, c = join(in_refs, slice(0, width)), join(in_refs, slice(width, 2 * width))
    for step, inner in enumerate(tiles(hidden_ref.shape[1])):
        gate, up = dot(x, gate_ref[:, inner]), dot(x, up_ref[:, inner])
        s = jax.nn.sigmoid(gate)
        active = gate * s
        hidden = (active * up).astype(bf16)
        hidden_ref[:, inner] = hidden
        grad_hidden = dot(c, down_ref[:, inner])
        gu = (grad_hidden * active).astype(bf16)
        gg = (grad_hidden * up * s * (1.0 + gate * (1.0 - s))).astype(bf16)
        gu_ref[:, inner] = gu
        gg_ref[:, inner] = gg
        for cols in chunks(width):
            add_to(acc, step == 0, cols, dot(hidden, down_ref[cols, inner], ((1,), (1,))))
            back = slice(width + cols.start, width + cols.stop)
            grad = dot(gg, gate_ref[cols, inner], ((1,), (1,))) + dot(gu, up_ref[cols, inner], ((1,), (1,)))
            add_to(acc, step == 0, back, grad)
    store(out_refs, slice(None), acc[...])


def both(form, rows_in, *weights):
    return expert_call(both_kernel, form, rows_in, weights, [], 2 * weights[0].shape[0], [bf16] * 3, "expert_both")


def weight_kernel(counts, grads, adds, scale, beside, ids_ref, *refs):
    lefts = []
    for n in counts:
        lefts.append(join(refs[:n]))
        refs = refs[n:]
    number = 1 if beside else len(grads)
    outs, refs = refs[-number:], refs[:-number]
    if beside:
        ff = outs[0].shape[1] // len(grads)
        outs = [outs[0].at[:, i * ff : (i + 1) * ff] for i in range(len(grads))]
    rights, others = refs[: len(refs) - adds * len(grads)], refs[len(refs) - adds * len(grads) :]
    for i, (left, right) in enumerate(grads):
        rows = jnp.concatenate([rights[2 * right][...], rights[2 * right + 1][...]], axis=0)
        sums = dot(lefts[left], rows, ((0,), (0,)))
        for j in range(adds):
            sums = sums + others[j * len(grads) + i][...].astype(f32)
        if scale:
            sums = sums * grad_scale
        outs[i][...] = sums.astype(outs[i].dtype)


def weight_sums(form, ids, lefts, grads, share, adds=(), scale=False, dtype=bf16, beside=False):
    ff = grads[0][1][0].shape[1]
    steps = ids.shape[0]
    arrays, specs, counts = [], [], []
    for parts in lefts:
        counts.append(sum(len(p[0]) for p in parts))
        for held, part in parts:
            shares = held[0].shape[1] // share
            if part is None:
                part, blocks = 0, shares
            else:
                blocks = shares // 2
            arrays += held
            specs += [
                pl.BlockSpec((form.height, share), lambda i, ids_ref, at=part * blocks: (0, at + ids_ref[i]))
            ] * len(held)
    for _, pair in grads:
        arrays += pair
        specs += [pl.BlockSpec((form.rows, ff), lambda i, ids_ref: (0, 0))] * 2
    step = pl.BlockSpec((share, ff), lambda i, ids_ref: (i, 0))
    for group in adds:
        for array, column in group:
            arrays.append(array)
            specs.append(pl.BlockSpec((share, ff), lambda i, ids_ref, column=column: (i, column)))
    if beside:
        out_shape = [result((steps * share, len(grads) * ff), dtype)]
        out_specs = [pl.BlockSpec((share, len(grads) * ff), lambda i, ids_ref: (i, 0))]
    else:
        out_shape = [result((steps * share, ff), dtype)] * len(grads)
        out_specs = [step] * len(grads)
    return pl.pallas_call(
        functools.partial(weight_kernel, counts, [(g[0], i) for i, g in enumerate(grads)], len(adds), scale, beside),
        grid_spec=pltpu.PrefetchScalarGridSpec(
            num_scalar_prefetch=1, grid=(steps,), in_specs=specs, out_specs=out_specs
        ),
        out_shape=out_shape,
        compiler_params=params(),
        cost_estimate=cost(4 * form.rows * steps * share * ff, 4 * steps * share * ff),
        name="weight_sums",
    )(ids, *in_hbm(arrays))


def local(hits, cotangent, combine, expert_ids, gate_weight, up_weight, down_weight):
    tokens, width = hits.shape
    experts = lax.axis_size("exp")
    copies = lax.axis_size("ctx")
    half = experts // 2
    capacity = 3 * tokens // experts
    form = Blocks(half, capacity)
    far_hits = exchange(jnp.concatenate([hits, pack_meta(expert_ids, combine)], axis=1), "exp", half)
    far_cot = exchange(after(cotangent, far_hits), "exp", half)
    far_meta = (far_hits,)
    meta = (expert_ids.T, combine.T)

    weights = load([gate_weight, up_weight, down_weight])
    own_send = gather(form, after(meta, weights[0]), [hits, cotangent], (False, True), width)
    own = form.send(own_send)
    x1_sent = gather(form, after(far_meta, own_send[0]), [far_hits], (False,), width)
    x1 = form.send(x1_sent)
    back0, hidden0, gg0, gu0 = both(form, after(own, x1_sent[0]), *weights)
    out1, hidden1, active1, slope1 = forward(form, after(x1, hidden0), *weights)
    out1_back = form.send(out1)
    c1_sent = gather(form, after(far_meta, hidden1), [far_cot], (True,), width)
    c1 = form.send(c1_sent)
    (far_mixed,) = back(form, after(far_meta, c1_sent[0]), far_cot, out1_back, (0, None))
    got_mixed = exchange(far_mixed, "exp", half)

    share = width // copies
    order = [r for r in range(0, copies, 2)]
    order.sort(key=lambda r: [-(r >> b & 1) for b in range(1, copies.bit_length())])
    order = jnp.asarray(order, jnp.int32)
    here = lax.axis_index("ctx")
    on = copies // 4
    theirs, ours = here ^ 1 ^ order, here ^ order
    x_rows, c_rows = [(own, 0), (x1, None)], [(own, 1), (c1, None)]
    down = [(0, (hidden0, hidden1))]

    (down_low,) = weight_sums(form, after(theirs[:on], far_mixed, c1), [c_rows], down, share)
    down_got = exchange(down_low, "ctx", 1)
    back0_got = form.send(after(back0, down_low))
    (down_on,) = weight_sums(form, ours[:on], [c_rows], down, share, [[(down_got, 0)]])
    pad = jnp.zeros((share // 8, down_on.shape[1]), bf16)
    down_there = exchange(jnp.concatenate([down_on, pad], axis=0), "ctx", 2)
    gin1, gg1, gu1 = backward(form, after(c1, down_on), active1, slope1, *weights)
    gin1_back = form.send(gin1)
    gate, up = [(0, (gg0, gg1))], [(0, (gu0, gu1))]
    (gate_low,) = weight_sums(form, theirs[:on], [x_rows], gate, share)
    gate_got = exchange(gate_low, "ctx", 1)
    (down_low,) = weight_sums(form, after(theirs[on:], gate_low), [c_rows], down, share)
    down_got = exchange(down_low, "ctx", 1)
    (up_low,) = weight_sums(form, after(theirs[:on], down_low, back0_got, got_mixed), [x_rows], up, share)
    up_got = exchange(up_low, "ctx", 1)
    (both_on,) = weight_sums(
        form,
        after(ours[:on], up_low, down_there, down_got),
        [x_rows],
        gate + up,
        share,
        [[(gate_got, 0), (up_got, 0)]],
        beside=True,
    )
    both_there = exchange(both_on, "ctx", 2)
    (far_grad,) = back(form, after(far_meta, both_on), far_cot, gin1_back, (None, 0))
    got_grad = exchange(far_grad, "exp", half)

    last = copies == 4
    kind = dict(scale=last, dtype=bf16 if last else f32)

    def stay(sums):
        bit = 4
        while bit < copies:
            middle = sums.shape[0] // 2
            sums = sums[middle:] + exchange(sums[:middle].astype(bf16), "ctx", bit).astype(f32)
            bit *= 2
        return (sums if last else (sums * grad_scale).astype(bf16))[None]

    lows = weight_sums(form, after(theirs[on:], far_grad), [x_rows], gate + up, share)
    gate_got, up_got = [exchange(low, "ctx", 1) for low in lows]
    (down_sums,) = weight_sums(
        form, after(ours[on:], lows[0]), [c_rows], down, share, [[(down_got, 0)], [(down_there, 0)]], **kind
    )
    mixed, combine_grads, input_grads = back(
        form, after(meta, down_sums, gate_got, up_got), cotangent, back0_got, (0, width), combine, (got_mixed, got_grad)
    )
    gate_sums, up_sums = weight_sums(
        form,
        after(ours[on:], mixed),
        [x_rows],
        gate + up,
        share,
        [[(gate_got, 0), (up_got, 0)], [(both_there, 0), (both_there, 1)]],
        **kind,
    )
    return (mixed, input_grads, combine_grads, stay(gate_sums), stay(up_sums), stay(down_sums))


def solution(mesh):
    rows = P(("ctx", "exp"), None)
    weight = P("exp", None, None)
    grads = P("exp", "ctx", None)
    return jax.shard_map(
        local,
        mesh=mesh,
        in_specs=(rows, rows, rows, rows, weight, weight, weight),
        out_specs=(rows, rows, rows, grads, grads, grads),
        check_vma=False,
    )
```

time: 250 us -> 192 us (0.77)
  matrix products: 46.3 us -> 0 us
  Pallas kernels: 0 us -> 41.6 us
  local copies, waits for them, and re-layouts: 48.7 us -> 21.9 us
  waiting for transfers between devices: 111 us -> 91.4 us
  other arithmetic: 11.4 us -> 2.47 us
    dot_general x30 -> x0, matrix products: 46.3 us -> none  [dot(): return lax.dot_general(a, b, (dims, ((), ())), preferred_element_type=f32)]
    pallas_call x0 -> x19, Pallas kernels: none -> 41.6 us  [the longest x9 18.9 us: weight_sums(): pl.pallas_call(functools.partial(weight_kernel, counts, [(g[0], i) for i,...]
    ppermute x30, waiting for transfers between devices: 111 us -> 91.4 us  [exchange(): return lax.ppermute(x, axis, [(i, i ^ bit) for i in range(size)])]
    dynamic_slice x2 -> x0, local copies, waits for them, and re-layouts: 11.3 us -> none  [scatter_sum(): lax.dynamic_index_in_dim(cols, low, 2, keepdims=False)]
    reshape x2 -> x0, local copies, waits for them, and re-layouts: 6.71 us -> none  [scatter_sum(): cols = left.reshape(rows, size // 2, 2, share)]
    unnamed x113 -> x124, local copies, waits for them, and re-layouts: 25.7 us -> 20.5 us
    concatenate x5 -> x2, other arithmetic: 5.76 us -> 1.1 us  [the longest x1 1.09 us: local(): jnp.concatenate([hits, pack_meta(expert_ids, combine)], axis=1)]
    broadcast_in_dim x3 -> x0, other arithmetic: 3.2 us -> none  [local(): out.append((scatter_sum(left, right) * grad_scale).astype(bf16)[None])]
  transfers between devices with their start and end apart: 30 -> 30, of which waited for: 17 -> 14; matrix products, arithmetic and copies ran while one was open for 38% -> 1% of each run, Pallas kernels for 0% -> 17%
where the time goes in v2:
time: 192 us
  waiting for transfers between devices  91.4 us (48%)
  Pallas kernels  41.6 us (22%)
  starting transfers between devices  33.1 us (17%)
  local copies, waits for them, and re-layouts  21.9 us (11%)
  other arithmetic  2.47 us (1%)
    ppermute x30, waiting for transfers between devices, exchange(): return lax.ppermute(x, axis, [(i, i ^ bit) for i in range(size)])  91.4 us
    ppermute x30, starting transfers between devices, exchange(): return lax.ppermute(x, axis, [(i, i ^ bit) for i in range(size)])  33.1 us
    unnamed x124, local copies, waits for them, and re-layouts  20.5 us
    pallas_call x9, Pallas kernels, weight_sums(): pl.pallas_call(functools.partial(weight_kernel, counts, [(g[0], i) for i,...  18.9 us
    pallas_call x3, Pallas kernels, expert_call(): pl.pallas_call(functools.partial(kernel, form.count), out_shape=out_shape...  12.4 us
    pallas_call x3, Pallas kernels, back(): pl.pallas_call(functools.partial(back_kernel, form, offsets, combine is n...  6.41 us
  transfers between devices with their start and end apart: 30, of which 14 were waited for; matrix products, arithmetic and copies ran while one was open for 1% of the time, Pallas kernels for 17%

profile of v2, /device:TPU:0, one launch (start us, length us, event | category | flops | bytes accessed | tf_op | source)
XLA Modules:
  0.0 191.7 jit_solution(5960756657136752156)
XLA Ops:
  3.2 4.1 %collective-permute-start = (bf16[128,2176]{1,0:T(8,128)(2,1)S(1)}, bf16[128,2176]{1,0:T(8,128)(2,1)S(1)}, u32[]{:S(2)}, u32[]{:S(2)}) collective-permute-start(bf16[128,2176]{1,0:T(8,128)(2,1)S(1)} %fusion.1), channel_id=1, source_target_pairs={{0,4},{1,5},{2,6},{3,7},{4,0},{5,1},{6,2},{7,3},{8,12},{9,13},{10,... | collective-permute-start | bytes 1671176 | tf_op jit(solution)/shard_map/ppermute | solution.py:22
  14.1 2.1 %gather_slots.3 = (bf16[48,4096]{1,0:T(8,128)(2,1)S(1)}, bf16[48,4096]{1,0:T(8,128)(2,1)S(1)}, bf16[48,4096]{1,0:T(8,128)(2,1)S(1)}, bf16[48,4096]{1,0:T(8,128)(2,1)S(1)}) custom-call(s32[2,128]{1,0:T(2,128)S(1)} %bitcast.7, f32[2,128]{1,0:T(2,128)S(1)} %bitcast.5, bf16[128,2048]{1,0:T(8,128)(2,1)S(1)} %copy-done.29, bf16[128,2048]{1,0:T(8,128)(2,1)} %refs_3_.3), custom_call_target="tpu_custom_call" | custom-call | flops 1 | bytes 1 | tf_op jit(solution)/shard_map/gather_slots/pallas_call | solution.py:160
  19.7 12.3 %collective-permute-done.refs_0_.refs_1_ = bf16[128,2176]{1,0:T(8,128)(2,1)S(1)} collective-permute-done((bf16[128,2176]{1,0:T(8,128)(2,1)S(1)}, bf16[128,2176]{1,0:T(8,128)(2,1)S(1)}, u32[]{:S(2)}, u32[]{:S(2)}) %collective-permute-start) | collective-permute-done | bytes 557088 | tf_op jit(solution)/shard_map/ppermute | solution.py:22
  34.2 4.0 %collective-permute-start.5 = (bf16[48,2048]{1,0:T(8,128)(2,1)S(1)}, bf16[48,2048]{1,0:T(8,128)(2,1)S(1)}, u32[]{:S(2)}, u32[]{:S(2)}) collective-permute-start(bf16[48,2048]{1,0:T(8,128)(2,1)S(1)} %get-tuple-element.90), channel_id=1, source_target_pairs={{0,2},{1,3},{2,0},{3,1},{4,6},{5,7},{6,4},{7,5},{8,10},{9,11},{10,... | collective-permute-start | bytes 589832 | tf_op jit(solution)/shard_map/ppermute | solution.py:22
  38.2 4.8 %collective-permute-done.2.refs_2_ = bf16[48,4096]{1,0:T(8,128)(2,1)S(1)} collective-permute-done((bf16[48,4096]{1,0:T(8,128)(2,1)S(1)}, bf16[48,4096]{1,0:T(8,128)(2,1)S(1)}, u32[]{:S(2)}, u32[]{:S(2)}) %collective-permute-start.2) | collective-permute-done | bytes 393248 | tf_op jit(solution)/shard_map/ppermute | solution.py:22
  43.3 16.8 %collective-permute-done.3.refs_3_ = bf16[48,4096]{1,0:T(8,128)(2,1)S(1)} collective-permute-done((bf16[48,4096]{1,0:T(8,128)(2,1)S(1)}, bf16[48,4096]{1,0:T(8,128)(2,1)S(1)}, u32[]{:S(2)}, u32[]{:S(2)}) %collective-permute-start.3) | collective-permute-done | bytes 393248 | tf_op jit(solution)/shard_map/ppermute | solution.py:22
  60.1 5.5 %expert_both.1 = (bf16[48,4096]{1,0:T(8,128)(2,1)S(1)}, bf16[48,4096]{1,0:T(8,128)(2,1)S(1)}, bf16[48,4096]{1,0:T(8,128)(2,1)S(1)}, bf16[48,4096]{1,0:T(8,128)(2...) custom-call(bf16[48,4096]{1,0:T(8,128)(2,1)S(1)} %get-tuple-element.92.refs_0_, ...), custom_call_target="tpu_custom_call" | custom-call | flops 1 | bytes 1 | tf_op jit(solution)/shard_map/expert_both/pallas_call | solution.py:316
  67.9 3.3 %expert_forward.1 = (bf16[48,2048]{1,0:T(8,128)(2,1)S(1)}, bf16[48,2048]{1,0:T(8,128)(2,1)}, bf16[48,2048]{1,0:T(8,128)(2,1)S(1)}, bf16[48,2048]{1,0:T(8,128)(2,...) custom-call(bf16[48,2048]{1,0:T(8,128)(2,1)S(1)} %get-tuple-element.100.refs_0_.refs_4_, ...), custom_call_target="tpu_custom_call" | custom-call | flops 1 | bytes 1 | tf_op jit(solution)/shard_map/expert_forward/pallas_call | solution.py:316
  76.6 2.5 %collective-permute-start.13 = (bf16[48,2048]{1,0:T(8,128)(2,1)}, bf16[48,2048]{1,0:T(8,128)(2,1)S(1)}, u32[]{:S(2)}, u32[]{:S(2)}) collective-permute-start(bf16[48,2048]{1,0:T(8,128)(2,1)} %copy-done.58), channel_id=1, source_target_pairs={{0,3},{1,2},{2,1},{3,0},{4,7},{5,6},{6,5},{7,4},{8,11},{9,10},{10,... | collective-permute-start | bytes 589832 | tf_op jit(solution)/shard_map/ppermute | solution.py:22
  83.1 6.1 %collective-permute-done.11.refs_3_ = bf16[48,2048]{1,0:T(8,128)(2,1)} collective-permute-done((bf16[48,2048]{1,0:T(8,128)(2,1)}, bf16[48,2048]{1,0:T(8,128)(2,1)}, u32[]{:S(2)}, u32[]{:S(2)}) %collective-permute-start.11) | collective-permute-done | bytes 196640 | tf_op jit(solution)/shard_map/ppermute | solution.py:22
  97.1 2.5 %collective-permute-start.15 = (bf16[48,4096]{1,0:T(8,128)(2,1)S(1)}, bf16[48,4096]{1,0:T(8,128)(2,1)S(1)}, u32[]{:S(2)}, u32[]{:S(2)}) collective-permute-start(bf16[48,4096]{1,0:T(8,128)(2,1)S(1)} %copy-done.57), channel_id=1, source_target_pairs={{0,1},{1,0},{2,3},{3,2},{4,5},{5,4},{6,7},{7,6},{8,9},{9,8},{10,11... | collective-permute-start | bytes 1179656 | tf_op jit(solution)/shard_map/ppermute | solution.py:22
  105.3 3.6 %expert_backward.1 = (bf16[48,2048]{1,0:T(8,128)(2,1)S(1)}, bf16[48,2048]{1,0:T(8,128)(2,1)S(1)}, bf16[48,2048]{1,0:T(8,128)(2,1)S(1)}, bf16[48,2048]{1,0:T(8,12...) custom-call(bf16[48,2048]{1,0:T(8,128)(2,1)S(1)} %get-tuple-element.117.refs_4_.refs_0_, ...), custom_call_target="tpu_custom_call" | custom-call | flops 1 | bytes 1 | tf_op jit(solution)/shard_map/expert_backward/pallas_call | solution.py:316
  111.6 12.2 %collective-permute-done.18.refs_8_ = bf16[128,2176]{1,0:T(8,128)(2,1)S(1)} collective-permute-done((bf16[128,2176]{1,0:T(8,128)(2,1)S(1)}, bf16[128,2176]{1,0:T(8,128)(2,1)S(1)}, u32[]{:S(2)}, u32[]{:S(2)}) %collective-permute-start.18) | collective-permute-done | bytes 557088 | tf_op jit(solution)/shard_map/ppermute | solution.py:22
  123.9 5.5 %collective-permute-done.17.refs_7_ = bf16[48,4096]{1,0:T(8,128)(2,1)S(1)} collective-permute-done((bf16[48,4096]{1,0:T(8,128)(2,1)S(1)}, bf16[48,4096]{1,0:T(8,128)(2,1)S(1)}, u32[]{:S(2)}, u32[]{:S(2)}) %collective-permute-start.17) | collective-permute-done | bytes 393248 | tf_op jit(solution)/shard_map/ppermute | solution.py:22
  134.2 2.8 %weight_sums.14 = bf16[512,1536]{1,0:T(8,128)(2,1)} custom-call(s32[1]{0:T(128)} %get-tuple-element.136.ids_ref, bf16[48,4096]{1,0:T(8,128)(2,1)S(1)} %get-tuple-element.92.refs_0_, bf16[48,4096]{1,0:T(8,128)(2,1)S(1)} %collective-permute-done.1.refs_1_, bf16[48,4096]{1,0:T(8,128)(2,1)S(1)} %collective-permute-done.2.refs_2_, ...), custom_call_target="tpu_custom_call" | custom-call | flops 1 | bytes 1 | tf_op jit(solution)/shard_map/weight_sums/pallas_call | solution.py:435
  138.5 3.1 %collective-permute-start.23 = (bf16[48,2048]{1,0:T(8,128)(2,1)S(1)}, bf16[48,2048]{1,0:T(8,128)(2,1)S(1)}, u32[]{:S(2)}, u32[]{:S(2)}) collective-permute-start(bf16[48,2048]{1,0:T(8,128)(2,1)S(1)} %get-tuple-element.139), channel_id=1, source_target_pairs={{0,1},{1,0},{2,3},{3,2},{4,5},{5,4},{6,7},{7,6},{8,9},{9,8},{10,11... | collective-permute-start | bytes 589832 | tf_op jit(solution)/shard_map/ppermute | solution.py:22
  143.1 3.5 %collective-permute-done.23.refs_3_ = bf16[48,2048]{1,0:T(8,128)(2,1)S(1)} collective-permute-done((bf16[48,2048]{1,0:T(8,128)(2,1)S(1)}, bf16[48,2048]{1,0:T(8,128)(2,1)S(1)}, u32[]{:S(2)}, u32[]{:S(2)}) %collective-permute-start.23) | collective-permute-done | bytes 196640 | tf_op jit(solution)/shard_map/ppermute | solution.py:22
  146.6 2.9 %collective-permute-done.24.refs_4_ = bf16[48,2048]{1,0:T(8,128)(2,1)S(1)} collective-permute-done((bf16[48,2048]{1,0:T(8,128)(2,1)S(1)}, bf16[48,2048]{1,0:T(8,128)(2,1)S(1)}, u32[]{:S(2)}, u32[]{:S(2)}) %collective-permute-start.24) | collective-permute-done | bytes 196640 | tf_op jit(solution)/shard_map/ppermute | solution.py:22
  149.5 2.5 %collective-permute-done.25.refs_5_ = bf16[48,2048]{1,0:T(8,128)(2,1)S(1)} collective-permute-done((bf16[48,2048]{1,0:T(8,128)(2,1)S(1)}, bf16[48,2048]{1,0:T(8,128)(2,1)S(1)}, u32[]{:S(2)}, u32[]{:S(2)}) %collective-permute-start.25) | collective-permute-done | bytes 196640 | tf_op jit(solution)/shard_map/ppermute | solution.py:22
  153.3 2.5 %weight_sums.15 = (bf16[512,768]{1,0:T(8,128)(2,1)}, bf16[512,768]{1,0:T(8,128)(2,1)}) custom-call(s32[1]{0:T(128)} %get-tuple-element.142.ids_ref, bf16[48,4096]{1,0:T(8,128)(2,1)S(1)} %get-tuple-element.92.refs_0_, bf16[48,4096]{1,0:T(8,128)(2,1)S(1)} %collective-permute-done.1.refs_1_, bf16[48,4096]{1,0:T(8,128)(2,1)S(1)} %collective-permute-done.2.refs_2_, ...), custom_call_target="tpu_custom_call" | custom-call | flops 1 | bytes 1 | tf_op jit(solution)/shard_map/weight_sums/pallas_call | solution.py:435
  160.2 2.4 %weight_sums.16 = bf16[512,768]{1,0:T(8,128)(2,1)} custom-call(s32[1]{0:T(128)} %get-tuple-element.151.ids_ref, bf16[48,4096]{1,0:T(8,128)(2,1)S(1)} %get-tuple-element.92.refs_0_, bf16[48,4096]{1,0:T(8,128)(2,1)S(1)} %collective-permute-done.1.refs_1_, bf16[48,4096]{1,0:T(8,128)(2,1)S(1)} %collective-permute-done.2.refs_2_, ...), custom_call_target="tpu_custom_call" | custom-call | flops 1 | bytes 1 | tf_op jit(solution)/shard_map/weight_sums/pallas_call | solution.py:435
  162.6 19.8 %collective-permute-done.28.refs_9_ = bf16[128,2048]{1,0:T(8,128)(2,1)} collective-permute-done((bf16[128,2048]{1,0:T(8,128)(2,1)}, bf16[128,2048]{1,0:T(8,128)(2,1)}, u32[]{:S(2)}, u32[]{:S(2)}) %collective-permute-start.28) | collective-permute-done | bytes 524320 | tf_op jit(solution)/shard_map/ppermute | solution.py:22
  182.4 3.1 %sum_slots.5 = (bf16[128,2048]{1,0:T(8,128)(2,1)}, f32[128,2]{1,0:T(8,128)S(1)}, bf16[128,2048]{1,0:T(8,128)(2,1)}) custom-call(s32[2,128]{1,0:T(2,128)S(1)} %bitcast.8, f32[2,128]{1,0:T(2,128)S(1)} %bitcast.6, f32[128,2]{1,0:T(8,128)S(1)} %copy.20.refs_2_, bf16[128,2048]{1,0:T(8,128)(2,1)} %refs_3_.3, bf16[48,4096]{1,0:T(8,128)(2,1)S(1)} %copy-done.41, ...), custom_call_target="tpu_custom_call" | custom-call | flops 1 | bytes 1 | tf_op jit(solution)/shard_map/sum_slots/pallas_call | solution.py:243
  187.1 4.6 %weight_sums.17 = (bf16[512,768]{1,0:T(8,128)(2,1)}, bf16[512,768]{1,0:T(8,128)(2,1)}) custom-call(s32[1]{0:T(128)} %get-tuple-element.151.ids_ref, bf16[48,4096]{1,0:T(8,128)(2,1)S(1)} %get-tuple-element.92.refs_0_, bf16[48,4096]{1,0:T(8,128)(2,1)S(1)} %collective-permute-done.1.refs_1_, bf16[48,4096]{1,0:T(8,128)(2,1)S(1)} %collective-permute-done.2.refs_2_, ...), custom_call_target="tpu_custom_call" | custom-call | flops 1 | bytes 1 | tf_op jit(solution)/shard_map/weight_sums/pallas_call | solution.py:435
  (188 shorter events, 58.0 us)
Async XLA Ops:
  3.2 28.8 %collective-permute-start = (bf16[128,2176]{1,0:T(8,128)(2,1)S(1)}, bf16[128,2176]{1,0:T(8,128)(2,1)S(1)}, u32[]{:S(2)}, u32[]{:S(2)}) collective-permute-start(bf16[128,2176]{1,0:T(8,128)(2,1)S(1)} %fusion.1), channel_id=1, source_target_pairs={{0,4},{1,5},{2,6},{3,7},{4,0},{5,1},{6,2},{7,3},{8,12},{9,13},{10,... | collective-permute-start | bytes 1671176 | tf_op jit(solution)/shard_map/ppermute | solution.py:22
  16.2 18.0 %collective-permute-start.1 = (bf16[48,4096]{1,0:T(8,128)(2,1)S(1)}, bf16[48,4096]{1,0:T(8,128)(2,1)S(1)}, u32[]{:S(2)}, u32[]{:S(2)}) collective-permute-start(bf16[48,4096]{1,0:T(8,128)(2,1)S(1)} %get-tuple-element.84), channel_id=1, source_target_pairs={{0,1},{1,0},{2,3},{3,2},{4,5},{5,4},{6,7},{7,6},{8,9},{9,8},{10,11... | collective-permute-start | bytes 1179656 | tf_op jit(solution)/shard_map/ppermute | solution.py:22
  17.7 25.3 %collective-permute-start.2 = (bf16[48,4096]{1,0:T(8,128)(2,1)S(1)}, bf16[48,4096]{1,0:T(8,128)(2,1)S(1)}, u32[]{:S(2)}, u32[]{:S(2)}) collective-permute-start(bf16[48,4096]{1,0:T(8,128)(2,1)S(1)} %get-tuple-element.85), channel_id=1, source_target_pairs={{0,2},{1,3},{2,0},{3,1},{4,6},{5,7},{6,4},{7,5},{8,10},{9,11},{10,... | collective-permute-start | bytes 1179656 | tf_op jit(solution)/shard_map/ppermute | solution.py:22
  19.3 40.8 %collective-permute-start.3 = (bf16[48,4096]{1,0:T(8,128)(2,1)S(1)}, bf16[48,4096]{1,0:T(8,128)(2,1)S(1)}, u32[]{:S(2)}, u32[]{:S(2)}) collective-permute-start(bf16[48,4096]{1,0:T(8,128)(2,1)S(1)} %get-tuple-element.86), channel_id=1, source_target_pairs={{0,3},{1,2},{2,1},{3,0},{4,7},{5,6},{6,5},{7,4},{8,11},{9,10},{10,... | collective-permute-start | bytes 1179656 | tf_op jit(solution)/shard_map/ppermute | solution.py:22
  32.0 47.1 %collective-permute-start.7 = (bf16[128,2048]{1,0:T(8,128)(2,1)}, bf16[128,2048]{1,0:T(8,128)(2,1)S(1)}, u32[]{:S(2)}, u32[]{:S(2)}) collective-permute-start(bf16[128,2048]{1,0:T(8,128)(2,1)} %refs_3_.3), channel_id=1, source_target_pairs={{0,4},{1,5},{2,6},{3,7},{4,0},{5,1},{6,2},{7,3},{8,12},{9,13},{10,... | collective-permute-start | bytes 1572872 | tf_op jit(solution)/shard_map/ppermute | solution.py:22
  32.6 35.3 %collective-permute-start.4 = (bf16[48,2048]{1,0:T(8,128)(2,1)S(1)}, bf16[48,2048]{1,0:T(8,128)(2,1)S(1)}, u32[]{:S(2)}, u32[]{:S(2)}) collective-permute-start(bf16[48,2048]{1,0:T(8,128)(2,1)S(1)} %get-tuple-element.89), channel_id=1, source_target_pairs={{0,1},{1,0},{2,3},{3,2},{4,5},{5,4},{6,7},{7,6},{8,9},{9,8},{10,11... | collective-permute-start | bytes 589832 | tf_op jit(solution)/shard_map/ppermute | solution.py:22
  34.2 33.7 %collective-permute-start.5 = (bf16[48,2048]{1,0:T(8,128)(2,1)S(1)}, bf16[48,2048]{1,0:T(8,128)(2,1)S(1)}, u32[]{:S(2)}, u32[]{:S(2)}) collective-permute-start(bf16[48,2048]{1,0:T(8,128)(2,1)S(1)} %get-tuple-element.90), channel_id=1, source_target_pairs={{0,2},{1,3},{2,0},{3,1},{4,6},{5,7},{6,4},{7,5},{8,10},{9,11},{10,... | collective-permute-start | bytes 589832 | tf_op jit(solution)/shard_map/ppermute | solution.py:22
  43.0 24.9 %collective-permute-start.6 = (bf16[48,2048]{1,0:T(8,128)(2,1)S(1)}, bf16[48,2048]{1,0:T(8,128)(2,1)S(1)}, u32[]{:S(2)}, u32[]{:S(2)}) collective-permute-start(bf16[48,2048]{1,0:T(8,128)(2,1)S(1)} %get-tuple-element.91), channel_id=1, source_target_pairs={{0,3},{1,2},{2,1},{3,0},{4,7},{5,6},{6,5},{7,4},{8,11},{9,10},{10,... | collective-permute-start | bytes 589832 | tf_op jit(solution)/shard_map/ppermute | solution.py:22
  75.7 13.5 %collective-permute-start.11 = (bf16[48,2048]{1,0:T(8,128)(2,1)}, bf16[48,2048]{1,0:T(8,128)(2,1)}, u32[]{:S(2)}, u32[]{:S(2)}) collective-permute-start(bf16[48,2048]{1,0:T(8,128)(2,1)} %get-tuple-element.113), channel_id=1, source_target_pairs={{0,1},{1,0},{2,3},{3,2},{4,5},{5,4},{6,7},{7,6},{8,9},{9,8},{10,11... | collective-permute-start | bytes 589832 | tf_op jit(solution)/shard_map/ppermute | solution.py:22
  76.6 13.2 %collective-permute-start.12 = (bf16[48,2048]{1,0:T(8,128)(2,1)}, bf16[48,2048]{1,0:T(8,128)(2,1)S(1)}, u32[]{:S(2)}, u32[]{:S(2)}) collective-permute-start(bf16[48,2048]{1,0:T(8,128)(2,1)} %copy-done.59), channel_id=1, source_target_pairs={{0,2},{1,3},{2,0},{3,1},{4,6},{5,7},{6,4},{7,5},{8,10},{9,11},{10,... | collective-permute-start | bytes 589832 | tf_op jit(solution)/shard_map/ppermute | solution.py:22
  76.6 13.2 %collective-permute-start.13 = (bf16[48,2048]{1,0:T(8,128)(2,1)}, bf16[48,2048]{1,0:T(8,128)(2,1)S(1)}, u32[]{:S(2)}, u32[]{:S(2)}) collective-permute-start(bf16[48,2048]{1,0:T(8,128)(2,1)} %copy-done.58), channel_id=1, source_target_pairs={{0,3},{1,2},{2,1},{3,0},{4,7},{5,6},{6,5},{7,4},{8,11},{9,10},{10,... | collective-permute-start | bytes 589832 | tf_op jit(solution)/shard_map/ppermute | solution.py:22
  81.5 11.2 %collective-permute-start.10 = (bf16[48,2048]{1,0:T(8,128)(2,1)S(1)}, bf16[48,2048]{1,0:T(8,128)(2,1)S(1)}, u32[]{:S(2)}, u32[]{:S(2)}) collective-permute-start(bf16[48,2048]{1,0:T(8,128)(2,1)S(1)} %get-tuple-element.110), channel_id=1, source_target_pairs={{0,3},{1,2},{2,1},{3,0},{4,7},{5,6},{6,5},{7,4},{8,11},{9,10},{10,... | collective-permute-start | bytes 589832 | tf_op jit(solution)/shard_map/ppermute | solution.py:22
  82.0 12.1 %collective-permute-start.8 = (bf16[48,2048]{1,0:T(8,128)(2,1)S(1)}, bf16[48,2048]{1,0:T(8,128)(2,1)S(1)}, u32[]{:S(2)}, u32[]{:S(2)}) collective-permute-start(bf16[48,2048]{1,0:T(8,128)(2,1)S(1)} %get-tuple-element.108), channel_id=1, source_target_pairs={{0,1},{1,0},{2,3},{3,2},{4,5},{5,4},{6,7},{7,6},{8,9},{9,8},{10,11... | collective-permute-start | bytes 589832 | tf_op jit(solution)/shard_map/ppermute | solution.py:22
  96.4 27.4 %collective-permute-start.18 = (bf16[128,2176]{1,0:T(8,128)(2,1)S(1)}, bf16[128,2176]{1,0:T(8,128)(2,1)S(1)}, u32[]{:S(2)}, u32[]{:S(2)}) collective-permute-start(bf16[128,2176]{1,0:T(8,128)(2,1)S(1)} %sum_slots.3), channel_id=1, source_target_pairs={{0,4},{1,5},{2,6},{3,7},{4,0},{5,1},{6,2},{7,3},{8,12},{9,13},{10,... | collective-permute-start | bytes 1671176 | tf_op jit(solution)/shard_map/ppermute | solution.py:22
  97.1 26.8 %collective-permute-start.15 = (bf16[48,4096]{1,0:T(8,128)(2,1)S(1)}, bf16[48,4096]{1,0:T(8,128)(2,1)S(1)}, u32[]{:S(2)}, u32[]{:S(2)}) collective-permute-start(bf16[48,4096]{1,0:T(8,128)(2,1)S(1)} %copy-done.57), channel_id=1, source_target_pairs={{0,1},{1,0},{2,3},{3,2},{4,5},{5,4},{6,7},{7,6},{8,9},{9,8},{10,11... | collective-permute-start | bytes 1179656 | tf_op jit(solution)/shard_map/ppermute | solution.py:22
  99.6 24.3 %collective-permute-start.16 = (bf16[48,4096]{1,0:T(8,128)(2,1)S(1)}, bf16[48,4096]{1,0:T(8,128)(2,1)S(1)}, u32[]{:S(2)}, u32[]{:S(2)}) collective-permute-start(bf16[48,4096]{1,0:T(8,128)(2,1)S(1)} %copy-done.55), channel_id=1, source_target_pairs={{0,2},{1,3},{2,0},{3,1},{4,6},{5,7},{6,4},{7,5},{8,10},{9,11},{10,... | collective-permute-start | bytes 1179656 | tf_op jit(solution)/shard_map/ppermute | solution.py:22
  101.6 27.8 %collective-permute-start.17 = (bf16[48,4096]{1,0:T(8,128)(2,1)S(1)}, bf16[48,4096]{1,0:T(8,128)(2,1)S(1)}, u32[]{:S(2)}, u32[]{:S(2)}) collective-permute-start(bf16[48,4096]{1,0:T(8,128)(2,1)S(1)} %copy-done.53), channel_id=1, source_target_pairs={{0,3},{1,2},{2,1},{3,0},{4,7},{5,6},{6,5},{7,4},{8,11},{9,10},{10,... | collective-permute-start | bytes 1179656 | tf_op jit(solution)/shard_map/ppermute | solution.py:22
  103.7 27.5 %collective-permute-start.19 = (bf16[576,768]{1,0:T(8,128)(2,1)S(1)}, bf16[576,768]{1,0:T(8,128)(2,1)S(1)}, u32[]{:S(2)}, u32[]{:S(2)}) collective-permute-start(bf16[576,768]{1,0:T(8,128)(2,1)S(1)} %concatenate.12), channel_id=1, source_target_pairs={{0,16},{8,24},{16,0},{24,8},{1,17},{9,25},{17,1},{25,9},{2,18},{10... | collective-permute-start | bytes 2654216 | tf_op jit(solution)/shard_map/ppermute | solution.py:22
  123.8 7.4 %collective-permute-start.20 = (bf16[512,768]{1,0:T(8,128)(2,1)S(1)}, bf16[512,768]{1,0:T(8,128)(2,1)S(1)}, u32[]{:S(2)}, u32[]{:S(2)}) collective-permute-start(bf16[512,768]{1,0:T(8,128)(2,1)S(1)} %weight_sums.12), channel_id=1, source_target_pairs={{0,8},{8,0},{16,24},{24,16},{1,9},{9,1},{17,25},{25,17},{2,10},{10... | collective-permute-start | bytes 2359304 | tf_op jit(solution)/shard_map/ppermute | solution.py:22
  137.0 49.2 %collective-permute-start.29 = (bf16[512,1536]{1,0:T(8,128)(2,1)}, bf16[512,1536]{1,0:T(8,128)(2,1)}, u32[]{:S(2)}, u32[]{:S(2)}) collective-permute-start(bf16[512,1536]{1,0:T(8,128)(2,1)} %weight_sums.14), channel_id=1, source_target_pairs={{0,16},{8,24},{16,0},{24,8},{1,17},{9,25},{17,1},{25,9},{2,18},{10... | collective-permute-start | bytes 4718600 | tf_op jit(solution)/shard_map/ppermute | solution.py:22
  138.5 8.1 %collective-permute-start.23 = (bf16[48,2048]{1,0:T(8,128)(2,1)S(1)}, bf16[48,2048]{1,0:T(8,128)(2,1)S(1)}, u32[]{:S(2)}, u32[]{:S(2)}) collective-permute-start(bf16[48,2048]{1,0:T(8,128)(2,1)S(1)} %get-tuple-element.139), channel_id=1, source_target_pairs={{0,1},{1,0},{2,3},{3,2},{4,5},{5,4},{6,7},{7,6},{8,9},{9,8},{10,11... | collective-permute-start | bytes 589832 | tf_op jit(solution)/shard_map/ppermute | solution.py:22
  141.6 7.8 %collective-permute-start.24 = (bf16[48,2048]{1,0:T(8,128)(2,1)S(1)}, bf16[48,2048]{1,0:T(8,128)(2,1)S(1)}, u32[]{:S(2)}, u32[]{:S(2)}) collective-permute-start(bf16[48,2048]{1,0:T(8,128)(2,1)S(1)} %get-tuple-element.140), channel_id=1, source_target_pairs={{0,2},{1,3},{2,0},{3,1},{4,6},{5,7},{6,4},{7,5},{8,10},{9,11},{10,... | collective-permute-start | bytes 589832 | tf_op jit(solution)/shard_map/ppermute | solution.py:22
  141.6 10.3 %collective-permute-start.25 = (bf16[48,2048]{1,0:T(8,128)(2,1)S(1)}, bf16[48,2048]{1,0:T(8,128)(2,1)S(1)}, u32[]{:S(2)}, u32[]{:S(2)}) collective-permute-start(bf16[48,2048]{1,0:T(8,128)(2,1)S(1)} %get-tuple-element.141), channel_id=1, source_target_pairs={{0,3},{1,2},{2,1},{3,0},{4,7},{5,6},{6,5},{7,4},{8,11},{9,10},{10,... | collective-permute-start | bytes 589832 | tf_op jit(solution)/shard_map/ppermute | solution.py:22
  156.4 26.0 %collective-permute-start.28 = (bf16[128,2048]{1,0:T(8,128)(2,1)}, bf16[128,2048]{1,0:T(8,128)(2,1)}, u32[]{:S(2)}, u32[]{:S(2)}) collective-permute-start(bf16[128,2048]{1,0:T(8,128)(2,1)} %sum_slots.4), channel_id=1, source_target_pairs={{0,4},{1,5},{2,6},{3,7},{4,0},{5,1},{6,2},{7,3},{8,12},{9,13},{10,... | collective-permute-start | bytes 1572872 | tf_op jit(solution)/shard_map/ppermute | solution.py:22
  (67 other events, 706.6 us)

commit v3 on v2

v3 whole, which is shorter than its diff:
```python
import functools

import jax
import jax.numpy as jnp
from jax import lax
from jax.experimental import pallas as pl
from jax.experimental.pallas import tpu as pltpu
from jax.sharding import PartitionSpec as P

grad_scale = 0.0625
f32 = jnp.float32
bf16 = jnp.bfloat16
VMEM = pl.BlockSpec(memory_space=pltpu.VMEM)
SMEM = pl.BlockSpec(memory_space=pltpu.SMEM)


def dot(a, b, dims=((1,), (0,))):
    return lax.dot_general(a, b, (dims, ((), ())), preferred_element_type=f32)


def exchange(x, axis, bit):
    size = lax.axis_size(axis)
    return lax.ppermute(x, axis, [(i, i ^ bit) for i in range(size)])


def within_half(blocks):
    return [blocks[0]] + [exchange(blocks[s], "exp", s) for s in range(1, len(blocks))]


def in_hbm(arrays):
    return [pltpu.with_memory_space_constraint(a, pltpu.HBM) for a in arrays]


def result(shape, dtype):
    return jax.ShapeDtypeStruct(tuple(shape), dtype)


def params(**kw):
    return pltpu.CompilerParams(vmem_limit_bytes=24 * 1024 * 1024, **kw)


def cost(flops, bytes_accessed):
    return pl.CostEstimate(flops=1, bytes_accessed=1, transcendentals=0)


def after(value, *earlier):
    return lax.optimization_barrier((value, earlier))[0]


class Blocks:
    def __init__(self, half, capacity):
        self.half, self.capacity = half, capacity
        self.split = capacity % 16 == 0
        self.count = half if self.split else 1
        self.rows = half * capacity
        self.height = self.rows // self.count

    def shapes(self, width):
        return [result((self.height, width), bf16)] * self.count

    def send(self, arrays, early=None):
        if self.split:
            if early is not None:
                number, first, then = early
                arrays = after(arrays[:number], first) + after(arrays[number:], then)
            return within_half(arrays)
        blocks = [arrays[0][s * self.capacity : (s + 1) * self.capacity] for s in range(self.half)]
        return [jnp.concatenate(within_half(blocks), axis=0)]


def join(refs, cols=slice(None)):
    parts = [r[:, cols] for r in refs]
    return parts[0] if len(parts) == 1 else jnp.concatenate(parts, axis=0)


def store(refs, cols, value):
    height = refs[0].shape[0]
    for i, r in enumerate(refs):
        r[:, cols] = value[i * height : (i + 1) * height].astype(r.dtype)


def slot_plan(rows, form):
    tokens = rows[0].shape[1]
    me = lax.axis_index("exp")
    place = me % form.half
    slot = lax.broadcasted_iota(jnp.int32, (form.rows, 1), 0)
    block = jnp.zeros_like(slot)
    for i in range(1, form.half):
        block = block + (slot >= i * form.capacity).astype(jnp.int32)
    expert = (me - place + (block ^ place)).astype(f32)
    rank_here = (slot - block * form.capacity).astype(f32)
    first = (rows[0] == expert).astype(f32)
    second = (rows[1] == expert).astype(f32)
    row = lax.broadcasted_iota(jnp.int32, (tokens, tokens), 0)
    col = lax.broadcasted_iota(jnp.int32, (tokens, tokens), 1)
    earlier = (row < col).astype(f32).astype(bf16)
    rank = dot((first + second).astype(bf16), earlier)
    here = (rank == rank_here).astype(f32)
    return first * here, second * here


def packed_columns(ref):
    x = ref[...].astype(f32)
    return [x[:, k : k + 1] for k in range(2)] + [
        x[:, 2 + k : 3 + k] + x[:, 4 + k : 5 + k] + x[:, 6 + k : 7 + k] for k in range(2)
    ]


def packed_rows(ref):
    x = jnp.transpose(ref[...].astype(f32))
    return [x[k : k + 1] for k in range(2)] + [x[2 + k : 3 + k] + x[4 + k : 5 + k] + x[6 + k : 7 + k] for k in range(2)]


def plain_rows(ids_ref, combine_ref):
    ids = ids_ref[...].astype(f32)
    return [ids[0:1], ids[1:2], combine_ref[0:1, :], combine_ref[1:2, :]]


def chunks(width, step=512):
    step = min(step, width)
    return [slice(i, i + step) for i in range(0, width, step)]


def pack_rows(meta):
    rows = [meta[0], meta[1]]
    rest = [meta[2], meta[3]]
    for _ in range(3):
        top = [r.astype(bf16).astype(f32) for r in rest]
        rows += top
        rest = [r - t for r, t in zip(rest, top)]
    rows.append(jnp.zeros((128 - len(rows), meta[0].shape[1]), f32))
    return jnp.transpose(jnp.concatenate(rows, axis=0)).astype(bf16)


def gather_kernel(form, scaled, width, plain, *refs):
    meta, refs = (plain_rows(*refs[:2]), refs[2:]) if plain else (packed_rows(refs[0]), refs[1:])
    if plain:
        message_ref, refs = refs[-1], refs[:-1]
        message_ref[:, :width] = refs[0][...]
        message_ref[:, width:] = pack_rows(meta)
    inputs, outs = refs[: len(scaled)], refs[len(scaled) :]
    first, second = slot_plan(meta, form)
    either = (first + second).astype(bf16)
    weight = jnp.sum(first * meta[2] + second * meta[3], axis=1, keepdims=True)
    offset = 0
    for x, by_weight in zip(inputs, scaled):
        for cols in chunks(width):
            rows = dot(either, x[:, cols])
            if by_weight:
                rows = rows * weight
            store(outs, slice(offset + cols.start, offset + cols.stop), rows)
        offset += width


def meta_specs(meta, width):
    if len(meta) == 2:
        return [pl.BlockSpec(m.shape, lambda i: (0, 0)) for m in meta]
    return [pl.BlockSpec((meta[0].shape[0], 128), lambda i: (0, width // 128))]


def whole_spec(shape):
    return pl.BlockSpec(shape, lambda i: (0, 0))


def gather(form, meta, arrays, scaled, width):
    tokens = arrays[0].shape[0]
    total = width * len(arrays)
    plain = len(meta) == 2
    out_shape = form.shapes(total)
    if plain:
        out_shape = out_shape + [result((tokens, width + 128), bf16)]
    out = pl.pallas_call(
        functools.partial(gather_kernel, form, scaled, width, plain),
        grid=(1,),
        out_shape=out_shape,
        in_specs=meta_specs(meta, width) + [whole_spec((tokens, width)) for _ in arrays],
        out_specs=[whole_spec(x.shape) for x in out_shape],
        compiler_params=params(),
        cost_estimate=cost(2 * form.rows * tokens * total, 4 * form.rows * total),
        name="gather_slots",
    )(*(in_hbm([*meta, *arrays]) if plain else [*meta, *arrays]))
    return list(out)


def back_kernel(form, offsets, plain, more, *refs):
    count = form.count
    if plain:
        meta, weights = plain_rows(*refs[:2]), [refs[2][:, k : k + 1] for k in range(2)]
        refs = refs[3:]
    else:
        meta, weights = packed_rows(refs[0]), packed_columns(refs[0])[2:]
        refs = refs[1:]
    cot_ref, rows, refs = refs[0], refs[1 : 1 + count], refs[1 + count :]
    others, outs = (list(refs[:2]), list(refs[2:])) if more else ([], list(refs))
    plan = [p.astype(bf16) for p in slot_plan(meta, form)]
    out_at, grad_at = offsets
    width = cot_ref.shape[1]

    def put(i, cols, value):
        if more:
            value = value + others[i][:, cols].astype(f32)
        outs[i][:, cols] = value.astype(outs[i].dtype)

    def put_grad(cols, value):
        if more:
            value = value + others[1][:, cols].astype(f32)
        outs[-1][:, cols] = value.astype(bf16)

    def put_sums(sums):
        if more:
            tail = others[0][:, width:].astype(f32)
            for k in range(2):
                outs[1][:, k : k + 1] = sums[k] + tail[:, k : k + 1] + tail[:, 2 + k : 3 + k] + tail[:, 4 + k : 5 + k]
            return
        lane = lax.broadcasted_iota(jnp.int32, (sums[0].shape[0], 128), 1)
        tail = jnp.zeros(lane.shape, f32)
        for k in range(2):
            rest = sums[k]
            for piece in range(3):
                top = rest.astype(bf16).astype(f32)
                tail = jnp.where(lane == 2 * piece + k, top, tail)
                rest = rest - top
        outs[0][:, width:] = tail.astype(bf16)

    if out_at is not None:
        sums = [0.0, 0.0]
        for cols in chunks(width):
            block = join(rows, slice(out_at + cols.start, out_at + cols.stop))
            mixed = 0.0
            cot = cot_ref[:, cols].astype(f32)
            for k in range(2):
                pair = dot(plan[k], block, ((0,), (0,)))
                mixed = mixed + weights[k] * pair
                sums[k] = sums[k] + jnp.sum(cot * pair, axis=1, keepdims=True)
            put(0, cols, mixed)
        put_sums(sums)
    if grad_at is not None:
        either = plan[0] + plan[1]
        for cols in chunks(width):
            block = join(rows, slice(grad_at + cols.start, grad_at + cols.stop))
            put_grad(cols, dot(either, block, ((0,), (0,))))


def back(form, meta, cot, rows, offsets, combine=None, others=()):
    tokens, width = cot.shape
    shapes = []
    if offsets[0] is not None:
        shapes += [result((tokens, width + (0 if others else 128)), bf16)]
    if others:
        shapes += [result((tokens, 2), f32)]
    if offsets[1] is not None:
        shapes += [result((tokens, width), bf16)]
    own = [] if combine is None else [combine]
    arrays = own + [cot] + list(rows) + list(others)
    return pl.pallas_call(
        functools.partial(back_kernel, form, offsets, combine is not None, len(others) > 0),
        grid=(1,),
        out_shape=shapes,
        in_specs=meta_specs(meta, width) + [whole_spec(a.shape) for a in arrays],
        out_specs=[whole_spec(x.shape) for x in shapes],
        compiler_params=params(),
        cost_estimate=cost(4 * form.rows * tokens * width, 4 * form.rows * width),
        name="sum_slots",
    )(*meta, *arrays)


def tiles(ff):
    return chunks(ff, 256 if ff % 256 == 0 else ff)


def fetch(refs, buffers, sems, steps):
    copies = [
        [
            pltpu.make_async_copy(w.at[0, :, inner], b.at[:, inner], sems.at[i, step])
            for i, (w, b) in enumerate(zip(refs, buffers))
        ]
        for step, inner in enumerate(steps)
    ]
    for group in copies:
        for c in group:
            c.start()

    def wait(step):
        for c in copies[step]:
            c.wait()

    return wait


def add_to(acc, first, cols, value):
    if first:
        acc[:, cols] = value
    else:
        acc[:, cols] += value


def pick(ids_ref, refs, at, out_ref, out_at, width):
    number = ids_ref.shape[0]
    share = width // (2 * number)
    height = refs[0].shape[0]
    for p in range(number):
        cols = pl.ds(pl.multiple_of(at + ids_ref[p] * share, share), share)
        for i, r in enumerate(refs):
            out_ref[i * height : (i + 1) * height, out_at + p * share : out_at + (p + 1) * share] = r[:, cols]
    return out_at + number * share


def pick_kernel(count, ids_ref, *refs):
    pick(ids_ref, refs[:count], 0, refs[count], 0, refs[0].shape[1])


def pick_shares(form, ids, arrays):
    width = arrays[0].shape[1]
    return pl.pallas_call(
        functools.partial(pick_kernel, form.count),
        out_shape=jax.ShapeDtypeStruct((form.rows, width // 2), bf16),
        in_specs=[SMEM] + [VMEM] * form.count,
        out_specs=VMEM,
        compiler_params=params(),
        cost_estimate=cost(1, 1),
        name="pick_shares",
    )(ids, *arrays)


def forward_kernel(count, *refs):
    x_refs, ids_ref, held = refs[:count], refs[count], refs[count + 1 : count + 4]
    out_refs = refs[count + 4 : 2 * count + 4]
    swap_ref, hidden_ref, active_ref, slope_ref, acc, gate_ref, up_ref, down_ref, sems = refs[2 * count + 4 :]
    wait = fetch(held, (gate_ref, up_ref, down_ref), sems, tiles(hidden_ref.shape[1]))
    x = join(x_refs)
    ff = hidden_ref.shape[1]
    used = pick(ids_ref, x_refs, 0, swap_ref, 0, x.shape[1])
    for step, inner in enumerate(tiles(hidden_ref.shape[1])):
        wait(step)
        gate, up = dot(x, gate_ref[:, inner]), dot(x, up_ref[:, inner])
        s = jax.nn.sigmoid(gate)
        active = gate * s
        hidden = (active * up).astype(bf16)
        hidden_ref[:, inner] = hidden
        swap_ref[:, used + inner.start : used + inner.stop] = hidden
        active_ref[:, inner] = active
        slope_ref[:, inner] = up * s * (1.0 + gate * (1.0 - s))
        for cols in chunks(acc.shape[1]):
            add_to(acc, step == 0, cols, dot(hidden, down_ref[cols, inner], ((1,), (1,))))
    store(out_refs, slice(None), acc[...])


def expert_call(kernel, form, inputs, weights, more, out_width, inner_types, name):
    _, width, ff = weights[0].shape
    rows = form.rows
    out_shape = form.shapes(out_width) + [jax.ShapeDtypeStruct((rows, w), t) for w, t in inner_types]
    operands = [*inputs, *more]
    out = pl.pallas_call(
        functools.partial(kernel, form.count),
        out_shape=out_shape,
        in_specs=[SMEM if o.dtype == jnp.int32 else VMEM for o in operands] + [pl.BlockSpec(memory_space=pl.ANY)] * 3,
        out_specs=[VMEM] * len(out_shape),
        scratch_shapes=[pltpu.VMEM((rows, out_width), f32)]
        + [pltpu.VMEM((width, ff), bf16)] * 3
        + [pltpu.SemaphoreType.DMA((3, len(tiles(ff))))],
        compiler_params=params(),
        cost_estimate=cost(6 * rows * width * ff, 6 * width * ff),
        name=name,
    )(*operands, *in_hbm(weights))
    return list(out[: form.count]), *out[form.count :]


def forward(form, x, ids, *weights):
    _, width, ff = weights[0].shape
    types = [(width // 2 + ff, bf16), (ff, bf16), (ff, f32), (ff, f32)]
    return expert_call(forward_kernel, form, x, weights, [ids], width, types, "expert_forward")


def backward_kernel(count, *refs):
    c_refs, active_ref, slope_ref, held = refs[:count], refs[count], refs[count + 1], refs[count + 2 : count + 5]
    in_refs = refs[count + 5 : 2 * count + 5]
    gg_ref, gu_ref, acc, gate_ref, up_ref, down_ref, sems = refs[2 * count + 5 :]
    wait = fetch(held, (gate_ref, up_ref, down_ref), sems, tiles(gg_ref.shape[1]))
    c = join(c_refs)
    for step, inner in enumerate(tiles(gg_ref.shape[1])):
        wait(step)
        grad_hidden = dot(c, down_ref[:, inner])
        gu = (grad_hidden * active_ref[:, inner]).astype(bf16)
        gg = (grad_hidden * slope_ref[:, inner]).astype(bf16)
        gu_ref[:, inner] = gu
        gg_ref[:, inner] = gg
        for cols in chunks(acc.shape[1]):
            back = dot(gg, gate_ref[cols, inner], ((1,), (1,))) + dot(gu, up_ref[cols, inner], ((1,), (1,)))
            add_to(acc, step == 0, cols, back)
    store(in_refs, slice(None), acc[...])


def backward(form, c, active, slope, *weights):
    more = [active, slope]
    _, width, ff = weights[0].shape
    return expert_call(backward_kernel, form, c, weights, more, width, [(ff, bf16)] * 2, "expert_backward")


def both_kernel(count, *refs):
    in_refs, ids_ref, held = refs[:count], refs[count], refs[count + 1 : count + 4]
    out_refs = refs[count + 4 : 2 * count + 4]
    picked_ref, inner_ref, acc, gate_ref, up_ref, down_ref, sems = refs[2 * count + 4 :]
    width, ff = acc.shape[1] // 2, gate_ref.shape[1]
    wait = fetch(held, (gate_ref, up_ref, down_ref), sems, tiles(ff))
    used = pick(ids_ref, in_refs, 0, picked_ref, 0, width)
    pick(ids_ref, in_refs, width, picked_ref, used, width)
    hidden_ref, gg_ref, gu_ref = [inner_ref.at[:, i * ff : (i + 1) * ff] for i in range(3)]
    x, c = join(in_refs, slice(0, width)), join(in_refs, slice(width, 2 * width))
    for step, inner in enumerate(tiles(ff)):
        wait(step)
        gate, up = dot(x, gate_ref[:, inner]), dot(x, up_ref[:, inner])
        s = jax.nn.sigmoid(gate)
        active = gate * s
        hidden = (active * up).astype(bf16)
        hidden_ref[:, inner] = hidden
        grad_hidden = dot(c, down_ref[:, inner])
        gu = (grad_hidden * active).astype(bf16)
        gg = (grad_hidden * up * s * (1.0 + gate * (1.0 - s))).astype(bf16)
        gu_ref[:, inner] = gu
        gg_ref[:, inner] = gg
        for cols in chunks(width):
            add_to(acc, step == 0, cols, dot(hidden, down_ref[cols, inner], ((1,), (1,))))
            back = slice(width + cols.start, width + cols.stop)
            grad = dot(gg, gate_ref[cols, inner], ((1,), (1,))) + dot(gu, up_ref[cols, inner], ((1,), (1,)))
            add_to(acc, step == 0, back, grad)
    store(out_refs, slice(None), acc[...])


def both(form, rows_in, ids, *weights):
    _, width, ff = weights[0].shape
    return expert_call(both_kernel, form, rows_in, weights, [ids], 2 * width, [(width, bf16), (3 * ff, bf16)], "expert_both")


def weight_kernel(counts, adds, scale, ids_ref, *refs):
    groups = []
    for n in counts:
        groups.append(join(refs[:n]))
        refs = refs[n:]
    left = jnp.concatenate(groups, axis=0)
    number = len(refs) // (len(counts) + adds + 1)
    rights, refs = refs[: number * len(counts)], refs[number * len(counts) :]
    others, outs = refs[:-number], refs[-number:]
    for i in range(number):
        right = jnp.concatenate([r[...] for r in rights[i * len(counts) : (i + 1) * len(counts)]], axis=0)
        sums = dot(left, right, ((0,), (0,)))
        if adds:
            sums = sums + others[i][...].astype(f32)
        if scale:
            sums = sums * grad_scale
        outs[i][...] = sums.astype(outs[i].dtype)


def weight_sums(form, ids, at, left, rights, share, ff, add=None, scale=False, dtype=bf16, hbm=False):
    first, steps = at[0], at[1] - at[0]
    arrays, specs = [], []
    for held, column, picked in left:
        block = column // share
        for h in held:
            arrays.append(h)
            if picked:
                specs.append(pl.BlockSpec((h.shape[0], share), lambda i, ids_ref, b=block: (0, b + first + i)))
            else:
                specs.append(pl.BlockSpec((h.shape[0], share), lambda i, ids_ref, b=block: (0, b + ids_ref[first + i])))
    for right in rights:
        for array, column in right:
            arrays.append(array)
            specs.append(pl.BlockSpec((form.rows, ff), lambda i, ids_ref, b=column // ff: (0, b)))
    for array, column in add or []:
        arrays.append(array)
        specs.append(pl.BlockSpec((share, ff), lambda i, ids_ref, b=column // ff: (i, b)))
    number = len(rights)
    widths = [ff] * number
    if hbm:
        arrays = in_hbm(arrays)
    return pl.pallas_call(
        functools.partial(weight_kernel, [len(g[0]) for g in left], 1 if add else 0, scale),
        grid_spec=pltpu.PrefetchScalarGridSpec(
            num_scalar_prefetch=1,
            grid=(steps,),
            in_specs=specs,
            out_specs=[pl.BlockSpec((share, w), lambda i, ids_ref: (i, 0)) for w in widths],
        ),
        out_shape=[jax.ShapeDtypeStruct((steps * share, w), dtype) for w in widths],
        compiler_params=params(),
        cost_estimate=cost(1, 1),
        name="weight_sums",
    )(ids, *arrays)


def finish_kernel(number, *refs):
    for keep, got, out in zip(refs[:number], refs[number : 2 * number], refs[2 * number :]):
        out[...] = ((keep[...] + got[...].astype(f32)) * grad_scale).astype(bf16)


def finish(keeps, gots):
    number = len(keeps)
    rows, ff = keeps[0].shape
    tile = rows // 2
    return pl.pallas_call(
        functools.partial(finish_kernel, number),
        grid=(rows // tile,),
        out_shape=[result((rows, ff), bf16)] * number,
        in_specs=[pl.BlockSpec((tile, ff), lambda i: (i, 0))] * (2 * number),
        out_specs=[pl.BlockSpec((tile, ff), lambda i: (i, 0))] * number,
        compiler_params=params(),
        cost_estimate=cost(1, 1),
        name="finish_weights",
    )(*keeps, *gots)


def local(hits, cotangent, combine, expert_ids, gate_weight, up_weight, down_weight):
    tokens, width = hits.shape
    experts = lax.axis_size("exp")
    copies = lax.axis_size("ctx")
    half = experts // 2
    capacity = 3 * tokens // experts
    form = Blocks(half, capacity)
    meta = (expert_ids.T, combine.T)
    *own_send, message = gather(form, meta, [hits, cotangent], (False, True), width)
    far_hits = exchange(message, "exp", half)
    far_cot = exchange(after(cotangent, far_hits), "exp", half)
    far_meta = (far_hits,)

    share, ff = width // copies, gate_weight.shape[2]
    order = [r for r in range(0, copies, 2)]
    order.sort(key=lambda r: [-(r >> b & 1) for b in range(1, copies.bit_length())])
    order = jnp.asarray(order, jnp.int32)
    here = lax.axis_index("ctx")
    theirs, ours = here ^ 1 ^ order, here ^ order
    swap = lambda x: exchange(x, "ctx", 1)

    weights = (gate_weight, up_weight, down_weight)
    own = form.send(own_send)
    x1_sent = gather(form, after(far_meta, own), [far_hits], (False,), width)
    x1 = form.send(x1_sent)
    back0, own_picked, own_inner = both(form, after(own, x1_sent[0]), theirs, *weights)
    picked_got, inner_got = swap(own_picked), swap(own_inner)
    c1_sent = gather(form, after(far_meta, own_picked), [far_cot], (True,), width)
    c1 = form.send(c1_sent)
    out1, x1_swap, hidden1, active1, slope1 = forward(form, after(x1, c1_sent[0]), theirs, *weights)
    x1_got = swap(x1_swap)
    out1_back = form.send(out1)

    on, all_ = copies // 4, copies // 2
    half_width = width // 2
    c1_got = swap(pick_shares(form, after(theirs, hidden1), c1))
    x_left = [(own, 0, False), (x1, 0, False), ([picked_got], 0, True), ([x1_got], 0, True)]
    c_left = [(own, width, False), (c1, 0, False), ([picked_got], half_width, True), ([c1_got], 0, True)]
    at_hidden, at_gate, at_up = [i * ff for i in range(3)]

    def right(far, far_got, column, far_column=0):
        return [(own_inner, column), (far, 0), (inner_got, column), (far_got, far_column)]

    hidden1_got = x1_got[:, half_width:]
    down = [right(hidden1, hidden1_got, at_hidden)]
    (down_on,) = weight_sums(form, ours, (0, on), c_left, down, share, ff)
    down_there = exchange(down_on, "ctx", 2)
    gin1, gg1, gu1 = backward(form, after(c1, down_on), active1, slope1, *weights)
    gin1_back = form.send(gin1)
    (far_mixed,) = back(form, after(far_meta, gg1), far_cot, out1_back, (0, None))
    got_mixed = exchange(far_mixed, "exp", half)
    both_rights = [right(gg1, swap(gg1), at_gate), right(gu1, swap(gu1), at_up)]
    gate_on, up_on = weight_sums(form, after(ours, far_mixed), (0, on), x_left, both_rights, share, ff)
    gate_there, up_there = exchange(gate_on, "ctx", 2), exchange(up_on, "ctx", 2)
    (far_grad,) = back(form, after(far_meta, gate_on, down_there), far_cot, gin1_back, (None, 0))
    got_grad = exchange(far_grad, "exp", half)

    def last_bits(keep, got):
        bit = 4
        while bit < copies:
            sums = keep + got.astype(f32)
            middle = sums.shape[0] // 2
            keep, got = sums[middle:], exchange(sums[:middle].astype(bf16), "ctx", bit)
            bit *= 2
        return keep, got

    back0_got = form.send(back0, (2, down_on, far_grad))
    (down_keep,) = weight_sums(form, after(ours, far_grad, got_mixed, back0_got[1 % form.count]), (on, all_), c_left, down, share, ff, dtype=f32, hbm=True)
    gate_keep, up_keep = weight_sums(
        form, after(ours, down_keep), (on, all_), x_left, both_rights, share, ff, dtype=f32, hbm=True
    )
    mixed, combine_grads, input_grads = back(
        form,
        after(meta, gate_keep),
        cotangent,
        back0_got,
        (0, width),
        combine,
        (got_mixed, got_grad),
    )
    down_grads, gate_grads, up_grads = [
        finish([k for k, _ in pairs], [g for _, g in pairs])
        for pairs in [[last_bits(down_keep, down_there)]]
    ][0] + finish(*zip(*[last_bits(gate_keep, gate_there), last_bits(up_keep, up_there)]))
    return (mixed, input_grads, combine_grads, gate_grads[None], up_grads[None], down_grads[None])


def solution(mesh):
    rows = P(("ctx", "exp"), None)
    weight = P("exp", None, None)
    grads = P("exp", "ctx", None)
    return jax.shard_map(
        local,
        mesh=mesh,
        in_specs=(rows, rows, rows, rows, weight, weight, weight),
        out_specs=(rows, rows, rows, grads, grads, grads),
        check_vma=False,
    )
```

time: 192 us -> 168 us (0.88)
  local copies, waits for them, and re-layouts: 21.9 us -> 4.38 us
  waiting for transfers between devices: 91.4 us -> 79.1 us
  Pallas kernels: 41.6 us -> 47.2 us
  starting transfers between devices: 33.1 us -> 35.1 us
    unnamed x124 -> x76, local copies, waits for them, and re-layouts: 20.5 us -> 4.36 us
    ppermute x30 -> x31, waiting for transfers between devices: 91.4 us -> 79.1 us  [exchange(): return lax.ppermute(x, axis, [(i, i ^ bit) for i in range(size)])]
    pallas_call x3, Pallas kernels: 12.4 us -> 21 us  [expert_call(): pl.pallas_call(functools.partial(kernel, form.count), out_shape=out_shape...]
    pallas_call x13 -> x10, Pallas kernels: 22.8 us -> 19.1 us  [the longest x4 11.1 us: weight_sums(): pl.pallas_call(functools.partial(weight_kernel, [len(g[0]) for g in left]...]
    ppermute x30 -> x31, starting transfers between devices: 33.1 us -> 35.1 us  [exchange(): return lax.ppermute(x, axis, [(i, i ^ bit) for i in range(size)])]
  transfers between devices with their start and end apart: 30 -> 31, of which waited for: 14 -> 12; matrix products, arithmetic and copies ran while one was open for 1% -> 0% of each run, Pallas kernels for 17% -> 24%
where the time goes in v3:
time: 168 us
  waiting for transfers between devices  79.1 us (47%)
  Pallas kernels  47.2 us (28%)
  starting transfers between devices  35.1 us (21%)
  local copies, waits for them, and re-layouts  4.38 us (3%)
    ppermute x31, waiting for transfers between devices, exchange(): return lax.ppermute(x, axis, [(i, i ^ bit) for i in range(size)])  79.1 us
    ppermute x31, starting transfers between devices, exchange(): return lax.ppermute(x, axis, [(i, i ^ bit) for i in range(size)])  35.1 us
    pallas_call x3, Pallas kernels, expert_call(): pl.pallas_call(functools.partial(kernel, form.count), out_shape=out_shape...  21 us
    pallas_call x4, Pallas kernels, weight_sums(): pl.pallas_call(functools.partial(weight_kernel, [len(g[0]) for g in left]...  11.1 us
    pallas_call x3, Pallas kernels, back(): pl.pallas_call(functools.partial(back_kernel, form, offsets, combine is n...  7.18 us
    unnamed x76, local copies, waits for them, and re-layouts  4.36 us
    pallas_call x3, Pallas kernels, gather(): pl.pallas_call(functools.partial(gather_kernel, form, scaled, width, plai...  4.09 us
  transfers between devices with their start and end apart: 31, of which 12 were waited for; matrix products, arithmetic and copies ran while one was open for 0% of the time, Pallas kernels for 24%

profile of v3, /device:TPU:0, one launch (start us, length us, event | category | flops | bytes accessed | tf_op | source)
XLA Modules:
  0.0 167.6 jit_solution(7945890403870287604)
XLA Ops:
  0.6 2.0 %gather_slots.3 = (bf16[48,4096]{1,0:T(8,128)(2,1)S(1)}, bf16[48,4096]{1,0:T(8,128)(2,1)S(1)}, bf16[48,4096]{1,0:T(8,128)(2,1)S(1)}, bf16[48,4096]{1,0:T(8,128)(2,1)S(1)}, bf16[128,2176]{1,0:T(8,128)(2,1)S(1)}) custom-call(s32[2,128]{1,0:T(2,128)} %bitcast.7, f32[2,128]{1,0:T(2,128)} %bitcast.5, bf16[128,2048]{1,0:T(8,128)(2,1)} %refs_2_.2, ...), custom_call_target="tpu_custom_call" | custom-call | flops 1 | bytes 1 | tf_op jit(solution)/shard_map/gather_slots/pallas_call | solution.py:172
  2.6 4.1 %collective-permute-start = (bf16[128,2176]{1,0:T(8,128)(2,1)S(1)}, bf16[128,2176]{1,0:T(8,128)(2,1)S(1)}, u32[]{:S(2)}, u32[]{:S(2)}) collective-permute-start(bf16[128,2176]{1,0:T(8,128)(2,1)S(1)} %get-tuple-element.75), channel_id=1, source_target_pairs={{0,4},{1,5},{2,6},{3,7},{4,0},{5,1},{6,2},{7,3},{8,12},{9,13},{10,... | collective-permute-start | bytes 1671176 | tf_op jit(solution)/shard_map/ppermute | solution.py:23
  10.2 21.2 %collective-permute-done.refs_0_.refs_1_ = bf16[128,2176]{1,0:T(8,128)(2,1)S(1)} collective-permute-done((bf16[128,2176]{1,0:T(8,128)(2,1)S(1)}, bf16[128,2176]{1,0:T(8,128)(2,1)S(1)}, u32[]{:S(2)}, u32[]{:S(2)}) %collective-permute-start) | collective-permute-done | bytes 557088 | tf_op jit(solution)/shard_map/ppermute | solution.py:23
  31.4 9.6 %collective-permute-done.3.refs_3_ = bf16[48,4096]{1,0:T(8,128)(2,1)S(1)} collective-permute-done((bf16[48,4096]{1,0:T(8,128)(2,1)S(1)}, bf16[48,4096]{1,0:T(8,128)(2,1)S(1)}, u32[]{:S(2)}, u32[]{:S(2)}) %collective-permute-start.3) | collective-permute-done | bytes 393248 | tf_op jit(solution)/shard_map/ppermute | solution.py:23
  43.5 2.3 %collective-permute-start.11 = (bf16[48,2048]{1,0:T(8,128)(2,1)S(1)}, bf16[48,2048]{1,0:T(8,128)(2,1)S(1)}, u32[]{:S(2)}, u32[]{:S(2)}) collective-permute-start(bf16[48,2048]{1,0:T(8,128)(2,1)S(1)} %get-tuple-element.95), channel_id=1, source_target_pairs={{0,3},{1,2},{2,1},{3,0},{4,7},{5,6},{6,5},{7,4},{8,11},{9,10},{10,... | collective-permute-start | bytes 589832 | tf_op jit(solution)/shard_map/ppermute | solution.py:23
  45.8 9.1 %expert_both.1 = (bf16[48,4096]{1,0:T(8,128)(2,1)S(1)}, bf16[48,4096]{1,0:T(8,128)(2,1)S(1)}, bf16[48,4096]{1,0:T(8,128)(2,1)}, bf16[48,4096]{1,0:T(8,128)(2,1)}...) custom-call(bf16[48,4096]{1,0:T(8,128)(2,1)S(1)} %get-tuple-element.82.refs_0_, ...), custom_call_target="tpu_custom_call" | custom-call | flops 1 | bytes 1 | tf_op jit(solution)/shard_map/expert_both/pallas_call | solution.py:353
  60.7 5.4 %expert_forward.1 = (bf16[48,2048]{1,0:T(8,128)(2,1)S(1)}, bf16[48,2048]{1,0:T(8,128)(2,1)S(1)}, bf16[48,2048]{1,0:T(8,128)(2,1)S(1)}, bf16[48,2048]{1,0:T(8,128...) custom-call(bf16[48,2048]{1,0:T(8,128)(2,1)S(1)} %get-tuple-element., ...), custom_call_target="tpu_custom_call" | custom-call | flops 1 | bytes 1 | tf_op jit(solution)/shard_map/expert_forward/pallas_call | solution.py:353
  69.5 4.5 %collective-permute-done.6.refs_2_.refs_6_ = bf16[48,2048]{1,0:T(8,128)(2,1)S(1)} collective-permute-done((bf16[48,2048]{1,0:T(8,128)(2,1)S(1)}, bf16[48,2048]{1,0:T(8,128)(2,1)S(1)}, u32[]{:S(2)}, u32[]{:S(2)}) %collective-permute-start.6) | collective-permute-done | bytes 196640 | tf_op jit(solution)/shard_map/ppermute | solution.py:23
  74.0 4.9 %collective-permute-done.7.refs_3_.refs_7_ = bf16[48,2048]{1,0:T(8,128)(2,1)S(1)} collective-permute-done((bf16[48,2048]{1,0:T(8,128)(2,1)S(1)}, bf16[48,2048]{1,0:T(8,128)(2,1)S(1)}, u32[]{:S(2)}, u32[]{:S(2)}) %collective-permute-start.7) | collective-permute-done | bytes 196640 | tf_op jit(solution)/shard_map/ppermute | solution.py:23
  84.7 6.4 %expert_backward.1 = (bf16[48,2048]{1,0:T(8,128)(2,1)S(1)}, bf16[48,2048]{1,0:T(8,128)(2,1)S(1)}, bf16[48,2048]{1,0:T(8,128)(2,1)S(1)}, bf16[48,2048]{1,0:T(8,12...) custom-call(bf16[48,2048]{1,0:T(8,128)(2,1)S(1)} %get-tuple-element.104.refs_0_.refs_4_, ...), custom_call_target="tpu_custom_call" | custom-call | flops 1 | bytes 1 | tf_op jit(solution)/shard_map/expert_backward/pallas_call | solution.py:353
  92.2 2.2 %collective-permute-start.17 = (bf16[48,2048]{1,0:T(8,128)(2,1)S(1)}, bf16[48,2048]{1,0:T(8,128)(2,1)S(1)}, u32[]{:S(2)}, u32[]{:S(2)}) collective-permute-start(bf16[48,2048]{1,0:T(8,128)(2,1)S(1)} %get-tuple-element.115), channel_id=1, source_target_pairs={{0,3},{1,2},{2,1},{3,0},{4,7},{5,6},{6,5},{7,4},{8,11},{9,10},{10,... | collective-permute-start | bytes 589832 | tf_op jit(solution)/shard_map/ppermute | solution.py:23
  94.5 4.5 %collective-permute-done.16.refs_4_ = bf16[48,2048]{1,0:T(8,128)(2,1)S(1)} collective-permute-done((bf16[48,2048]{1,0:T(8,128)(2,1)S(1)}, bf16[48,2048]{1,0:T(8,128)(2,1)S(1)}, u32[]{:S(2)}, u32[]{:S(2)}) %collective-permute-start.16) | collective-permute-done | bytes 196640 | tf_op jit(solution)/shard_map/ppermute | solution.py:23
  100.7 3.3 %collective-permute-done.17.refs_5_ = bf16[48,2048]{1,0:T(8,128)(2,1)S(1)} collective-permute-done((bf16[48,2048]{1,0:T(8,128)(2,1)S(1)}, bf16[48,2048]{1,0:T(8,128)(2,1)S(1)}, u32[]{:S(2)}, u32[]{:S(2)}) %collective-permute-start.17) | collective-permute-done | bytes 196640 | tf_op jit(solution)/shard_map/ppermute | solution.py:23
  106.2 3.0 %collective-permute-start.24 = (bf16[128,2176]{1,0:T(8,128)(2,1)S(1)}, bf16[128,2176]{1,0:T(8,128)(2,1)S(1)}, u32[]{:S(2)}, u32[]{:S(2)}) collective-permute-start(bf16[128,2176]{1,0:T(8,128)(2,1)S(1)} %sum_slots.3), channel_id=1, source_target_pairs={{0,4},{1,5},{2,6},{3,7},{4,0},{5,1},{6,2},{7,3},{8,12},{9,13},{10,... | collective-permute-start | bytes 1671176 | tf_op jit(solution)/shard_map/ppermute | solution.py:23
  110.7 2.9 %weight_sums.5 = (bf16[512,768]{1,0:T(8,128)(2,1)}, bf16[512,768]{1,0:T(8,128)(2,1)}) custom-call(s32[2]{0:T(128)S(1)} %get-tuple-element.128.ids_ref, bf16[48,4096]{1,0:T(8,128)(2,1)S(1)} %get-tuple-element.82.refs_0_, bf16[48,4096]{1,0:T(8,128)(2,1)S(1)} %copy-done.5, bf16[48,4096]{1,0:T(8,128)(2,1)S(1)} %copy-done.7, bf16[48,4096]{1,0:T(8,128)(2,1)S(1)} %copy-done.9, ...), custom_call_target="tpu_custom_call" | custom-call | flops 1 | bytes 1 | tf_op jit(solution)/shard_map/weight_sums/pallas_call | solution.py:475
  116.0 8.8 %collective-permute-done.23.refs_5_ = bf16[48,2048]{1,0:T(8,128)(2,1)S(1)} collective-permute-done((bf16[48,2048]{1,0:T(8,128)(2,1)S(1)}, bf16[48,2048]{1,0:T(8,128)(2,1)S(1)}, u32[]{:S(2)}, u32[]{:S(2)}) %collective-permute-start.23) | collective-permute-done | bytes 196640 | tf_op jit(solution)/shard_map/ppermute | solution.py:23
  124.8 2.4 %sum_slots.4 = bf16[128,2048]{1,0:T(8,128)(2,1)} custom-call(bf16[128,2176]{1,0:T(8,128)(2,1)S(1)} %collective-permute-done.refs_0_.refs_1_, bf16[128,2048]{1,0:T(8,128)(2,1)} %collective-permute-done.4.refs_1_, bf16[48,2048]{1,0:T(8,128)(2,1)S(1)} %get-tuple-element.120.refs_2_, bf16[48,2048]{1,0:T(8,128)(2,1)S(1)} %collective-permute-done.21.refs_3_, ...), custom_call_target="tpu_custom_call" | custom-call | flops 1 | bytes 1 | tf_op jit(solution)/shard_map/sum_slots/pallas_call | solution.py:255
  127.2 4.2 %collective-permute-start.28 = (bf16[128,2048]{1,0:T(8,128)(2,1)}, bf16[128,2048]{1,0:T(8,128)(2,1)S(1)}, u32[]{:S(2)}, u32[]{:S(2)}) collective-permute-start(bf16[128,2048]{1,0:T(8,128)(2,1)} %sum_slots.4), channel_id=1, source_target_pairs={{0,4},{1,5},{2,6},{3,7},{4,0},{5,1},{6,2},{7,3},{8,12},{9,13},{10,... | collective-permute-start | bytes 1572872 | tf_op jit(solution)/shard_map/ppermute | solution.py:23
  132.2 13.2 %collective-permute-done.24.refs_8_ = bf16[128,2176]{1,0:T(8,128)(2,1)S(1)} collective-permute-done((bf16[128,2176]{1,0:T(8,128)(2,1)S(1)}, bf16[128,2176]{1,0:T(8,128)(2,1)S(1)}, u32[]{:S(2)}, u32[]{:S(2)}) %collective-permute-start.24) | collective-permute-done | bytes 557088 | tf_op jit(solution)/shard_map/ppermute | solution.py:23
  147.1 2.9 %weight_sums.6.refs_0_ = f32[512,768]{1,0:T(8,128)S(1)} custom-call(s32[2]{0:T(128)S(1)} %get-tuple-element.128.ids_ref, bf16[48,4096]{1,0:T(8,128)(2,1)} %copy-done.3, bf16[48,4096]{1,0:T(8,128)(2,1)} %copy-done.4, bf16[48,4096]{1,0:T(8,128)(2,1)} %copy-done.6, bf16[48,4096]{1,0:T(8,128)(2,1)} %copy-done.8, bf16[48,2048]{1,0:T(8,128)(2,1)} %copy-done.11, ...), custom_call_target="tpu_custom_call" | custom-call | flops 1 | bytes 1 | tf_op jit(solution)/shard_map/weight_sums/pallas_call | solution.py:475
  152.3 3.9 %weight_sums.7 = (f32[512,768]{1,0:T(8,128)S(1)}, f32[512,768]{1,0:T(8,128)S(1)}) custom-call(s32[2]{0:T(128)S(1)} %get-tuple-element.128.ids_ref, bf16[48,4096]{1,0:T(8,128)(2,1)} %copy-done.3, bf16[48,4096]{1,0:T(8,128)(2,1)} %copy-done.4, bf16[48,4096]{1,0:T(8,128)(2,1)} %copy-done.6, bf16[48,4096]{1,0:T(8,128)(2,1)} %copy-done.8, ...), custom_call_target="tpu_custom_call" | custom-call | flops 1 | bytes 1 | tf_op jit(solution)/shard_map/weight_sums/pallas_call | solution.py:475
  156.2 2.4 %finish_weights.2 = (bf16[512,768]{1,0:T(8,128)(2,1)}, bf16[512,768]{1,0:T(8,128)(2,1)}) custom-call(f32[512,768]{1,0:T(8,128)S(1)} %get-tuple-element.129.refs_0_, f32[512,768]{1,0:T(8,128)S(1)} %get-tuple-element.140.refs_1_, bf16[512,768]{1,0:T(8,128)(2,1)} %collective-permute-done.29.refs_2_, bf16[512,768]{1,0:T(8,128)(2,1)S(1)} %collective-permute-done.30.refs_3_), custom_call_target="tpu_custom_call" | custom-call | flops 1 | bytes 1 | tf_op jit(solution)/shard_map/finish_weights/pallas_call | solution.py:499
  158.6 5.4 %collective-permute-done.27.refs_7_ = bf16[48,4096]{1,0:T(8,128)(2,1)} collective-permute-done((bf16[48,4096]{1,0:T(8,128)(2,1)}, bf16[48,4096]{1,0:T(8,128)(2,1)}, u32[]{:S(2)}, u32[]{:S(2)}) %collective-permute-start.27) | collective-permute-done | bytes 393248 | tf_op jit(solution)/shard_map/ppermute | solution.py:23
  164.0 2.9 %sum_slots.5 = (bf16[128,2048]{1,0:T(8,128)(2,1)}, f32[128,2]{1,0:T(8,128)S(1)}, bf16[128,2048]{1,0:T(8,128)(2,1)}) custom-call(s32[2,128]{1,0:T(2,128)S(1)} %bitcast.8, f32[2,128]{1,0:T(2,128)S(1)} %bitcast.6, f32[128,2]{1,0:T(8,128)S(1)} %copy.14.refs_2_, bf16[128,2048]{1,0:T(8,128)(2,1)S(1)} %copy-done.16, bf16[48,4096]{1,0:T(8,128)(2,1)S(1)} %copy-done.32, ...), custom_call_target="tpu_custom_call" | custom-call | flops 1 | bytes 1 | tf_op jit(solution)/shard_map/sum_slots/pallas_call | solution.py:255
  (132 shorter events, 34.9 us)
Async XLA Ops:
  2.6 28.8 %collective-permute-start = (bf16[128,2176]{1,0:T(8,128)(2,1)S(1)}, bf16[128,2176]{1,0:T(8,128)(2,1)S(1)}, u32[]{:S(2)}, u32[]{:S(2)}) collective-permute-start(bf16[128,2176]{1,0:T(8,128)(2,1)S(1)} %get-tuple-element.75), channel_id=1, source_target_pairs={{0,4},{1,5},{2,6},{3,7},{4,0},{5,1},{6,2},{7,3},{8,12},{9,13},{10,... | collective-permute-start | bytes 1671176 | tf_op jit(solution)/shard_map/ppermute | solution.py:23
  6.7 24.7 %collective-permute-start.1 = (bf16[48,4096]{1,0:T(8,128)(2,1)S(1)}, bf16[48,4096]{1,0:T(8,128)(2,1)S(1)}, u32[]{:S(2)}, u32[]{:S(2)}) collective-permute-start(bf16[48,4096]{1,0:T(8,128)(2,1)S(1)} %get-tuple-element.77), channel_id=1, source_target_pairs={{0,1},{1,0},{2,3},{3,2},{4,5},{5,4},{6,7},{7,6},{8,9},{9,8},{10,11... | collective-permute-start | bytes 1179656 | tf_op jit(solution)/shard_map/ppermute | solution.py:23
  8.2 23.2 %collective-permute-start.2 = (bf16[48,4096]{1,0:T(8,128)(2,1)S(1)}, bf16[48,4096]{1,0:T(8,128)(2,1)S(1)}, u32[]{:S(2)}, u32[]{:S(2)}) collective-permute-start(bf16[48,4096]{1,0:T(8,128)(2,1)S(1)} %get-tuple-element.78), channel_id=1, source_target_pairs={{0,2},{1,3},{2,0},{3,1},{4,6},{5,7},{6,4},{7,5},{8,10},{9,11},{10,... | collective-permute-start | bytes 1179656 | tf_op jit(solution)/shard_map/ppermute | solution.py:23
  9.8 31.2 %collective-permute-start.3 = (bf16[48,4096]{1,0:T(8,128)(2,1)S(1)}, bf16[48,4096]{1,0:T(8,128)(2,1)S(1)}, u32[]{:S(2)}, u32[]{:S(2)}) collective-permute-start(bf16[48,4096]{1,0:T(8,128)(2,1)S(1)} %get-tuple-element.79), channel_id=1, source_target_pairs={{0,3},{1,2},{2,1},{3,0},{4,7},{5,6},{6,5},{7,4},{8,11},{9,10},{10,... | collective-permute-start | bytes 1179656 | tf_op jit(solution)/shard_map/ppermute | solution.py:23
  31.4 25.7 %collective-permute-start.4 = (bf16[128,2048]{1,0:T(8,128)(2,1)}, bf16[128,2048]{1,0:T(8,128)(2,1)}, u32[]{:S(2)}, u32[]{:S(2)}) collective-permute-start(bf16[128,2048]{1,0:T(8,128)(2,1)} %refs_3_.3), channel_id=1, source_target_pairs={{0,4},{1,5},{2,6},{3,7},{4,0},{5,1},{6,2},{7,3},{8,12},{9,13},{10,... | collective-permute-start | bytes 1572872 | tf_op jit(solution)/shard_map/ppermute | solution.py:23
  41.6 18.4 %collective-permute-start.9 = (bf16[48,2048]{1,0:T(8,128)(2,1)S(1)}, bf16[48,2048]{1,0:T(8,128)(2,1)S(1)}, u32[]{:S(2)}, u32[]{:S(2)}) collective-permute-start(bf16[48,2048]{1,0:T(8,128)(2,1)S(1)} %get-tuple-element.93), channel_id=1, source_target_pairs={{0,1},{1,0},{2,3},{3,2},{4,5},{5,4},{6,7},{7,6},{8,9},{9,8},{10,11... | collective-permute-start | bytes 589832 | tf_op jit(solution)/shard_map/ppermute | solution.py:23
  43.5 16.5 %collective-permute-start.10 = (bf16[48,2048]{1,0:T(8,128)(2,1)S(1)}, bf16[48,2048]{1,0:T(8,128)(2,1)S(1)}, u32[]{:S(2)}, u32[]{:S(2)}) collective-permute-start(bf16[48,2048]{1,0:T(8,128)(2,1)S(1)} %get-tuple-element.94), channel_id=1, source_target_pairs={{0,2},{1,3},{2,0},{3,1},{4,6},{5,7},{6,4},{7,5},{8,10},{9,11},{10,... | collective-permute-start | bytes 589832 | tf_op jit(solution)/shard_map/ppermute | solution.py:23
  43.5 17.2 %collective-permute-start.11 = (bf16[48,2048]{1,0:T(8,128)(2,1)S(1)}, bf16[48,2048]{1,0:T(8,128)(2,1)S(1)}, u32[]{:S(2)}, u32[]{:S(2)}) collective-permute-start(bf16[48,2048]{1,0:T(8,128)(2,1)S(1)} %get-tuple-element.95), channel_id=1, source_target_pairs={{0,3},{1,2},{2,1},{3,0},{4,7},{5,6},{6,5},{7,4},{8,11},{9,10},{10,... | collective-permute-start | bytes 589832 | tf_op jit(solution)/shard_map/ppermute | solution.py:23
  55.7 24.0 %collective-permute-start.13 = (bf16[192,2304]{1,0:T(8,128)(2,1)S(1)}, bf16[192,2304]{1,0:T(8,128)(2,1)S(1)}, u32[]{:S(2)}, u32[]{:S(2)}) collective-permute-start(bf16[192,2304]{1,0:T(8,128)(2,1)S(1)} %get-tuple-element.102.refs_10_.refs_14_), channel_id=1, source_target_pairs={{0,8},{8,0},{16,24},{24,16},{1,9},{9,1},{17,25},{25,17},{2,10},{10... | collective-permute-start | bytes 2654216 | tf_op jit(solution)/shard_map/ppermute | solution.py:23
  59.9 19.7 %collective-permute-start.8 = (bf16[192,2048]{1,0:T(8,128)(2,1)S(1)}, bf16[192,2048]{1,0:T(8,128)(2,1)S(1)}, u32[]{:S(2)}, u32[]{:S(2)}) collective-permute-start(bf16[192,2048]{1,0:T(8,128)(2,1)S(1)} %get-tuple-element.86), channel_id=1, source_target_pairs={{0,8},{8,0},{16,24},{24,16},{1,9},{9,1},{17,25},{25,17},{2,10},{10... | collective-permute-start | bytes 2359304 | tf_op jit(solution)/shard_map/ppermute | solution.py:23
  66.2 13.4 %collective-permute-start.14 = (bf16[192,1792]{1,0:T(8,128)(2,1)S(1)}, bf16[192,1792]{1,0:T(8,128)(2,1)S(1)}, u32[]{:S(2)}, u32[]{:S(2)}) collective-permute-start(bf16[192,1792]{1,0:T(8,128)(2,1)S(1)} %get-tuple-element.103), channel_id=1, source_target_pairs={{0,8},{8,0},{16,24},{24,16},{1,9},{9,1},{17,25},{25,17},{2,10},{10... | collective-permute-start | bytes 2064392 | tf_op jit(solution)/shard_map/ppermute | solution.py:23
  67.6 11.3 %collective-permute-start.7 = (bf16[48,2048]{1,0:T(8,128)(2,1)S(1)}, bf16[48,2048]{1,0:T(8,128)(2,1)S(1)}, u32[]{:S(2)}, u32[]{:S(2)}) collective-permute-start(bf16[48,2048]{1,0:T(8,128)(2,1)S(1)} %get-tuple-element.92), channel_id=1, source_target_pairs={{0,3},{1,2},{2,1},{3,0},{4,7},{5,6},{6,5},{7,4},{8,11},{9,10},{10,... | collective-permute-start | bytes 589832 | tf_op jit(solution)/shard_map/ppermute | solution.py:23
  82.7 33.0 %collective-permute-start.20 = (bf16[512,768]{1,0:T(8,128)(2,1)S(1)}, bf16[512,768]{1,0:T(8,128)(2,1)S(1)}, u32[]{:S(2)}, u32[]{:S(2)}) collective-permute-start(bf16[512,768]{1,0:T(8,128)(2,1)S(1)} %weight_sums.4), channel_id=1, source_target_pairs={{0,16},{8,24},{16,0},{24,8},{1,17},{9,25},{17,1},{25,9},{2,18},{10... | collective-permute-start | bytes 2359304 | tf_op jit(solution)/shard_map/ppermute | solution.py:23
  91.1 15.1 %collective-permute-start.19 = (bf16[192,768]{1,0:T(8,128)(2,1)S(1)}, bf16[192,768]{1,0:T(8,128)(2,1)S(1)}, u32[]{:S(2)}, u32[]{:S(2)}) collective-permute-start(bf16[192,768]{1,0:T(8,128)(2,1)S(1)} %get-tuple-element.117.refs_15_), channel_id=1, source_target_pairs={{0,8},{8,0},{16,24},{24,16},{1,9},{9,1},{17,25},{25,17},{2,10},{10... | collective-permute-start | bytes 884744 | tf_op jit(solution)/shard_map/ppermute | solution.py:23
  92.2 11.8 %collective-permute-start.17 = (bf16[48,2048]{1,0:T(8,128)(2,1)S(1)}, bf16[48,2048]{1,0:T(8,128)(2,1)S(1)}, u32[]{:S(2)}, u32[]{:S(2)}) collective-permute-start(bf16[48,2048]{1,0:T(8,128)(2,1)S(1)} %get-tuple-element.115), channel_id=1, source_target_pairs={{0,3},{1,2},{2,1},{3,0},{4,7},{5,6},{6,5},{7,4},{8,11},{9,10},{10,... | collective-permute-start | bytes 589832 | tf_op jit(solution)/shard_map/ppermute | solution.py:23
  94.5 14.7 %collective-permute-start.18 = (bf16[192,768]{1,0:T(8,128)(2,1)S(1)}, bf16[192,768]{1,0:T(8,128)(2,1)S(1)}, u32[]{:S(2)}, u32[]{:S(2)}) collective-permute-start(bf16[192,768]{1,0:T(8,128)(2,1)S(1)} %get-tuple-element.110.refs_11_), channel_id=1, source_target_pairs={{0,8},{8,0},{16,24},{24,16},{1,9},{9,1},{17,25},{25,17},{2,10},{10... | collective-permute-start | bytes 884744 | tf_op jit(solution)/shard_map/ppermute | solution.py:23
  99.0 14.7 %collective-permute-start.21 = (bf16[48,2048]{1,0:T(8,128)(2,1)S(1)}, bf16[48,2048]{1,0:T(8,128)(2,1)S(1)}, u32[]{:S(2)}, u32[]{:S(2)}) collective-permute-start(bf16[48,2048]{1,0:T(8,128)(2,1)S(1)} %get-tuple-element.121), channel_id=1, source_target_pairs={{0,1},{1,0},{2,3},{3,2},{4,5},{5,4},{6,7},{7,6},{8,9},{9,8},{10,11... | collective-permute-start | bytes 589832 | tf_op jit(solution)/shard_map/ppermute | solution.py:23
  106.2 39.2 %collective-permute-start.24 = (bf16[128,2176]{1,0:T(8,128)(2,1)S(1)}, bf16[128,2176]{1,0:T(8,128)(2,1)S(1)}, u32[]{:S(2)}, u32[]{:S(2)}) collective-permute-start(bf16[128,2176]{1,0:T(8,128)(2,1)S(1)} %sum_slots.3), channel_id=1, source_target_pairs={{0,4},{1,5},{2,6},{3,7},{4,0},{5,1},{6,2},{7,3},{8,12},{9,13},{10,... | collective-permute-start | bytes 1671176 | tf_op jit(solution)/shard_map/ppermute | solution.py:23
  109.2 22.2 %collective-permute-start.25 = (bf16[48,4096]{1,0:T(8,128)(2,1)S(1)}, bf16[48,4096]{1,0:T(8,128)(2,1)S(1)}, u32[]{:S(2)}, u32[]{:S(2)}) collective-permute-start(bf16[48,4096]{1,0:T(8,128)(2,1)S(1)} %get-tuple-element.126), channel_id=1, source_target_pairs={{0,1},{1,0},{2,3},{3,2},{4,5},{5,4},{6,7},{7,6},{8,9},{9,8},{10,11... | collective-permute-start | bytes 1179656 | tf_op jit(solution)/shard_map/ppermute | solution.py:23
  113.7 42.6 %collective-permute-start.30 = (bf16[512,768]{1,0:T(8,128)(2,1)}, bf16[512,768]{1,0:T(8,128)(2,1)S(1)}, u32[]{:S(2)}, u32[]{:S(2)}) collective-permute-start(bf16[512,768]{1,0:T(8,128)(2,1)} %get-tuple-element.141), channel_id=1, source_target_pairs={{0,16},{8,24},{16,0},{24,8},{1,17},{9,25},{17,1},{25,9},{2,18},{10... | collective-permute-start | bytes 2359304 | tf_op jit(solution)/shard_map/ppermute | solution.py:23
  114.2 42.0 %collective-permute-start.29 = (bf16[512,768]{1,0:T(8,128)(2,1)}, bf16[512,768]{1,0:T(8,128)(2,1)}, u32[]{:S(2)}, u32[]{:S(2)}) collective-permute-start(bf16[512,768]{1,0:T(8,128)(2,1)} %get-tuple-element.118), channel_id=1, source_target_pairs={{0,16},{8,24},{16,0},{24,8},{1,17},{9,25},{17,1},{25,9},{2,18},{10... | collective-permute-start | bytes 2359304 | tf_op jit(solution)/shard_map/ppermute | solution.py:23
  127.2 36.8 %collective-permute-start.28 = (bf16[128,2048]{1,0:T(8,128)(2,1)}, bf16[128,2048]{1,0:T(8,128)(2,1)S(1)}, u32[]{:S(2)}, u32[]{:S(2)}) collective-permute-start(bf16[128,2048]{1,0:T(8,128)(2,1)} %sum_slots.4), channel_id=1, source_target_pairs={{0,4},{1,5},{2,6},{3,7},{4,0},{5,1},{6,2},{7,3},{8,12},{9,13},{10,... | collective-permute-start | bytes 1572872 | tf_op jit(solution)/shard_map/ppermute | solution.py:23
  132.2 26.4 %collective-permute-start.26 = (bf16[48,4096]{1,0:T(8,128)(2,1)}, bf16[48,4096]{1,0:T(8,128)(2,1)S(1)}, u32[]{:S(2)}, u32[]{:S(2)}) collective-permute-start(bf16[48,4096]{1,0:T(8,128)(2,1)} %get-tuple-element.135), channel_id=1, source_target_pairs={{0,2},{1,3},{2,0},{3,1},{4,6},{5,7},{6,4},{7,5},{8,10},{9,11},{10,... | collective-permute-start | bytes 1179656 | tf_op jit(solution)/shard_map/ppermute | solution.py:23
  146.2 17.8 %collective-permute-start.27 = (bf16[48,4096]{1,0:T(8,128)(2,1)}, bf16[48,4096]{1,0:T(8,128)(2,1)}, u32[]{:S(2)}, u32[]{:S(2)}) collective-permute-start(bf16[48,4096]{1,0:T(8,128)(2,1)} %get-tuple-element.136), channel_id=1, source_target_pairs={{0,3},{1,2},{2,1},{3,0},{4,7},{5,6},{6,5},{7,4},{8,11},{9,10},{10,... | collective-permute-start | bytes 1179656 | tf_op jit(solution)/shard_map/ppermute | solution.py:23
  (44 other events, 883.8 us)

commit v4 on v3

--- a/solution.py
+++ b/solution.py
@@ -23,8 +23,9 @@
     return lax.ppermute(x, axis, [(i, i ^ bit) for i in range(size)])
 
 
-def within_half(blocks):
-    return [blocks[0]] + [exchange(blocks[s], "exp", s) for s in range(1, len(blocks))]
+def within_half(blocks, places=None):
+    places = range(len(blocks)) if places is None else places
+    return [exchange(blocks[s], "exp", s) if s else blocks[0] for s in places]
 
 
 def in_hbm(arrays):
@@ -39,8 +40,8 @@
     return pltpu.CompilerParams(vmem_limit_bytes=24 * 1024 * 1024, **kw)
 
 
-def cost(flops, bytes_accessed):
-    return pl.CostEstimate(flops=1, bytes_accessed=1, transcendentals=0)
+def cost(weight):
+    return pl.CostEstimate(flops=1 + int(weight * 7.5e9), bytes_accessed=1, transcendentals=0)
 
 
 def after(value, *earlier):
@@ -58,12 +59,9 @@
     def shapes(self, width):
         return [result((self.height, width), bf16)] * self.count
 
-    def send(self, arrays, early=None):
+    def send(self, arrays, places=None):
         if self.split:
-            if early is not None:
-                number, first, then = early
-                arrays = after(arrays[:number], first) + after(arrays[number:], then)
-            return within_half(arrays)
+            return within_half(arrays, places)
         blocks = [arrays[0][s * self.capacity : (s + 1) * self.capacity] for s in range(self.half)]
         return [jnp.concatenate(within_half(blocks), axis=0)]
 
@@ -71,6 +69,10 @@
 def join(refs, cols=slice(None)):
     parts = [r[:, cols] for r in refs]
     return parts[0] if len(parts) == 1 else jnp.concatenate(parts, axis=0)
+
+
+def turned(blocks):
+    return list(blocks[:1]) + list(blocks[1:])[::-1]
 
 
 def store(refs, cols, value):
@@ -162,7 +164,7 @@
     return pl.BlockSpec(shape, lambda i: (0, 0))
 
 
-def gather(form, meta, arrays, scaled, width):
+def gather(form, meta, arrays, scaled, width, weight=0.0):
     tokens = arrays[0].shape[0]
     total = width * len(arrays)
     plain = len(meta) == 2
@@ -176,7 +178,7 @@
         in_specs=meta_specs(meta, width) + [whole_spec((tokens, width)) for _ in arrays],
         out_specs=[whole_spec(x.shape) for x in out_shape],
         compiler_params=params(),
-        cost_estimate=cost(2 * form.rows * tokens * total, 4 * form.rows * total),
+        cost_estimate=cost(weight),
         name="gather_slots",
     )(*(in_hbm([*meta, *arrays]) if plain else [*meta, *arrays]))
     return list(out)
@@ -190,8 +192,8 @@
     else:
         meta, weights = packed_rows(refs[0]), packed_columns(refs[0])[2:]
         refs = refs[1:]
-    cot_ref, rows, refs = refs[0], refs[1 : 1 + count], refs[1 + count :]
-    others, outs = (list(refs[:2]), list(refs[2:])) if more else ([], list(refs))
+    cot_ref, rows, refs = refs[0], turned(refs[1 : 1 + count]), refs[1 + count :]
+    others, outs = (list(refs[:1]), list(refs[1:])) if more else ([], list(refs))
     plan = [p.astype(bf16) for p in slot_plan(meta, form)]
     out_at, grad_at = offsets
     width = cot_ref.shape[1]
@@ -202,17 +204,15 @@
         outs[i][:, cols] = value.astype(outs[i].dtype)
 
     def put_grad(cols, value):
+        outs[-1][:, cols] = value.astype(outs[-1].dtype)
+
+    def put_sums(sums):
+        lane = lax.broadcasted_iota(jnp.int32, (sums[0].shape[0], 128), 1)
         if more:
-            value = value + others[1][:, cols].astype(f32)
-        outs[-1][:, cols] = value.astype(bf16)
-
-    def put_sums(sums):
-        if more:
-            tail = others[0][:, width:].astype(f32)
-            for k in range(2):
-                outs[1][:, k : k + 1] = sums[k] + tail[:, k : k + 1] + tail[:, 2 + k : 3 + k] + tail[:, 4 + k : 5 + k]
+            tail = jnp.transpose(others[0][:, width:].astype(f32))
+            rows = jnp.transpose(jnp.where(lane == 0, sums[0], jnp.where(lane == 1, sums[1], 0.0)))
+            outs[1][...] = rows[0:2] + tail[0:2] + tail[2:4] + tail[4:6]
             return
-        lane = lax.broadcasted_iota(jnp.int32, (sums[0].shape[0], 128), 1)
         tail = jnp.zeros(lane.shape, f32)
         for k in range(2):
             rest = sums[k]
@@ -241,17 +241,17 @@
             put_grad(cols, dot(either, block, ((0,), (0,))))
 
 
-def back(form, meta, cot, rows, offsets, combine=None, others=()):
+def back(form, meta, cot, rows, offsets, combine=None, others=(), weight=0.0):
     tokens, width = cot.shape
     shapes = []
     if offsets[0] is not None:
         shapes += [result((tokens, width + (0 if others else 128)), bf16)]
     if others:
-        shapes += [result((tokens, 2), f32)]
+        shapes += [result((2, tokens), f32)]
     if offsets[1] is not None:
-        shapes += [result((tokens, width), bf16)]
+        shapes += [jax.ShapeDtypeStruct((tokens, width), f32 if others else bf16)]
     own = [] if combine is None else [combine]
-    arrays = own + [cot] + list(rows) + list(others)
+    arrays = own + [cot] + turned(rows) + list(others)
     return pl.pallas_call(
         functools.partial(back_kernel, form, offsets, combine is not None, len(others) > 0),
         grid=(1,),
@@ -259,7 +259,7 @@
         in_specs=meta_specs(meta, width) + [whole_spec(a.shape) for a in arrays],
         out_specs=[whole_spec(x.shape) for x in shapes],
         compiler_params=params(),
-        cost_estimate=cost(4 * form.rows * tokens * width, 4 * form.rows * width),
+        cost_estimate=cost(weight),
         name="sum_slots",
     )(*meta, *arrays)
 
@@ -306,10 +306,10 @@
 
 
 def pick_kernel(count, ids_ref, *refs):
-    pick(ids_ref, refs[:count], 0, refs[count], 0, refs[0].shape[1])
-
-
-def pick_shares(form, ids, arrays):
+    pick(ids_ref, turned(refs[:count]), 0, refs[count], 0, refs[0].shape[1])
+
+
+def pick_shares(form, ids, arrays, weight=0.0):
     width = arrays[0].shape[1]
     return pl.pallas_call(
         functools.partial(pick_kernel, form.count),
@@ -317,13 +317,13 @@
         in_specs=[SMEM] + [VMEM] * form.count,
         out_specs=VMEM,
         compiler_params=params(),
-        cost_estimate=cost(1, 1),
+        cost_estimate=cost(weight),
         name="pick_shares",
-    )(ids, *arrays)
+    )(ids, *turned(arrays))
 
 
 def forward_kernel(count, *refs):
-    x_refs, ids_ref, held = refs[:count], refs[count], refs[count + 1 : count + 4]
+    x_refs, ids_ref, held = turned(refs[:count]), refs[count], refs[count + 1 : count + 4]
     out_refs = refs[count + 4 : 2 * count + 4]
     swap_ref, hidden_ref, active_ref, slope_ref, acc, gate_ref, up_ref, down_ref, sems = refs[2 * count + 4 :]
     wait = fetch(held, (gate_ref, up_ref, down_ref), sems, tiles(hidden_ref.shape[1]))
@@ -345,11 +345,11 @@
     store(out_refs, slice(None), acc[...])
 
 
-def expert_call(kernel, form, inputs, weights, more, out_width, inner_types, name):
+def expert_call(kernel, form, inputs, weights, more, out_width, inner_types, name, weight=0.0):
     _, width, ff = weights[0].shape
     rows = form.rows
     out_shape = form.shapes(out_width) + [jax.ShapeDtypeStruct((rows, w), t) for w, t in inner_types]
-    operands = [*inputs, *more]
+    operands = [*turned(inputs), *more]
     out = pl.pallas_call(
         functools.partial(kernel, form.count),
         out_shape=out_shape,
@@ -359,20 +359,20 @@
         + [pltpu.VMEM((width, ff), bf16)] * 3
         + [pltpu.SemaphoreType.DMA((3, len(tiles(ff))))],
         compiler_params=params(),
-        cost_estimate=cost(6 * rows * width * ff, 6 * width * ff),
+        cost_estimate=cost(weight),
         name=name,
     )(*operands, *in_hbm(weights))
     return list(out[: form.count]), *out[form.count :]
 
 
-def forward(form, x, ids, *weights):
+def forward(form, x, ids, *weights, weight=0.0):
     _, width, ff = weights[0].shape
     types = [(width // 2 + ff, bf16), (ff, bf16), (ff, f32), (ff, f32)]
-    return expert_call(forward_kernel, form, x, weights, [ids], width, types, "expert_forward")
+    return expert_call(forward_kernel, form, x, weights, [ids], width, types, "expert_forward", weight)
 
 
 def backward_kernel(count, *refs):
-    c_refs, active_ref, slope_ref, held = refs[:count], refs[count], refs[count + 1], refs[count + 2 : count + 5]
+    c_refs, active_ref, slope_ref, held = turned(refs[:count]), refs[count], refs[count + 1], refs[count + 2 : count + 5]
     in_refs = refs[count + 5 : 2 * count + 5]
     gg_ref, gu_ref, acc, gate_ref, up_ref, down_ref, sems = refs[2 * count + 5 :]
     wait = fetch(held, (gate_ref, up_ref, down_ref), sems, tiles(gg_ref.shape[1]))
@@ -390,14 +390,14 @@
     store(in_refs, slice(None), acc[...])
 
 
-def backward(form, c, active, slope, *weights):
+def backward(form, c, active, slope, *weights, weight=0.0):
     more = [active, slope]
     _, width, ff = weights[0].shape
-    return expert_call(backward_kernel, form, c, weights, more, width, [(ff, bf16)] * 2, "expert_backward")
+    return expert_call(backward_kernel, form, c, weights, more, width, [(ff, bf16)] * 2, "expert_backward", weight)
 
 
 def both_kernel(count, *refs):
-    in_refs, ids_ref, held = refs[:count], refs[count], refs[count + 1 : count + 4]
+    in_refs, ids_ref, held = turned(refs[:count]), refs[count], refs[count + 1 : count + 4]
     out_refs = refs[count + 4 : 2 * count + 4]
     picked_ref, inner_ref, acc, gate_ref, up_ref, down_ref, sems = refs[2 * count + 4 :]
     width, ff = acc.shape[1] // 2, gate_ref.shape[1]
@@ -431,31 +431,27 @@
     return expert_call(both_kernel, form, rows_in, weights, [ids], 2 * width, [(width, bf16), (3 * ff, bf16)], "expert_both")
 
 
-def weight_kernel(counts, adds, scale, ids_ref, *refs):
+def weight_kernel(counts, number, ids_ref, *refs):
     groups = []
     for n in counts:
-        groups.append(join(refs[:n]))
+        groups.append(join(turned(refs[:n])))
         refs = refs[n:]
     left = jnp.concatenate(groups, axis=0)
-    number = len(refs) // (len(counts) + adds + 1)
-    rights, refs = refs[: number * len(counts)], refs[number * len(counts) :]
-    others, outs = refs[:-number], refs[-number:]
+    rights, outs = refs[: number * len(counts)], refs[number * len(counts) :]
+    if len(outs) < number:
+        ff = outs[0].shape[1] // number
+        outs = [outs[0].at[:, i * ff : (i + 1) * ff] for i in range(number)]
     for i in range(number):
         right = jnp.concatenate([r[...] for r in rights[i * len(counts) : (i + 1) * len(counts)]], axis=0)
-        sums = dot(left, right, ((0,), (0,)))
-        if adds:
-            sums = sums + others[i][...].astype(f32)
-        if scale:
-            sums = sums * grad_scale
-        outs[i][...] = sums.astype(outs[i].dtype)
-
-
-def weight_sums(form, ids, at, left, rights, share, ff, add=None, scale=False, dtype=bf16, hbm=False):
+        outs[i][...] = dot(left, right, ((0,), (0,))).astype(outs[i].dtype)
+
+
+def weight_sums(form, ids, at, left, rights, share, ff, dtype=bf16, hbm=False, beside=False, weight=0.0):
     first, steps = at[0], at[1] - at[0]
     arrays, specs = [], []
     for held, column, picked in left:
         block = column // share
-        for h in held:
+        for h in turned(held):
             arrays.append(h)
             if picked:
                 specs.append(pl.BlockSpec((h.shape[0], share), lambda i, ids_ref, b=block: (0, b + first + i)))
@@ -465,15 +461,12 @@
         for array, column in right:
             arrays.append(array)
             specs.append(pl.BlockSpec((form.rows, ff), lambda i, ids_ref, b=column // ff: (0, b)))
-    for array, column in add or []:
-        arrays.append(array)
-        specs.append(pl.BlockSpec((share, ff), lambda i, ids_ref, b=column // ff: (i, b)))
     number = len(rights)
-    widths = [ff] * number
+    widths = [number * ff] if beside else [ff] * number
     if hbm:
         arrays = in_hbm(arrays)
     return pl.pallas_call(
-        functools.partial(weight_kernel, [len(g[0]) for g in left], 1 if add else 0, scale),
+        functools.partial(weight_kernel, [len(g[0]) for g in left], number),
         grid_spec=pltpu.PrefetchScalarGridSpec(
             num_scalar_prefetch=1,
             grid=(steps,),
@@ -482,9 +475,28 @@
         ),
         out_shape=[jax.ShapeDtypeStruct((steps * share, w), dtype) for w in widths],
         compiler_params=params(),
-        cost_estimate=cost(1, 1),
+        cost_estimate=cost(weight),
         name="weight_sums",
     )(ids, *arrays)
+
+
+def add_kernel(a_ref, b_ref, out_ref):
+    out_ref[...] = (a_ref[...] + b_ref[...].astype(f32)).astype(bf16)
+
+
+def add_up(a, b):
+    rows, width = a.shape
+    block = pl.BlockSpec((rows, width // 2), lambda i: (0, i))
+    return pl.pallas_call(
+        add_kernel,
+        grid=(2,),
+        out_shape=result((rows, width), bf16),
+        in_specs=[block] * 2,
+        out_specs=block,
+        compiler_params=params(),
+        cost_estimate=cost(0),
+        name="add_halves",
+    )(a, b)
 
 
 def finish_kernel(number, *refs):
@@ -492,20 +504,20 @@
         out[...] = ((keep[...] + got[...].astype(f32)) * grad_scale).astype(bf16)
 
 
-def finish(keeps, gots):
-    number = len(keeps)
-    rows, ff = keeps[0].shape
+def finish(keep, got, number, weight=0.0):
+    rows, ff = keep.shape[0], keep.shape[1] // number
     tile = rows // 2
+    sides = [pl.BlockSpec((tile, ff), lambda i, n=n: (i, n)) for n in range(number)]
     return pl.pallas_call(
         functools.partial(finish_kernel, number),
         grid=(rows // tile,),
         out_shape=[result((rows, ff), bf16)] * number,
-        in_specs=[pl.BlockSpec((tile, ff), lambda i: (i, 0))] * (2 * number),
+        in_specs=sides * 2,
         out_specs=[pl.BlockSpec((tile, ff), lambda i: (i, 0))] * number,
         compiler_params=params(),
-        cost_estimate=cost(1, 1),
+        cost_estimate=cost(weight),
         name="finish_weights",
-    )(*keeps, *gots)
+    )(*[keep] * number, *[got] * number)
 
 
 def local(hits, cotangent, combine, expert_ids, gate_weight, up_weight, down_weight):
@@ -537,33 +549,44 @@
     picked_got, inner_got = swap(own_picked), swap(own_inner)
     c1_sent = gather(form, after(far_meta, own_picked), [far_cot], (True,), width)
     c1 = form.send(c1_sent)
-    out1, x1_swap, hidden1, active1, slope1 = forward(form, after(x1, c1_sent[0]), theirs, *weights)
+    out1, x1_swap, hidden1, active1, slope1 = forward(form, after(x1, c1_sent[0]), theirs, *weights, weight=0.25)
     x1_got = swap(x1_swap)
     out1_back = form.send(out1)
 
     on, all_ = copies // 4, copies // 2
     half_width = width // 2
-    c1_got = swap(pick_shares(form, after(theirs, hidden1), c1))
+    c1_got = swap(pick_shares(form, after(theirs, hidden1), c1, weight=0.35))
     x_left = [(own, 0, False), (x1, 0, False), ([picked_got], 0, True), ([x1_got], 0, True)]
     c_left = [(own, width, False), (c1, 0, False), ([picked_got], half_width, True), ([c1_got], 0, True)]
     at_hidden, at_gate, at_up = [i * ff for i in range(3)]
 
-    def right(far, far_got, column, far_column=0):
-        return [(own_inner, column), (far, 0), (inner_got, column), (far_got, far_column)]
+    def right(far, far_got, column):
+        return [(own_inner, column), (far, 0), (inner_got, column), (far_got, 0)]
 
     hidden1_got = x1_got[:, half_width:]
     down = [right(hidden1, hidden1_got, at_hidden)]
     (down_on,) = weight_sums(form, ours, (0, on), c_left, down, share, ff)
     down_there = exchange(down_on, "ctx", 2)
-    gin1, gg1, gu1 = backward(form, after(c1, down_on), active1, slope1, *weights)
+    early = (form.half - 1,) if form.split else ()
+    back0_first = form.send(after(back0, down_on), early) if early else []
+    gin1, gg1, gu1 = backward(form, after(c1, down_on), active1, slope1, *weights, weight=0.5)
     gin1_back = form.send(gin1)
-    (far_mixed,) = back(form, after(far_meta, gg1), far_cot, out1_back, (0, None))
+    (far_mixed,) = back(form, after(far_meta, gg1), far_cot, out1_back, (0, None), weight=0.3)
     got_mixed = exchange(far_mixed, "exp", half)
     both_rights = [right(gg1, swap(gg1), at_gate), right(gu1, swap(gu1), at_up)]
-    gate_on, up_on = weight_sums(form, after(ours, far_mixed), (0, on), x_left, both_rights, share, ff)
-    gate_there, up_there = exchange(gate_on, "ctx", 2), exchange(up_on, "ctx", 2)
-    (far_grad,) = back(form, after(far_meta, gate_on, down_there), far_cot, gin1_back, (None, 0))
+    (both_on,) = weight_sums(
+        form, after(ours, far_mixed, back0_first), (0, on), x_left, both_rights, share, ff, beside=True, weight=0.3
+    )
+    both_there = exchange(both_on, "ctx", 2)
+    (far_grad,) = back(
+        form, after(far_meta, both_on, down_there), far_cot, gin1_back, (None, 0), weight=1.8
+    )
     got_grad = exchange(far_grad, "exp", half)
+    late = [p for p in range(form.half) if p not in early] if form.split else None
+    back0_got = back0_first + form.send(after(back0, far_grad), late)
+    if early:
+        places = list(early) + late
+        back0_got = [back0_got[places.index(p)] for p in range(form.half)]
 
     def last_bits(keep, got):
         bit = 4
@@ -574,25 +597,36 @@
             bit *= 2
         return keep, got
 
-    back0_got = form.send(back0, (2, down_on, far_grad))
-    (down_keep,) = weight_sums(form, after(ours, far_grad, got_mixed, back0_got[1 % form.count]), (on, all_), c_left, down, share, ff, dtype=f32, hbm=True)
-    gate_keep, up_keep = weight_sums(
-        form, after(ours, down_keep), (on, all_), x_left, both_rights, share, ff, dtype=f32, hbm=True
+    (down_keep,) = weight_sums(
+        form, after(ours, far_grad), (on, all_), c_left, down, share, ff, dtype=f32, hbm=True, weight=0.35
     )
-    mixed, combine_grads, input_grads = back(
+    (down_grads,) = finish(*last_bits(down_keep, down_there), 1)
+    (both_keep,) = weight_sums(
         form,
-        after(meta, gate_keep),
+        after(ours, down_keep, got_mixed),
+        (on, all_),
+        x_left,
+        both_rights,
+        share,
+        ff,
+        dtype=f32,
+        hbm=True,
+        beside=True,
+        weight=0.2,
+    )
+    gate_grads, up_grads = finish(*last_bits(both_keep, both_there), 2, weight=0.1)
+    mixed, combine_grads, own_grad = back(
+        form,
+        after(meta, gate_grads),
         cotangent,
         back0_got,
         (0, width),
         combine,
-        (got_mixed, got_grad),
+        (got_mixed,),
+        weight=0.0,
     )
-    down_grads, gate_grads, up_grads = [
-        finish([k for k, _ in pairs], [g for _, g in pairs])
-        for pairs in [[last_bits(down_keep, down_there)]]
-    ][0] + finish(*zip(*[last_bits(gate_keep, gate_there), last_bits(up_keep, up_there)]))
-    return (mixed, input_grads, combine_grads, gate_grads[None], up_grads[None], down_grads[None])
+    input_grads = add_up(own_grad, got_grad)
+    return (mixed, input_grads, combine_grads.T, gate_grads[None], up_grads[None], down_grads[None])
 
 
 def solution(mesh):

time: 168 us -> 147 us (0.88)
  waiting for transfers between devices: 79.1 us -> 55.2 us
  Pallas kernels: 47.2 us -> 50.2 us
    ppermute x31 -> x30, waiting for transfers between devices: 79.1 us -> 55.2 us  [exchange(): return lax.ppermute(x, axis, [(i, i ^ bit) for i in range(size)])]
    pallas_call x0 -> x1, Pallas kernels: none -> 1.83 us  [add_up(): pl.pallas_call(add_kernel, grid=(2,), out_shape=result((rows, width), bf1...]
    ppermute x31 -> x30, starting transfers between devices: 35.1 us -> 36.1 us  [exchange(): return lax.ppermute(x, axis, [(i, i ^ bit) for i in range(size)])]
    unnamed x76 -> x75, local copies, waits for them, and re-layouts: 4.36 us -> 3.52 us
  transfers between devices with their start and end apart: 31 -> 30, of which waited for: 12 -> 9; matrix products, arithmetic and copies ran while one was open for 0% -> 1% of each run, Pallas kernels for 24% -> 31%
where the time goes in v4:
time: 147 us
  waiting for transfers between devices  55.2 us (38%)
  Pallas kernels  50.2 us (34%)
  starting transfers between devices  36.1 us (25%)
  local copies, waits for them, and re-layouts  3.54 us (2%)
    ppermute x30, waiting for transfers between devices, exchange(): return lax.ppermute(x, axis, [(i, i ^ bit) for i in range(size)])  55.2 us
    ppermute x30, starting transfers between devices, exchange(): return lax.ppermute(x, axis, [(i, i ^ bit) for i in range(size)])  36.1 us
    pallas_call x3, Pallas kernels, expert_call(): pl.pallas_call(functools.partial(kernel, form.count), out_shape=out_shape...  21 us
    pallas_call x4, Pallas kernels, weight_sums(): pl.pallas_call(functools.partial(weight_kernel, [len(g[0]) for g in left]...  11.4 us
    pallas_call x3, Pallas kernels, back(): pl.pallas_call(functools.partial(back_kernel, form, offsets, combine is n...  8.01 us
    pallas_call x3, Pallas kernels, gather(): pl.pallas_call(functools.partial(gather_kernel, form, scaled, width, plai...  4.8 us
    unnamed x75, local copies, waits for them, and re-layouts  3.52 us
  transfers between devices with their start and end apart: 30, of which 9 were waited for; matrix products, arithmetic and copies ran while one was open for 1% of the time, Pallas kernels for 31%

profile of v4, /device:TPU:0, one launch (start us, length us, event | category | flops | bytes accessed | tf_op | source)
XLA Modules:
  0.0 146.9 jit_solution(7845650084314254515)
XLA Ops:
  0.6 2.7 %gather_slots.3 = (bf16[48,4096]{1,0:T(8,128)(2,1)S(1)}, bf16[48,4096]{1,0:T(8,128)(2,1)}, bf16[48,4096]{1,0:T(8,128)(2,1)S(1)}, bf16[48,4096]{1,0:T(8,128)(2,1)S(1)}, bf16[128,2176]{1,0:T(8,128)(2,1)S(1)}) custom-call(s32[2,128]{1,0:T(2,128)} %bitcast.8, f32[2,128]{1,0:T(2,128)} %bitcast.6, bf16[128,2048]{1,0:T(8,128)(2,1)} %refs_2_.2, ...), custom_call_target="tpu_custom_call" | custom-call | flops 1 | bytes 1 | tf_op jit(solution)/shard_map/gather_slots/pallas_call | solution.py:174
  3.3 4.0 %collective-permute-start = (bf16[128,2176]{1,0:T(8,128)(2,1)S(1)}, bf16[128,2176]{1,0:T(8,128)(2,1)S(1)}, u32[]{:S(2)}, u32[]{:S(2)}) collective-permute-start(bf16[128,2176]{1,0:T(8,128)(2,1)S(1)} %get-tuple-element.71), channel_id=1, source_target_pairs={{0,4},{1,5},{2,6},{3,7},{4,0},{5,1},{6,2},{7,3},{8,12},{9,13},{10,... | collective-permute-start | bytes 1671176 | tf_op jit(solution)/shard_map/ppermute | solution.py:23
  10.8 21.2 %collective-permute-done.refs_0_.refs_1_ = bf16[128,2176]{1,0:T(8,128)(2,1)S(1)} collective-permute-done((bf16[128,2176]{1,0:T(8,128)(2,1)S(1)}, bf16[128,2176]{1,0:T(8,128)(2,1)S(1)}, u32[]{:S(2)}, u32[]{:S(2)}) %collective-permute-start) | collective-permute-done | bytes 557088 | tf_op jit(solution)/shard_map/ppermute | solution.py:23
  32.0 9.6 %collective-permute-done.3.refs_1_ = bf16[48,4096]{1,0:T(8,128)(2,1)S(1)} collective-permute-done((bf16[48,4096]{1,0:T(8,128)(2,1)S(1)}, bf16[48,4096]{1,0:T(8,128)(2,1)S(1)}, u32[]{:S(2)}, u32[]{:S(2)}) %collective-permute-start.3) | collective-permute-done | bytes 393248 | tf_op jit(solution)/shard_map/ppermute | solution.py:23
  43.5 2.3 %collective-permute-start.11 = (bf16[48,2048]{1,0:T(8,128)(2,1)S(1)}, bf16[48,2048]{1,0:T(8,128)(2,1)S(1)}, u32[]{:S(2)}, u32[]{:S(2)}) collective-permute-start(bf16[48,2048]{1,0:T(8,128)(2,1)S(1)} %get-tuple-element.91), channel_id=1, source_target_pairs={{0,3},{1,2},{2,1},{3,0},{4,7},{5,6},{6,5},{7,4},{8,11},{9,10},{10,... | collective-permute-start | bytes 589832 | tf_op jit(solution)/shard_map/ppermute | solution.py:23
  46.4 9.1 %expert_both.1 = (bf16[48,4096]{1,0:T(8,128)(2,1)S(1)}, bf16[48,4096]{1,0:T(8,128)(2,1)}, bf16[48,4096]{1,0:T(8,128)(2,1)}, bf16[48,4096]{1,0:T(8,128)(2,1)S(1)}...) custom-call(bf16[48,4096]{1,0:T(8,128)(2,1)S(1)} %get-tuple-element.78.refs_0_, ...), custom_call_target="tpu_custom_call" | custom-call | flops 1 | bytes 1 | tf_op jit(solution)/shard_map/expert_both/pallas_call | solution.py:353
  63.9 5.4 %expert_forward.1 = (bf16[48,2048]{1,0:T(8,128)(2,1)S(1)}, bf16[48,2048]{1,0:T(8,128)(2,1)S(1)}, bf16[48,2048]{1,0:T(8,128)(2,1)S(1)}, bf16[48,2048]{1,0:T(8,128...) custom-call(bf16[48,2048]{1,0:T(8,128)(2,1)S(1)} %get-tuple-element., ...), custom_call_target="tpu_custom_call" | custom-call | flops 1875000064 | bytes 1 | tf_op jit(solution)/shard_map/expert_forward/pallas_call | solution.py:353
  69.5 3.0 %collective-permute-done.7.refs_1_.refs_5_ = bf16[48,2048]{1,0:T(8,128)(2,1)S(1)} collective-permute-done((bf16[48,2048]{1,0:T(8,128)(2,1)S(1)}, bf16[48,2048]{1,0:T(8,128)(2,1)S(1)}, u32[]{:S(2)}, u32[]{:S(2)}) %collective-permute-start.7) | collective-permute-done | bytes 196640 | tf_op jit(solution)/shard_map/ppermute | solution.py:23
  73.1 2.3 %collective-permute-start.15 = (bf16[48,2048]{1,0:T(8,128)(2,1)S(1)}, bf16[48,2048]{1,0:T(8,128)(2,1)S(1)}, u32[]{:S(2)}, u32[]{:S(2)}) collective-permute-start(bf16[48,2048]{1,0:T(8,128)(2,1)S(1)} %get-tuple-element.109), channel_id=1, source_target_pairs={{0,3},{1,2},{2,1},{3,0},{4,7},{5,6},{6,5},{7,4},{8,11},{9,10},{10,... | collective-permute-start | bytes 589832 | tf_op jit(solution)/shard_map/ppermute | solution.py:23
  79.6 2.5 %collective-permute-start.18 = (bf16[48,4096]{1,0:T(8,128)(2,1)S(1)}, bf16[48,4096]{1,0:T(8,128)(2,1)S(1)}, u32[]{:S(2)}, u32[]{:S(2)}) collective-permute-start(bf16[48,4096]{1,0:T(8,128)(2,1)S(1)} %get-tuple-element.116), channel_id=1, source_target_pairs={{0,3},{1,2},{2,1},{3,0},{4,7},{5,6},{6,5},{7,4},{8,11},{9,10},{10,... | collective-permute-start | bytes 1179656 | tf_op jit(solution)/shard_map/ppermute | solution.py:23
  82.2 6.5 %expert_backward.1 = (bf16[48,2048]{1,0:T(8,128)(2,1)S(1)}, bf16[48,2048]{1,0:T(8,128)(2,1)S(1)}, bf16[48,2048]{1,0:T(8,128)(2,1)S(1)}, bf16[48,2048]{1,0:T(8,12...) custom-call(bf16[48,2048]{1,0:T(8,128)(2,1)S(1)} %get-tuple-element.100.refs_0_.refs_4_, ...), custom_call_target="tpu_custom_call" | custom-call | flops 3750000128 | bytes 1 | tf_op jit(solution)/shard_map/expert_backward/pallas_call | solution.py:353
  89.7 2.7 %sum_slots.3 = bf16[128,2176]{1,0:T(8,128)(2,1)} custom-call(bf16[128,2176]{1,0:T(8,128)(2,1)S(1)} %copy-done.10, bf16[128,2048]{1,0:T(8,128)(2,1)} %collective-permute-done.4.refs_1_, bf16[48,2048]{1,0:T(8,128)(2,1)S(1)} %get-tuple-element.108.refs_2_, bf16[48,2048]{1,0:T(8,128)(2,1)S(1)} %collective-permute-done.15.refs_3_, ...), custom_call_target="tpu_custom_call" | custom-call | flops 2250000128 | bytes 1 | tf_op jit(solution)/shard_map/sum_slots/pallas_call | solution.py:255
  92.4 2.1 %collective-permute-done.18.refs_5_ = bf16[48,4096]{1,0:T(8,128)(2,1)S(1)} collective-permute-done((bf16[48,4096]{1,0:T(8,128)(2,1)S(1)}, bf16[48,4096]{1,0:T(8,128)(2,1)S(1)}, u32[]{:S(2)}, u32[]{:S(2)}) %collective-permute-start.18) | collective-permute-done | bytes 393248 | tf_op jit(solution)/shard_map/ppermute | solution.py:23
  95.3 3.1 %collective-permute-start.25 = (bf16[128,2176]{1,0:T(8,128)(2,1)}, bf16[128,2176]{1,0:T(8,128)(2,1)}, u32[]{:S(2)}, u32[]{:S(2)}) collective-permute-start(bf16[128,2176]{1,0:T(8,128)(2,1)} %sum_slots.3), channel_id=1, source_target_pairs={{0,4},{1,5},{2,6},{3,7},{4,0},{5,1},{6,2},{7,3},{8,12},{9,13},{10,... | collective-permute-start | bytes 1671176 | tf_op jit(solution)/shard_map/ppermute | solution.py:23
  98.3 1.7 %collective-permute-start.23 = (bf16[48,2048]{1,0:T(8,128)(2,1)S(1)}, bf16[48,2048]{1,0:T(8,128)(2,1)S(1)}, u32[]{:S(2)}, u32[]{:S(2)}) collective-permute-start(bf16[48,2048]{1,0:T(8,128)(2,1)S(1)} %get-tuple-element.122), channel_id=1, source_target_pairs={{0,2},{1,3},{2,0},{3,1},{4,6},{5,7},{6,4},{7,5},{8,10},{9,11},{10,... | collective-permute-start | bytes 589832 | tf_op jit(solution)/shard_map/ppermute | solution.py:23
  101.6 3.2 %weight_sums.5 = bf16[512,1536]{1,0:T(8,128)(2,1)} custom-call(s32[2]{0:T(128)S(1)} %get-tuple-element.125.ids_ref, bf16[48,4096]{1,0:T(8,128)(2,1)S(1)} %get-tuple-element.78.refs_0_, bf16[48,4096]{1,0:T(8,128)(2,1)S(1)} %copy-done.8, bf16[48,4096]{1,0:T(8,128)(2,1)S(1)} %copy-done.6, bf16[48,4096]{1,0:T(8,128)(2,1)S(1)} %collective-permute-done.1.refs_3_, ...), custom_call_target="tpu_custom_call" | custom-call | flops 2250000128 | bytes 1 | tf_op jit(solution)/shard_map/weight_sums/pallas_call | solution.py:468
  106.3 7.7 %collective-permute-done.23.refs_4_ = bf16[48,2048]{1,0:T(8,128)(2,1)S(1)} collective-permute-done((bf16[48,2048]{1,0:T(8,128)(2,1)S(1)}, bf16[48,2048]{1,0:T(8,128)(2,1)S(1)}, u32[]{:S(2)}, u32[]{:S(2)}) %collective-permute-start.23) | collective-permute-done | bytes 196640 | tf_op jit(solution)/shard_map/ppermute | solution.py:23
  114.0 2.4 %sum_slots.4 = bf16[128,2048]{1,0:T(8,128)(2,1)} custom-call(bf16[128,2176]{1,0:T(8,128)(2,1)S(1)} %copy-done.10, bf16[128,2048]{1,0:T(8,128)(2,1)} %collective-permute-done.4.refs_1_, bf16[48,2048]{1,0:T(8,128)(2,1)S(1)} %get-tuple-element.120.refs_2_, bf16[48,2048]{1,0:T(8,128)(2,1)S(1)} %collective-permute-done.22.refs_3_, ...), custom_call_target="tpu_custom_call" | custom-call | flops 13500000256 | bytes 1 | tf_op jit(solution)/shard_map/sum_slots/pallas_call | solution.py:255
  116.4 3.4 %collective-permute-start.29 = (bf16[128,2048]{1,0:T(8,128)(2,1)}, bf16[128,2048]{1,0:T(8,128)(2,1)}, u32[]{:S(2)}, u32[]{:S(2)}) collective-permute-start(bf16[128,2048]{1,0:T(8,128)(2,1)} %sum_slots.4), channel_id=1, source_target_pairs={{0,4},{1,5},{2,6},{3,7},{4,0},{5,1},{6,2},{7,3},{8,12},{9,13},{10,... | collective-permute-start | bytes 1572872 | tf_op jit(solution)/shard_map/ppermute | solution.py:23
  120.5 2.9 %weight_sums.6.refs_0_ = f32[512,768]{1,0:T(8,128)S(1)} custom-call(s32[2]{0:T(128)S(1)} %get-tuple-element.125.ids_ref, bf16[48,4096]{1,0:T(8,128)(2,1)} %copy-done.3, bf16[48,4096]{1,0:T(8,128)(2,1)} %copy-done.7, bf16[48,4096]{1,0:T(8,128)(2,1)} %copy-done.5, bf16[48,4096]{1,0:T(8,128)(2,1)} %copy-done.4, bf16[48,2048]{1,0:T(8,128)(2,1)} %copy-done.31, ...), custom_call_target="tpu_custom_call" | custom-call | flops 2624999936 | bytes 1 | tf_op jit(solution)/shard_map/weight_sums/pallas_call | solution.py:468
  126.3 9.1 %collective-permute-done.25.refs_8_ = bf16[128,2176]{1,0:T(8,128)(2,1)} collective-permute-done((bf16[128,2176]{1,0:T(8,128)(2,1)}, bf16[128,2176]{1,0:T(8,128)(2,1)}, u32[]{:S(2)}, u32[]{:S(2)}) %collective-permute-start.25) | collective-permute-done | bytes 557088 | tf_op jit(solution)/shard_map/ppermute | solution.py:23
  135.3 3.9 %weight_sums.7.refs_0_.refs_1_ = f32[512,1536]{1,0:T(8,128)S(1)} custom-call(s32[2]{0:T(128)S(1)} %get-tuple-element.125.ids_ref, bf16[48,4096]{1,0:T(8,128)(2,1)} %copy-done.3, bf16[48,4096]{1,0:T(8,128)(2,1)} %copy-done.7, bf16[48,4096]{1,0:T(8,128)(2,1)} %copy-done.5, bf16[48,4096]{1,0:T(8,128)(2,1)} %copy-done.4, bf16[48,2048]{1,0:T(8,128)(2,1)} %copy-done.13, ...), custom_call_target="tpu_custom_call" | custom-call | flops 1500000000 | bytes 1 | tf_op jit(solution)/shard_map/weight_sums/pallas_call | solution.py:468
  141.3 2.9 %sum_slots.5 = (bf16[128,2048]{1,0:T(8,128)(2,1)}, f32[2,128]{1,0:T(2,128)}, f32[128,2048]{1,0:T(8,128)S(1)}) custom-call(s32[2,128]{1,0:T(2,128)S(1)} %bitcast.9, f32[2,128]{1,0:T(2,128)S(1)} %bitcast.7, f32[128,2]{1,0:T(8,128)S(1)} %copy-done.30, bf16[128,2048]{1,0:T(8,128)(2,1)S(1)} %copy-done.12, bf16[48,4096]{1,0:T(8,128)(2,1)S(1)} %copy-done.25, ...), custom_call_target="tpu_custom_call" | custom-call | flops 1 | bytes 1 | tf_op jit(solution)/shard_map/sum_slots/pallas_call | solution.py:255
  145.0 1.8 %add_halves.1 = bf16[128,2048]{1,0:T(8,128)(2,1)} custom-call(f32[128,2048]{1,0:T(8,128)S(1)} %get-tuple-element.133.a_ref, bf16[128,2048]{1,0:T(8,128)(2,1)} %collective-permute-done.29.b_ref), custom_call_target="tpu_custom_call" | custom-call | flops 1 | bytes 1 | tf_op jit(solution)/shard_map/add_halves/pallas_call | solution.py:490
  (130 shorter events, 30.3 us)
Async XLA Ops:
  3.3 28.7 %collective-permute-start = (bf16[128,2176]{1,0:T(8,128)(2,1)S(1)}, bf16[128,2176]{1,0:T(8,128)(2,1)S(1)}, u32[]{:S(2)}, u32[]{:S(2)}) collective-permute-start(bf16[128,2176]{1,0:T(8,128)(2,1)S(1)} %get-tuple-element.71), channel_id=1, source_target_pairs={{0,4},{1,5},{2,6},{3,7},{4,0},{5,1},{6,2},{7,3},{8,12},{9,13},{10,... | collective-permute-start | bytes 1671176 | tf_op jit(solution)/shard_map/ppermute | solution.py:23
  7.3 24.7 %collective-permute-start.1 = (bf16[48,4096]{1,0:T(8,128)(2,1)}, bf16[48,4096]{1,0:T(8,128)(2,1)S(1)}, u32[]{:S(2)}, u32[]{:S(2)}) collective-permute-start(bf16[48,4096]{1,0:T(8,128)(2,1)} %get-tuple-element.73), channel_id=1, source_target_pairs={{0,1},{1,0},{2,3},{3,2},{4,5},{5,4},{6,7},{7,6},{8,9},{9,8},{10,11... | collective-permute-start | bytes 1179656 | tf_op jit(solution)/shard_map/ppermute | solution.py:23
  8.8 23.2 %collective-permute-start.2 = (bf16[48,4096]{1,0:T(8,128)(2,1)S(1)}, bf16[48,4096]{1,0:T(8,128)(2,1)S(1)}, u32[]{:S(2)}, u32[]{:S(2)}) collective-permute-start(bf16[48,4096]{1,0:T(8,128)(2,1)S(1)} %get-tuple-element.74), channel_id=1, source_target_pairs={{0,2},{1,3},{2,0},{3,1},{4,6},{5,7},{6,4},{7,5},{8,10},{9,11},{10,... | collective-permute-start | bytes 1179656 | tf_op jit(solution)/shard_map/ppermute | solution.py:23
  10.4 31.2 %collective-permute-start.3 = (bf16[48,4096]{1,0:T(8,128)(2,1)S(1)}, bf16[48,4096]{1,0:T(8,128)(2,1)S(1)}, u32[]{:S(2)}, u32[]{:S(2)}) collective-permute-start(bf16[48,4096]{1,0:T(8,128)(2,1)S(1)} %get-tuple-element.75), channel_id=1, source_target_pairs={{0,3},{1,2},{2,1},{3,0},{4,7},{5,6},{6,5},{7,4},{8,11},{9,10},{10,... | collective-permute-start | bytes 1179656 | tf_op jit(solution)/shard_map/ppermute | solution.py:23
  32.0 25.7 %collective-permute-start.4 = (bf16[128,2048]{1,0:T(8,128)(2,1)}, bf16[128,2048]{1,0:T(8,128)(2,1)}, u32[]{:S(2)}, u32[]{:S(2)}) collective-permute-start(bf16[128,2048]{1,0:T(8,128)(2,1)} %refs_3_.3), channel_id=1, source_target_pairs={{0,4},{1,5},{2,6},{3,7},{4,0},{5,1},{6,2},{7,3},{8,12},{9,13},{10,... | collective-permute-start | bytes 1572872 | tf_op jit(solution)/shard_map/ppermute | solution.py:23
  42.2 18.4 %collective-permute-start.9 = (bf16[48,2048]{1,0:T(8,128)(2,1)S(1)}, bf16[48,2048]{1,0:T(8,128)(2,1)S(1)}, u32[]{:S(2)}, u32[]{:S(2)}) collective-permute-start(bf16[48,2048]{1,0:T(8,128)(2,1)S(1)} %get-tuple-element.89), channel_id=1, source_target_pairs={{0,1},{1,0},{2,3},{3,2},{4,5},{5,4},{6,7},{7,6},{8,9},{9,8},{10,11... | collective-permute-start | bytes 589832 | tf_op jit(solution)/shard_map/ppermute | solution.py:23
  43.5 17.6 %collective-permute-start.10 = (bf16[48,2048]{1,0:T(8,128)(2,1)S(1)}, bf16[48,2048]{1,0:T(8,128)(2,1)S(1)}, u32[]{:S(2)}, u32[]{:S(2)}) collective-permute-start(bf16[48,2048]{1,0:T(8,128)(2,1)S(1)} %get-tuple-element.90), channel_id=1, source_target_pairs={{0,2},{1,3},{2,0},{3,1},{4,6},{5,7},{6,4},{7,5},{8,10},{9,11},{10,... | collective-permute-start | bytes 589832 | tf_op jit(solution)/shard_map/ppermute | solution.py:23
  43.5 17.6 %collective-permute-start.11 = (bf16[48,2048]{1,0:T(8,128)(2,1)S(1)}, bf16[48,2048]{1,0:T(8,128)(2,1)S(1)}, u32[]{:S(2)}, u32[]{:S(2)}) collective-permute-start(bf16[48,2048]{1,0:T(8,128)(2,1)S(1)} %get-tuple-element.91), channel_id=1, source_target_pairs={{0,3},{1,2},{2,1},{3,0},{4,7},{5,6},{6,5},{7,4},{8,11},{9,10},{10,... | collective-permute-start | bytes 589832 | tf_op jit(solution)/shard_map/ppermute | solution.py:23
  60.6 16.2 %collective-permute-start.13 = (bf16[192,2304]{1,0:T(8,128)(2,1)S(1)}, bf16[192,2304]{1,0:T(8,128)(2,1)S(1)}, u32[]{:S(2)}, u32[]{:S(2)}) collective-permute-start(bf16[192,2304]{1,0:T(8,128)(2,1)S(1)} %get-tuple-element.98.refs_10_.refs_14_), channel_id=1, source_target_pairs={{0,8},{8,0},{16,24},{24,16},{1,9},{9,1},{17,25},{25,17},{2,10},{10... | collective-permute-start | bytes 2654216 | tf_op jit(solution)/shard_map/ppermute | solution.py:23
  60.6 15.4 %collective-permute-start.8 = (bf16[192,2048]{1,0:T(8,128)(2,1)S(1)}, bf16[192,2048]{1,0:T(8,128)(2,1)S(1)}, u32[]{:S(2)}, u32[]{:S(2)}) collective-permute-start(bf16[192,2048]{1,0:T(8,128)(2,1)S(1)} %get-tuple-element.82), channel_id=1, source_target_pairs={{0,8},{8,0},{16,24},{24,16},{1,9},{9,1},{17,25},{25,17},{2,10},{10... | collective-permute-start | bytes 2359304 | tf_op jit(solution)/shard_map/ppermute | solution.py:23
  73.1 15.5 %collective-permute-start.15 = (bf16[48,2048]{1,0:T(8,128)(2,1)S(1)}, bf16[48,2048]{1,0:T(8,128)(2,1)S(1)}, u32[]{:S(2)}, u32[]{:S(2)}) collective-permute-start(bf16[48,2048]{1,0:T(8,128)(2,1)S(1)} %get-tuple-element.109), channel_id=1, source_target_pairs={{0,3},{1,2},{2,1},{3,0},{4,7},{5,6},{6,5},{7,4},{8,11},{9,10},{10,... | collective-permute-start | bytes 589832 | tf_op jit(solution)/shard_map/ppermute | solution.py:23
  75.5 13.3 %collective-permute-start.16 = (bf16[48,2048]{1,0:T(8,128)(2,1)S(1)}, bf16[48,2048]{1,0:T(8,128)(2,1)S(1)}, u32[]{:S(2)}, u32[]{:S(2)}) collective-permute-start(bf16[48,2048]{1,0:T(8,128)(2,1)S(1)} %get-tuple-element.110), channel_id=1, source_target_pairs={{0,2},{1,3},{2,0},{3,1},{4,6},{5,7},{6,4},{7,5},{8,10},{9,11},{10,... | collective-permute-start | bytes 589832 | tf_op jit(solution)/shard_map/ppermute | solution.py:23
  76.0 13.3 %collective-permute-start.17 = (bf16[48,2048]{1,0:T(8,128)(2,1)S(1)}, bf16[48,2048]{1,0:T(8,128)(2,1)S(1)}, u32[]{:S(2)}, u32[]{:S(2)}) collective-permute-start(bf16[48,2048]{1,0:T(8,128)(2,1)S(1)} %get-tuple-element.111), channel_id=1, source_target_pairs={{0,1},{1,0},{2,3},{3,2},{4,5},{5,4},{6,7},{7,6},{8,9},{9,8},{10,11... | collective-permute-start | bytes 589832 | tf_op jit(solution)/shard_map/ppermute | solution.py:23
  78.3 26.4 %collective-permute-start.21 = (bf16[512,768]{1,0:T(8,128)(2,1)S(1)}, bf16[512,768]{1,0:T(8,128)(2,1)S(1)}, u32[]{:S(2)}, u32[]{:S(2)}) collective-permute-start(bf16[512,768]{1,0:T(8,128)(2,1)S(1)} %weight_sums.4), channel_id=1, source_target_pairs={{0,16},{8,24},{16,0},{24,8},{1,17},{9,25},{17,1},{25,9},{2,18},{10... | collective-permute-start | bytes 2359304 | tf_op jit(solution)/shard_map/ppermute | solution.py:23
  79.6 14.8 %collective-permute-start.18 = (bf16[48,4096]{1,0:T(8,128)(2,1)S(1)}, bf16[48,4096]{1,0:T(8,128)(2,1)S(1)}, u32[]{:S(2)}, u32[]{:S(2)}) collective-permute-start(bf16[48,4096]{1,0:T(8,128)(2,1)S(1)} %get-tuple-element.116), channel_id=1, source_target_pairs={{0,3},{1,2},{2,1},{3,0},{4,7},{5,6},{6,5},{7,4},{8,11},{9,10},{10,... | collective-permute-start | bytes 1179656 | tf_op jit(solution)/shard_map/ppermute | solution.py:23
  88.8 11.3 %collective-permute-start.19 = (bf16[192,768]{1,0:T(8,128)(2,1)S(1)}, bf16[192,768]{1,0:T(8,128)(2,1)S(1)}, u32[]{:S(2)}, u32[]{:S(2)}) collective-permute-start(bf16[192,768]{1,0:T(8,128)(2,1)S(1)} %get-tuple-element.106.refs_11_), channel_id=1, source_target_pairs={{0,8},{8,0},{16,24},{24,16},{1,9},{9,1},{17,25},{25,17},{2,10},{10... | collective-permute-start | bytes 884744 | tf_op jit(solution)/shard_map/ppermute | solution.py:23
  89.3 17.1 %collective-permute-start.22 = (bf16[48,2048]{1,0:T(8,128)(2,1)S(1)}, bf16[48,2048]{1,0:T(8,128)(2,1)S(1)}, u32[]{:S(2)}, u32[]{:S(2)}) collective-permute-start(bf16[48,2048]{1,0:T(8,128)(2,1)S(1)} %get-tuple-element.121), channel_id=1, source_target_pairs={{0,3},{1,2},{2,1},{3,0},{4,7},{5,6},{6,5},{7,4},{8,11},{9,10},{10,... | collective-permute-start | bytes 589832 | tf_op jit(solution)/shard_map/ppermute | solution.py:23
  95.3 40.1 %collective-permute-start.25 = (bf16[128,2176]{1,0:T(8,128)(2,1)}, bf16[128,2176]{1,0:T(8,128)(2,1)}, u32[]{:S(2)}, u32[]{:S(2)}) collective-permute-start(bf16[128,2176]{1,0:T(8,128)(2,1)} %sum_slots.3), channel_id=1, source_target_pairs={{0,4},{1,5},{2,6},{3,7},{4,0},{5,1},{6,2},{7,3},{8,12},{9,13},{10,... | collective-permute-start | bytes 1671176 | tf_op jit(solution)/shard_map/ppermute | solution.py:23
  98.3 15.7 %collective-permute-start.23 = (bf16[48,2048]{1,0:T(8,128)(2,1)S(1)}, bf16[48,2048]{1,0:T(8,128)(2,1)S(1)}, u32[]{:S(2)}, u32[]{:S(2)}) collective-permute-start(bf16[48,2048]{1,0:T(8,128)(2,1)S(1)} %get-tuple-element.122), channel_id=1, source_target_pairs={{0,2},{1,3},{2,0},{3,1},{4,6},{5,7},{6,4},{7,5},{8,10},{9,11},{10,... | collective-permute-start | bytes 589832 | tf_op jit(solution)/shard_map/ppermute | solution.py:23
  100.1 14.0 %collective-permute-start.24 = (bf16[48,2048]{1,0:T(8,128)(2,1)S(1)}, bf16[48,2048]{1,0:T(8,128)(2,1)S(1)}, u32[]{:S(2)}, u32[]{:S(2)}) collective-permute-start(bf16[48,2048]{1,0:T(8,128)(2,1)S(1)} %get-tuple-element.123), channel_id=1, source_target_pairs={{0,1},{1,0},{2,3},{3,2},{4,5},{5,4},{6,7},{7,6},{8,9},{9,8},{10,11... | collective-permute-start | bytes 589832 | tf_op jit(solution)/shard_map/ppermute | solution.py:23
  104.7 35.0 %collective-permute-start.26 = (bf16[512,1536]{1,0:T(8,128)(2,1)}, bf16[512,1536]{1,0:T(8,128)(2,1)S(1)}, u32[]{:S(2)}, u32[]{:S(2)}) collective-permute-start(bf16[512,1536]{1,0:T(8,128)(2,1)} %weight_sums.5), channel_id=1, source_target_pairs={{0,16},{8,24},{16,0},{24,8},{1,17},{9,25},{17,1},{25,9},{2,18},{10... | collective-permute-start | bytes 4718600 | tf_op jit(solution)/shard_map/ppermute | solution.py:23
  116.4 28.6 %collective-permute-start.29 = (bf16[128,2048]{1,0:T(8,128)(2,1)}, bf16[128,2048]{1,0:T(8,128)(2,1)}, u32[]{:S(2)}, u32[]{:S(2)}) collective-permute-start(bf16[128,2048]{1,0:T(8,128)(2,1)} %sum_slots.4), channel_id=1, source_target_pairs={{0,4},{1,5},{2,6},{3,7},{4,0},{5,1},{6,2},{7,3},{8,12},{9,13},{10,... | collective-permute-start | bytes 1572872 | tf_op jit(solution)/shard_map/ppermute | solution.py:23
  119.9 21.4 %collective-permute-start.27 = (bf16[48,4096]{1,0:T(8,128)(2,1)}, bf16[48,4096]{1,0:T(8,128)(2,1)S(1)}, u32[]{:S(2)}, u32[]{:S(2)}) collective-permute-start(bf16[48,4096]{1,0:T(8,128)(2,1)} %get-tuple-element.130), channel_id=1, source_target_pairs={{0,2},{1,3},{2,0},{3,1},{4,6},{5,7},{6,4},{7,5},{8,10},{9,11},{10,... | collective-permute-start | bytes 1179656 | tf_op jit(solution)/shard_map/ppermute | solution.py:23
  119.9 21.4 %collective-permute-start.28 = (bf16[48,4096]{1,0:T(8,128)(2,1)}, bf16[48,4096]{1,0:T(8,128)(2,1)}, u32[]{:S(2)}, u32[]{:S(2)}) collective-permute-start(bf16[48,4096]{1,0:T(8,128)(2,1)} %get-tuple-element.131), channel_id=1, source_target_pairs={{0,1},{1,0},{2,3},{3,2},{4,5},{5,4},{6,7},{7,6},{8,9},{9,8},{10,11... | collective-permute-start | bytes 1179656 | tf_op jit(solution)/shard_map/ppermute | solution.py:23
  (43 other events, 740.9 us)

commit v5 on v4

--- a/solution.py
+++ b/solution.py
@@ -361,7 +361,7 @@
         compiler_params=params(),
         cost_estimate=cost(weight),
         name=name,
-    )(*operands, *in_hbm(weights))
+    )(*operands, *(weights if name == "expert_backward" else in_hbm(weights)))
     return list(out[: form.count]), *out[form.count :]
 
 
@@ -568,7 +568,7 @@
     (down_on,) = weight_sums(form, ours, (0, on), c_left, down, share, ff)
     down_there = exchange(down_on, "ctx", 2)
     early = (form.half - 1,) if form.split else ()
-    back0_first = form.send(after(back0, down_on), early) if early else []
+    back0_first = form.send(after(back0, c1), early) if early else []
     gin1, gg1, gu1 = backward(form, after(c1, down_on), active1, slope1, *weights, weight=0.5)
     gin1_back = form.send(gin1)
     (far_mixed,) = back(form, after(far_meta, gg1), far_cot, out1_back, (0, None), weight=0.3)

time: 147 us -> 146 us (level)
    unnamed x75 -> x81, local copies, waits for them, and re-layouts: 3.52 us -> 3.53 us
where the time goes in v5:
time: 146 us; the launch traced here: 145 us
  waiting for transfers between devices  55.6 us (38%)
  Pallas kernels  48.9 us (33%)
  starting transfers between devices  35.2 us (24%)
  local copies, waits for them, and re-layouts  3.55 us (2%)
    ppermute x30, waiting for transfers between devices, exchange(): return lax.ppermute(x, axis, [(i, i ^ bit) for i in range(size)])  55.6 us
    ppermute x30, starting transfers between devices, exchange(): return lax.ppermute(x, axis, [(i, i ^ bit) for i in range(size)])  35.2 us
    pallas_call x3, Pallas kernels, expert_call(): pl.pallas_call(functools.partial(kernel, form.count), out_shape=out_shape...  19.7 us
    pallas_call x4, Pallas kernels, weight_sums(): pl.pallas_call(functools.partial(weight_kernel, [len(g[0]) for g in left]...  11.4 us
    pallas_call x3, Pallas kernels, back(): pl.pallas_call(functools.partial(back_kernel, form, offsets, combine is n...  8.03 us
    pallas_call x3, Pallas kernels, gather(): pl.pallas_call(functools.partial(gather_kernel, form, scaled, width, plai...  4.8 us
    unnamed x81, local copies, waits for them, and re-layouts  3.53 us
  transfers between devices with their start and end apart: 30, of which 9 were waited for; matrix products, arithmetic and copies ran while one was open for 1% of the time, Pallas kernels for 31%

profile of v5, /device:TPU:0, one launch (start us, length us, event | category | flops | bytes accessed | tf_op | source)
XLA Modules:
  0.0 145.0 jit_solution(14978675690829490714)
XLA Ops:
  0.6 2.7 %gather_slots.3 = (bf16[48,4096]{1,0:T(8,128)(2,1)S(1)}, bf16[48,4096]{1,0:T(8,128)(2,1)}, bf16[48,4096]{1,0:T(8,128)(2,1)S(1)}, bf16[48,4096]{1,0:T(8,128)(2,1)S(1)}, bf16[128,2176]{1,0:T(8,128)(2,1)S(1)}) custom-call(s32[2,128]{1,0:T(2,128)} %bitcast.8, f32[2,128]{1,0:T(2,128)} %bitcast.6, bf16[128,2048]{1,0:T(8,128)(2,1)} %refs_2_.2, ...), custom_call_target="tpu_custom_call" | custom-call | flops 1 | bytes 1 | tf_op jit(solution)/shard_map/gather_slots/pallas_call | solution.py:174
  3.3 4.0 %collective-permute-start = (bf16[128,2176]{1,0:T(8,128)(2,1)S(1)}, bf16[128,2176]{1,0:T(8,128)(2,1)S(1)}, u32[]{:S(2)}, u32[]{:S(2)}) collective-permute-start(bf16[128,2176]{1,0:T(8,128)(2,1)S(1)} %get-tuple-element.71), channel_id=1, source_target_pairs={{0,4},{1,5},{2,6},{3,7},{4,0},{5,1},{6,2},{7,3},{8,12},{9,13},{10,... | collective-permute-start | bytes 1671176 | tf_op jit(solution)/shard_map/ppermute | solution.py:23
  10.8 21.2 %collective-permute-done.refs_0_.refs_1_ = bf16[128,2176]{1,0:T(8,128)(2,1)S(1)} collective-permute-done((bf16[128,2176]{1,0:T(8,128)(2,1)S(1)}, bf16[128,2176]{1,0:T(8,128)(2,1)S(1)}, u32[]{:S(2)}, u32[]{:S(2)}) %collective-permute-start) | collective-permute-done | bytes 557088 | tf_op jit(solution)/shard_map/ppermute | solution.py:23
  32.0 9.6 %collective-permute-done.3.refs_1_ = bf16[48,4096]{1,0:T(8,128)(2,1)S(1)} collective-permute-done((bf16[48,4096]{1,0:T(8,128)(2,1)S(1)}, bf16[48,4096]{1,0:T(8,128)(2,1)S(1)}, u32[]{:S(2)}, u32[]{:S(2)}) %collective-permute-start.3) | collective-permute-done | bytes 393248 | tf_op jit(solution)/shard_map/ppermute | solution.py:23
  43.5 2.3 %collective-permute-start.11 = (bf16[48,2048]{1,0:T(8,128)(2,1)S(1)}, bf16[48,2048]{1,0:T(8,128)(2,1)S(1)}, u32[]{:S(2)}, u32[]{:S(2)}) collective-permute-start(bf16[48,2048]{1,0:T(8,128)(2,1)S(1)} %get-tuple-element.91), channel_id=1, source_target_pairs={{0,3},{1,2},{2,1},{3,0},{4,7},{5,6},{6,5},{7,4},{8,11},{9,10},{10,... | collective-permute-start | bytes 589832 | tf_op jit(solution)/shard_map/ppermute | solution.py:23
  46.4 9.1 %expert_both.1 = (bf16[48,4096]{1,0:T(8,128)(2,1)S(1)}, bf16[48,4096]{1,0:T(8,128)(2,1)}, bf16[48,4096]{1,0:T(8,128)(2,1)}, bf16[48,4096]{1,0:T(8,128)(2,1)S(1)}...) custom-call(bf16[48,4096]{1,0:T(8,128)(2,1)S(1)} %get-tuple-element.78.refs_0_, ...), custom_call_target="tpu_custom_call" | custom-call | flops 1 | bytes 1 | tf_op jit(solution)/shard_map/expert_both/pallas_call | solution.py:353
  63.9 5.4 %expert_forward.1 = (bf16[48,2048]{1,0:T(8,128)(2,1)S(1)}, bf16[48,2048]{1,0:T(8,128)(2,1)S(1)}, bf16[48,2048]{1,0:T(8,128)(2,1)S(1)}, bf16[48,2048]{1,0:T(8,128...) custom-call(bf16[48,2048]{1,0:T(8,128)(2,1)S(1)} %get-tuple-element., ...), custom_call_target="tpu_custom_call" | custom-call | flops 1875000064 | bytes 1 | tf_op jit(solution)/shard_map/expert_forward/pallas_call | solution.py:353
  69.5 3.0 %collective-permute-done.7.refs_1_.refs_5_ = bf16[48,2048]{1,0:T(8,128)(2,1)S(1)} collective-permute-done((bf16[48,2048]{1,0:T(8,128)(2,1)S(1)}, bf16[48,2048]{1,0:T(8,128)(2,1)S(1)}, u32[]{:S(2)}, u32[]{:S(2)}) %collective-permute-start.7) | collective-permute-done | bytes 196640 | tf_op jit(solution)/shard_map/ppermute | solution.py:23
  73.1 2.3 %collective-permute-start.15 = (bf16[48,2048]{1,0:T(8,128)(2,1)S(1)}, bf16[48,2048]{1,0:T(8,128)(2,1)S(1)}, u32[]{:S(2)}, u32[]{:S(2)}) collective-permute-start(bf16[48,2048]{1,0:T(8,128)(2,1)S(1)} %get-tuple-element.109), channel_id=1, source_target_pairs={{0,3},{1,2},{2,1},{3,0},{4,7},{5,6},{6,5},{7,4},{8,11},{9,10},{10,... | collective-permute-start | bytes 589832 | tf_op jit(solution)/shard_map/ppermute | solution.py:23
  76.8 2.2 %collective-permute-start.18 = (bf16[48,4096]{1,0:T(8,128)(2,1)S(1)}, bf16[48,4096]{1,0:T(8,128)(2,1)S(1)}, u32[]{:S(2)}, u32[]{:S(2)}) collective-permute-start(bf16[48,4096]{1,0:T(8,128)(2,1)S(1)} %get-tuple-element.116), channel_id=1, source_target_pairs={{0,3},{1,2},{2,1},{3,0},{4,7},{5,6},{6,5},{7,4},{8,11},{9,10},{10,... | collective-permute-start | bytes 1179656 | tf_op jit(solution)/shard_map/ppermute | solution.py:23
  82.2 5.2 %expert_backward.1 = (bf16[48,2048]{1,0:T(8,128)(2,1)S(1)}, bf16[48,2048]{1,0:T(8,128)(2,1)S(1)}, bf16[48,2048]{1,0:T(8,128)(2,1)S(1)}, bf16[48,2048]{1,0:T(8,12...) custom-call(bf16[48,2048]{1,0:T(8,128)(2,1)S(1)} %get-tuple-element.100.refs_0_.refs_4_, ...), custom_call_target="tpu_custom_call" | custom-call | flops 3750000128 | bytes 1 | tf_op jit(solution)/shard_map/expert_backward/pallas_call | solution.py:353
  88.0 2.7 %sum_slots.3 = bf16[128,2176]{1,0:T(8,128)(2,1)} custom-call(bf16[128,2176]{1,0:T(8,128)(2,1)S(1)} %copy-done.13, bf16[128,2048]{1,0:T(8,128)(2,1)} %collective-permute-done.4.refs_1_, bf16[48,2048]{1,0:T(8,128)(2,1)S(1)} %get-tuple-element.108.refs_2_, bf16[48,2048]{1,0:T(8,128)(2,1)S(1)} %collective-permute-done.15.refs_3_, ...), custom_call_target="tpu_custom_call" | custom-call | flops 2250000128 | bytes 1 | tf_op jit(solution)/shard_map/sum_slots/pallas_call | solution.py:255
  90.8 3.4 %collective-permute-start.25 = (bf16[128,2176]{1,0:T(8,128)(2,1)}, bf16[128,2176]{1,0:T(8,128)(2,1)}, u32[]{:S(2)}, u32[]{:S(2)}) collective-permute-start(bf16[128,2176]{1,0:T(8,128)(2,1)} %sum_slots.3), channel_id=1, source_target_pairs={{0,4},{1,5},{2,6},{3,7},{4,0},{5,1},{6,2},{7,3},{8,12},{9,13},{10,... | collective-permute-start | bytes 1671176 | tf_op jit(solution)/shard_map/ppermute | solution.py:23
  94.9 2.1 %collective-permute-start.22 = (bf16[48,2048]{1,0:T(8,128)(2,1)S(1)}, bf16[48,2048]{1,0:T(8,128)(2,1)S(1)}, u32[]{:S(2)}, u32[]{:S(2)}) collective-permute-start(bf16[48,2048]{1,0:T(8,128)(2,1)S(1)} %get-tuple-element.121), channel_id=1, source_target_pairs={{0,3},{1,2},{2,1},{3,0},{4,7},{5,6},{6,5},{7,4},{8,11},{9,10},{10,... | collective-permute-start | bytes 589832 | tf_op jit(solution)/shard_map/ppermute | solution.py:23
  98.5 3.1 %weight_sums.5 = bf16[512,1536]{1,0:T(8,128)(2,1)} custom-call(s32[2]{0:T(128)S(1)} %get-tuple-element.125.ids_ref, bf16[48,4096]{1,0:T(8,128)(2,1)S(1)} %get-tuple-element.78.refs_0_, bf16[48,4096]{1,0:T(8,128)(2,1)S(1)} %copy-done.11, bf16[48,4096]{1,0:T(8,128)(2,1)S(1)} %copy-done.9, bf16[48,4096]{1,0:T(8,128)(2,1)S(1)} %collective-permute-done.1.refs_3_, ...), custom_call_target="tpu_custom_call" | custom-call | flops 2250000128 | bytes 1 | tf_op jit(solution)/shard_map/weight_sums/pallas_call | solution.py:468
  103.0 8.7 %collective-permute-done.22.refs_3_ = bf16[48,2048]{1,0:T(8,128)(2,1)S(1)} collective-permute-done((bf16[48,2048]{1,0:T(8,128)(2,1)S(1)}, bf16[48,2048]{1,0:T(8,128)(2,1)S(1)}, u32[]{:S(2)}, u32[]{:S(2)}) %collective-permute-start.22) | collective-permute-done | bytes 196640 | tf_op jit(solution)/shard_map/ppermute | solution.py:23
  111.6 3.3 %collective-permute-done.23.refs_4_ = bf16[48,2048]{1,0:T(8,128)(2,1)S(1)} collective-permute-done((bf16[48,2048]{1,0:T(8,128)(2,1)S(1)}, bf16[48,2048]{1,0:T(8,128)(2,1)S(1)}, u32[]{:S(2)}, u32[]{:S(2)}) %collective-permute-start.23) | collective-permute-done | bytes 196640 | tf_op jit(solution)/shard_map/ppermute | solution.py:23
  115.0 2.4 %sum_slots.4 = bf16[128,2048]{1,0:T(8,128)(2,1)} custom-call(bf16[128,2176]{1,0:T(8,128)(2,1)S(1)} %copy-done.13, bf16[128,2048]{1,0:T(8,128)(2,1)} %collective-permute-done.4.refs_1_, bf16[48,2048]{1,0:T(8,128)(2,1)S(1)} %get-tuple-element.120.refs_2_, bf16[48,2048]{1,0:T(8,128)(2,1)S(1)} %collective-permute-done.22.refs_3_, ...), custom_call_target="tpu_custom_call" | custom-call | flops 13500000256 | bytes 1 | tf_op jit(solution)/shard_map/sum_slots/pallas_call | solution.py:255
  117.4 2.5 %collective-permute-start.29 = (bf16[128,2048]{1,0:T(8,128)(2,1)}, bf16[128,2048]{1,0:T(8,128)(2,1)}, u32[]{:S(2)}, u32[]{:S(2)}) collective-permute-start(bf16[128,2048]{1,0:T(8,128)(2,1)} %sum_slots.4), channel_id=1, source_target_pairs={{0,4},{1,5},{2,6},{3,7},{4,0},{5,1},{6,2},{7,3},{8,12},{9,13},{10,... | collective-permute-start | bytes 1572872 | tf_op jit(solution)/shard_map/ppermute | solution.py:23
  120.6 2.9 %weight_sums.6.refs_0_ = f32[512,768]{1,0:T(8,128)S(1)} custom-call(s32[2]{0:T(128)S(1)} %get-tuple-element.125.ids_ref, bf16[48,4096]{1,0:T(8,128)(2,1)} %copy-done.6, bf16[48,4096]{1,0:T(8,128)(2,1)} %copy-done.10, bf16[48,4096]{1,0:T(8,128)(2,1)} %copy-done.8, bf16[48,4096]{1,0:T(8,128)(2,1)} %copy-done.7, bf16[48,2048]{1,0:T(8,128)(2,1)} %copy-done.34, ...), custom_call_target="tpu_custom_call" | custom-call | flops 2624999936 | bytes 1 | tf_op jit(solution)/shard_map/weight_sums/pallas_call | solution.py:468
  126.3 3.9 %weight_sums.7.refs_0_.refs_1_ = f32[512,1536]{1,0:T(8,128)S(1)} custom-call(s32[2]{0:T(128)S(1)} %get-tuple-element.125.ids_ref, bf16[48,4096]{1,0:T(8,128)(2,1)} %copy-done.6, bf16[48,4096]{1,0:T(8,128)(2,1)} %copy-done.10, bf16[48,4096]{1,0:T(8,128)(2,1)} %copy-done.8, bf16[48,4096]{1,0:T(8,128)(2,1)} %copy-done.7, bf16[48,2048]{1,0:T(8,128)(2,1)} %copy-done.16, ...), custom_call_target="tpu_custom_call" | custom-call | flops 1500000000 | bytes 1 | tf_op jit(solution)/shard_map/weight_sums/pallas_call | solution.py:468
  130.3 6.9 %collective-permute-done.26.refs_2_.refs_3_ = bf16[512,1536]{1,0:T(8,128)(2,1)S(1)} collective-permute-done((bf16[512,1536]{1,0:T(8,128)(2,1)}, bf16[512,1536]{1,0:T(8,128)(2,1)S(1)}, u32[]{:S(2)}, u32[]{:S(2)}) %collective-permute-start.26) | collective-permute-done | bytes 1572896 | tf_op jit(solution)/shard_map/ppermute | solution.py:23
  139.7 2.9 %sum_slots.5 = (bf16[128,2048]{1,0:T(8,128)(2,1)}, f32[2,128]{1,0:T(2,128)}, f32[128,2048]{1,0:T(8,128)S(1)}) custom-call(s32[2,128]{1,0:T(2,128)S(1)} %bitcast.9, f32[2,128]{1,0:T(2,128)S(1)} %bitcast.7, f32[128,2]{1,0:T(8,128)S(1)} %copy-done.33, bf16[128,2048]{1,0:T(8,128)(2,1)S(1)} %copy-done.15, bf16[48,4096]{1,0:T(8,128)(2,1)S(1)} %copy-done.28, ...), custom_call_target="tpu_custom_call" | custom-call | flops 1 | bytes 1 | tf_op jit(solution)/shard_map/sum_slots/pallas_call | solution.py:255
  143.2 1.8 %add_halves.1 = bf16[128,2048]{1,0:T(8,128)(2,1)} custom-call(f32[128,2048]{1,0:T(8,128)S(1)} %get-tuple-element.133.a_ref, bf16[128,2048]{1,0:T(8,128)(2,1)} %collective-permute-done.29.b_ref), custom_call_target="tpu_custom_call" | custom-call | flops 1 | bytes 1 | tf_op jit(solution)/shard_map/add_halves/pallas_call | solution.py:490
  (136 shorter events, 30.0 us)
Async XLA Ops:
  3.3 28.7 %collective-permute-start = (bf16[128,2176]{1,0:T(8,128)(2,1)S(1)}, bf16[128,2176]{1,0:T(8,128)(2,1)S(1)}, u32[]{:S(2)}, u32[]{:S(2)}) collective-permute-start(bf16[128,2176]{1,0:T(8,128)(2,1)S(1)} %get-tuple-element.71), channel_id=1, source_target_pairs={{0,4},{1,5},{2,6},{3,7},{4,0},{5,1},{6,2},{7,3},{8,12},{9,13},{10,... | collective-permute-start | bytes 1671176 | tf_op jit(solution)/shard_map/ppermute | solution.py:23
  7.3 24.7 %collective-permute-start.1 = (bf16[48,4096]{1,0:T(8,128)(2,1)}, bf16[48,4096]{1,0:T(8,128)(2,1)S(1)}, u32[]{:S(2)}, u32[]{:S(2)}) collective-permute-start(bf16[48,4096]{1,0:T(8,128)(2,1)} %get-tuple-element.73), channel_id=1, source_target_pairs={{0,1},{1,0},{2,3},{3,2},{4,5},{5,4},{6,7},{7,6},{8,9},{9,8},{10,11... | collective-permute-start | bytes 1179656 | tf_op jit(solution)/shard_map/ppermute | solution.py:23
  8.8 23.2 %collective-permute-start.2 = (bf16[48,4096]{1,0:T(8,128)(2,1)S(1)}, bf16[48,4096]{1,0:T(8,128)(2,1)S(1)}, u32[]{:S(2)}, u32[]{:S(2)}) collective-permute-start(bf16[48,4096]{1,0:T(8,128)(2,1)S(1)} %get-tuple-element.74), channel_id=1, source_target_pairs={{0,2},{1,3},{2,0},{3,1},{4,6},{5,7},{6,4},{7,5},{8,10},{9,11},{10,... | collective-permute-start | bytes 1179656 | tf_op jit(solution)/shard_map/ppermute | solution.py:23
  10.4 31.2 %collective-permute-start.3 = (bf16[48,4096]{1,0:T(8,128)(2,1)S(1)}, bf16[48,4096]{1,0:T(8,128)(2,1)S(1)}, u32[]{:S(2)}, u32[]{:S(2)}) collective-permute-start(bf16[48,4096]{1,0:T(8,128)(2,1)S(1)} %get-tuple-element.75), channel_id=1, source_target_pairs={{0,3},{1,2},{2,1},{3,0},{4,7},{5,6},{6,5},{7,4},{8,11},{9,10},{10,... | collective-permute-start | bytes 1179656 | tf_op jit(solution)/shard_map/ppermute | solution.py:23
  32.0 25.7 %collective-permute-start.4 = (bf16[128,2048]{1,0:T(8,128)(2,1)}, bf16[128,2048]{1,0:T(8,128)(2,1)}, u32[]{:S(2)}, u32[]{:S(2)}) collective-permute-start(bf16[128,2048]{1,0:T(8,128)(2,1)} %refs_3_.3), channel_id=1, source_target_pairs={{0,4},{1,5},{2,6},{3,7},{4,0},{5,1},{6,2},{7,3},{8,12},{9,13},{10,... | collective-permute-start | bytes 1572872 | tf_op jit(solution)/shard_map/ppermute | solution.py:23
  42.2 18.4 %collective-permute-start.9 = (bf16[48,2048]{1,0:T(8,128)(2,1)S(1)}, bf16[48,2048]{1,0:T(8,128)(2,1)S(1)}, u32[]{:S(2)}, u32[]{:S(2)}) collective-permute-start(bf16[48,2048]{1,0:T(8,128)(2,1)S(1)} %get-tuple-element.89), channel_id=1, source_target_pairs={{0,1},{1,0},{2,3},{3,2},{4,5},{5,4},{6,7},{7,6},{8,9},{9,8},{10,11... | collective-permute-start | bytes 589832 | tf_op jit(solution)/shard_map/ppermute | solution.py:23
  43.5 17.6 %collective-permute-start.10 = (bf16[48,2048]{1,0:T(8,128)(2,1)S(1)}, bf16[48,2048]{1,0:T(8,128)(2,1)S(1)}, u32[]{:S(2)}, u32[]{:S(2)}) collective-permute-start(bf16[48,2048]{1,0:T(8,128)(2,1)S(1)} %get-tuple-element.90), channel_id=1, source_target_pairs={{0,2},{1,3},{2,0},{3,1},{4,6},{5,7},{6,4},{7,5},{8,10},{9,11},{10,... | collective-permute-start | bytes 589832 | tf_op jit(solution)/shard_map/ppermute | solution.py:23
  43.5 17.6 %collective-permute-start.11 = (bf16[48,2048]{1,0:T(8,128)(2,1)S(1)}, bf16[48,2048]{1,0:T(8,128)(2,1)S(1)}, u32[]{:S(2)}, u32[]{:S(2)}) collective-permute-start(bf16[48,2048]{1,0:T(8,128)(2,1)S(1)} %get-tuple-element.91), channel_id=1, source_target_pairs={{0,3},{1,2},{2,1},{3,0},{4,7},{5,6},{6,5},{7,4},{8,11},{9,10},{10,... | collective-permute-start | bytes 589832 | tf_op jit(solution)/shard_map/ppermute | solution.py:23
  59.3 10.1 %collective-permute-start.5 = (bf16[48,2048]{1,0:T(8,128)(2,1)S(1)}, bf16[48,2048]{1,0:T(8,128)(2,1)S(1)}, u32[]{:S(2)}, u32[]{:S(2)}) collective-permute-start(bf16[48,2048]{1,0:T(8,128)(2,1)S(1)} %get-tuple-element.86), channel_id=1, source_target_pairs={{0,1},{1,0},{2,3},{3,2},{4,5},{5,4},{6,7},{7,6},{8,9},{9,8},{10,11... | collective-permute-start | bytes 589832 | tf_op jit(solution)/shard_map/ppermute | solution.py:23
  60.6 16.2 %collective-permute-start.13 = (bf16[192,2304]{1,0:T(8,128)(2,1)S(1)}, bf16[192,2304]{1,0:T(8,128)(2,1)S(1)}, u32[]{:S(2)}, u32[]{:S(2)}) collective-permute-start(bf16[192,2304]{1,0:T(8,128)(2,1)S(1)} %get-tuple-element.98.refs_10_.refs_14_), channel_id=1, source_target_pairs={{0,8},{8,0},{16,24},{24,16},{1,9},{9,1},{17,25},{25,17},{2,10},{10... | collective-permute-start | bytes 2654216 | tf_op jit(solution)/shard_map/ppermute | solution.py:23
  60.6 15.4 %collective-permute-start.8 = (bf16[192,2048]{1,0:T(8,128)(2,1)S(1)}, bf16[192,2048]{1,0:T(8,128)(2,1)S(1)}, u32[]{:S(2)}, u32[]{:S(2)}) collective-permute-start(bf16[192,2048]{1,0:T(8,128)(2,1)S(1)} %get-tuple-element.82), channel_id=1, source_target_pairs={{0,8},{8,0},{16,24},{24,16},{1,9},{9,1},{17,25},{25,17},{2,10},{10... | collective-permute-start | bytes 2359304 | tf_op jit(solution)/shard_map/ppermute | solution.py:23
  73.1 14.3 %collective-permute-start.15 = (bf16[48,2048]{1,0:T(8,128)(2,1)S(1)}, bf16[48,2048]{1,0:T(8,128)(2,1)S(1)}, u32[]{:S(2)}, u32[]{:S(2)}) collective-permute-start(bf16[48,2048]{1,0:T(8,128)(2,1)S(1)} %get-tuple-element.109), channel_id=1, source_target_pairs={{0,3},{1,2},{2,1},{3,0},{4,7},{5,6},{6,5},{7,4},{8,11},{9,10},{10,... | collective-permute-start | bytes 589832 | tf_op jit(solution)/shard_map/ppermute | solution.py:23
  75.5 12.1 %collective-permute-start.16 = (bf16[48,2048]{1,0:T(8,128)(2,1)S(1)}, bf16[48,2048]{1,0:T(8,128)(2,1)S(1)}, u32[]{:S(2)}, u32[]{:S(2)}) collective-permute-start(bf16[48,2048]{1,0:T(8,128)(2,1)S(1)} %get-tuple-element.110), channel_id=1, source_target_pairs={{0,2},{1,3},{2,0},{3,1},{4,6},{5,7},{6,4},{7,5},{8,10},{9,11},{10,... | collective-permute-start | bytes 589832 | tf_op jit(solution)/shard_map/ppermute | solution.py:23
  76.0 12.0 %collective-permute-start.17 = (bf16[48,2048]{1,0:T(8,128)(2,1)S(1)}, bf16[48,2048]{1,0:T(8,128)(2,1)S(1)}, u32[]{:S(2)}, u32[]{:S(2)}) collective-permute-start(bf16[48,2048]{1,0:T(8,128)(2,1)S(1)} %get-tuple-element.111), channel_id=1, source_target_pairs={{0,1},{1,0},{2,3},{3,2},{4,5},{5,4},{6,7},{7,6},{8,9},{9,8},{10,11... | collective-permute-start | bytes 589832 | tf_op jit(solution)/shard_map/ppermute | solution.py:23
  76.8 17.3 %collective-permute-start.18 = (bf16[48,4096]{1,0:T(8,128)(2,1)S(1)}, bf16[48,4096]{1,0:T(8,128)(2,1)S(1)}, u32[]{:S(2)}, u32[]{:S(2)}) collective-permute-start(bf16[48,4096]{1,0:T(8,128)(2,1)S(1)} %get-tuple-element.116), channel_id=1, source_target_pairs={{0,3},{1,2},{2,1},{3,0},{4,7},{5,6},{6,5},{7,4},{8,11},{9,10},{10,... | collective-permute-start | bytes 1179656 | tf_op jit(solution)/shard_map/ppermute | solution.py:23
  80.6 21.1 %collective-permute-start.21 = (bf16[512,768]{1,0:T(8,128)(2,1)S(1)}, bf16[512,768]{1,0:T(8,128)(2,1)S(1)}, u32[]{:S(2)}, u32[]{:S(2)}) collective-permute-start(bf16[512,768]{1,0:T(8,128)(2,1)S(1)} %weight_sums.4), channel_id=1, source_target_pairs={{0,16},{8,24},{16,0},{24,8},{1,17},{9,25},{17,1},{25,9},{2,18},{10... | collective-permute-start | bytes 2359304 | tf_op jit(solution)/shard_map/ppermute | solution.py:23
  90.8 35.6 %collective-permute-start.25 = (bf16[128,2176]{1,0:T(8,128)(2,1)}, bf16[128,2176]{1,0:T(8,128)(2,1)}, u32[]{:S(2)}, u32[]{:S(2)}) collective-permute-start(bf16[128,2176]{1,0:T(8,128)(2,1)} %sum_slots.3), channel_id=1, source_target_pairs={{0,4},{1,5},{2,6},{3,7},{4,0},{5,1},{6,2},{7,3},{8,12},{9,13},{10,... | collective-permute-start | bytes 1671176 | tf_op jit(solution)/shard_map/ppermute | solution.py:23
  94.9 16.7 %collective-permute-start.22 = (bf16[48,2048]{1,0:T(8,128)(2,1)S(1)}, bf16[48,2048]{1,0:T(8,128)(2,1)S(1)}, u32[]{:S(2)}, u32[]{:S(2)}) collective-permute-start(bf16[48,2048]{1,0:T(8,128)(2,1)S(1)} %get-tuple-element.121), channel_id=1, source_target_pairs={{0,3},{1,2},{2,1},{3,0},{4,7},{5,6},{6,5},{7,4},{8,11},{9,10},{10,... | collective-permute-start | bytes 589832 | tf_op jit(solution)/shard_map/ppermute | solution.py:23
  97.1 17.9 %collective-permute-start.23 = (bf16[48,2048]{1,0:T(8,128)(2,1)S(1)}, bf16[48,2048]{1,0:T(8,128)(2,1)S(1)}, u32[]{:S(2)}, u32[]{:S(2)}) collective-permute-start(bf16[48,2048]{1,0:T(8,128)(2,1)S(1)} %get-tuple-element.122), channel_id=1, source_target_pairs={{0,2},{1,3},{2,0},{3,1},{4,6},{5,7},{6,4},{7,5},{8,10},{9,11},{10,... | collective-permute-start | bytes 589832 | tf_op jit(solution)/shard_map/ppermute | solution.py:23
  97.5 17.4 %collective-permute-start.24 = (bf16[48,2048]{1,0:T(8,128)(2,1)S(1)}, bf16[48,2048]{1,0:T(8,128)(2,1)S(1)}, u32[]{:S(2)}, u32[]{:S(2)}) collective-permute-start(bf16[48,2048]{1,0:T(8,128)(2,1)S(1)} %get-tuple-element.123), channel_id=1, source_target_pairs={{0,1},{1,0},{2,3},{3,2},{4,5},{5,4},{6,7},{7,6},{8,9},{9,8},{10,11... | collective-permute-start | bytes 589832 | tf_op jit(solution)/shard_map/ppermute | solution.py:23
  101.7 35.5 %collective-permute-start.26 = (bf16[512,1536]{1,0:T(8,128)(2,1)}, bf16[512,1536]{1,0:T(8,128)(2,1)S(1)}, u32[]{:S(2)}, u32[]{:S(2)}) collective-permute-start(bf16[512,1536]{1,0:T(8,128)(2,1)} %weight_sums.5), channel_id=1, source_target_pairs={{0,16},{8,24},{16,0},{24,8},{1,17},{9,25},{17,1},{25,9},{2,18},{10... | collective-permute-start | bytes 4718600 | tf_op jit(solution)/shard_map/ppermute | solution.py:23
  117.4 25.8 %collective-permute-start.29 = (bf16[128,2048]{1,0:T(8,128)(2,1)}, bf16[128,2048]{1,0:T(8,128)(2,1)}, u32[]{:S(2)}, u32[]{:S(2)}) collective-permute-start(bf16[128,2048]{1,0:T(8,128)(2,1)} %sum_slots.4), channel_id=1, source_target_pairs={{0,4},{1,5},{2,6},{3,7},{4,0},{5,1},{6,2},{7,3},{8,12},{9,13},{10,... | collective-permute-start | bytes 1572872 | tf_op jit(solution)/shard_map/ppermute | solution.py:23
  119.9 19.8 %collective-permute-start.27 = (bf16[48,4096]{1,0:T(8,128)(2,1)}, bf16[48,4096]{1,0:T(8,128)(2,1)S(1)}, u32[]{:S(2)}, u32[]{:S(2)}) collective-permute-start(bf16[48,4096]{1,0:T(8,128)(2,1)} %get-tuple-element.130), channel_id=1, source_target_pairs={{0,2},{1,3},{2,0},{3,1},{4,6},{5,7},{6,4},{7,5},{8,10},{9,11},{10,... | collective-permute-start | bytes 1179656 | tf_op jit(solution)/shard_map/ppermute | solution.py:23
  119.9 19.7 %collective-permute-start.28 = (bf16[48,4096]{1,0:T(8,128)(2,1)}, bf16[48,4096]{1,0:T(8,128)(2,1)}, u32[]{:S(2)}, u32[]{:S(2)}) collective-permute-start(bf16[48,4096]{1,0:T(8,128)(2,1)} %get-tuple-element.131), channel_id=1, source_target_pairs={{0,1},{1,0},{2,3},{3,2},{4,5},{5,4},{6,7},{7,6},{8,9},{9,8},{10,11... | collective-permute-start | bytes 1179656 | tf_op jit(solution)/shard_map/ppermute | solution.py:23
  (46 other events, 769.7 us)

commit v6 on v5

--- a/solution.py
+++ b/solution.py
@@ -134,12 +134,27 @@
     return jnp.transpose(jnp.concatenate(rows, axis=0)).astype(bf16)
 
 
+def message_kernel(ids_ref, combine_ref, hits_ref, out_ref):
+    width = hits_ref.shape[1]
+    out_ref[:, :width] = hits_ref[...]
+    out_ref[:, width:] = pack_rows(plain_rows(ids_ref, combine_ref))
+
+
+def message_of(ids, combine, hits):
+    tokens, width = hits.shape
+    return pl.pallas_call(
+        message_kernel,
+        out_shape=result((tokens, width + 128), bf16),
+        in_specs=[VMEM] * 3,
+        out_specs=VMEM,
+        compiler_params=params(),
+        cost_estimate=cost(0),
+        name="message",
+    )(*in_hbm([ids, combine, hits]))
+
+
 def gather_kernel(form, scaled, width, plain, *refs):
     meta, refs = (plain_rows(*refs[:2]), refs[2:]) if plain else (packed_rows(refs[0]), refs[1:])
-    if plain:
-        message_ref, refs = refs[-1], refs[:-1]
-        message_ref[:, :width] = refs[0][...]
-        message_ref[:, width:] = pack_rows(meta)
     inputs, outs = refs[: len(scaled)], refs[len(scaled) :]
     first, second = slot_plan(meta, form)
     either = (first + second).astype(bf16)
@@ -169,8 +184,6 @@
     total = width * len(arrays)
     plain = len(meta) == 2
     out_shape = form.shapes(total)
-    if plain:
-        out_shape = out_shape + [result((tokens, width + 128), bf16)]
     out = pl.pallas_call(
         functools.partial(gather_kernel, form, scaled, width, plain),
         grid=(1,),
@@ -528,7 +541,8 @@
     capacity = 3 * tokens // experts
     form = Blocks(half, capacity)
     meta = (expert_ids.T, combine.T)
-    *own_send, message = gather(form, meta, [hits, cotangent], (False, True), width)
+    message = message_of(*meta, hits)
+    own_send = gather(form, after(meta, message), [hits, cotangent], (False, True), width)
     far_hits = exchange(message, "exp", half)
     far_cot = exchange(after(cotangent, far_hits), "exp", half)
     far_meta = (far_hits,)

time: 146 us -> 145 us (level)
  waiting for transfers between devices: 55.6 us -> 45.9 us
  starting transfers between devices: 35.2 us -> 42.7 us
  Pallas kernels: 48.9 us -> 50.4 us
    ppermute x30, waiting for transfers between devices: 55.6 us -> 45.9 us  [exchange(): return lax.ppermute(x, axis, [(i, i ^ bit) for i in range(size)])]
    ppermute x30, starting transfers between devices: 35.2 us -> 42.7 us  [exchange(): return lax.ppermute(x, axis, [(i, i ^ bit) for i in range(size)])]
    unnamed x81 -> x83, local copies, waits for them, and re-layouts: 3.53 us -> 3.54 us
  transfers between devices with their start and end apart: 30 -> 30, of which waited for: 9 -> 11; matrix products, arithmetic and copies ran while one was open for 1% -> 1% of each run, Pallas kernels for 31% -> 33%
where the time goes in v6:
time: 145 us; the launch traced here: 144 us
  Pallas kernels  50.4 us (35%)
  waiting for transfers between devices  45.9 us (32%)
  starting transfers between devices  42.7 us (29%)
  local copies, waits for them, and re-layouts  3.56 us (2%)
    ppermute x30, waiting for transfers between devices, exchange(): return lax.ppermute(x, axis, [(i, i ^ bit) for i in range(size)])  45.9 us
    ppermute x30, starting transfers between devices, exchange(): return lax.ppermute(x, axis, [(i, i ^ bit) for i in range(size)])  42.7 us
    pallas_call x3, Pallas kernels, expert_call(): pl.pallas_call(functools.partial(kernel, form.count), out_shape=out_shape...  19.8 us
    pallas_call x4, Pallas kernels, weight_sums(): pl.pallas_call(functools.partial(weight_kernel, [len(g[0]) for g in left]...  11.4 us
    pallas_call x3, Pallas kernels, back(): pl.pallas_call(functools.partial(back_kernel, form, offsets, combine is n...  8.02 us
    pallas_call x3, Pallas kernels, gather(): pl.pallas_call(functools.partial(gather_kernel, form, scaled, width, plai...  5.09 us
    unnamed x83, local copies, waits for them, and re-layouts  3.54 us
  transfers between devices with their start and end apart: 30, of which 11 were waited for; matrix products, arithmetic and copies ran while one was open for 1% of the time, Pallas kernels for 33%

profile of v6, /device:TPU:0, one launch (start us, length us, event | category | flops | bytes accessed | tf_op | source)
XLA Modules:
  0.0 143.7 jit_solution(16199573270693557724)
XLA Ops:
  1.9 4.1 %collective-permute-start = (bf16[128,2176]{1,0:T(8,128)(2,1)S(1)}, bf16[128,2176]{1,0:T(8,128)(2,1)S(1)}, u32[]{:S(2)}, u32[]{:S(2)}) collective-permute-start(bf16[128,2176]{1,0:T(8,128)(2,1)S(1)} %message.1), channel_id=1, source_target_pairs={{0,4},{1,5},{2,6},{3,7},{4,0},{5,1},{6,2},{7,3},{8,12},{9,13},{10,... | collective-permute-start | bytes 1671176 | tf_op jit(solution)/shard_map/ppermute | solution.py:23
  6.0 2.6 %gather_slots.3 = (bf16[48,4096]{1,0:T(8,128)(2,1)S(1)}, bf16[48,4096]{1,0:T(8,128)(2,1)}, bf16[48,4096]{1,0:T(8,128)(2,1)S(1)}, bf16[48,4096]{1,0:T(8,128)(2,1)S(1)}) custom-call(s32[2,128]{1,0:T(2,128)} %bitcast.10, f32[2,128]{1,0:T(2,128)} %bitcast.7, bf16[128,2048]{1,0:T(8,128)(2,1)} %refs_2_.2, bf16[128,2048]{1,0:T(8,128)(2,1)} %refs_3_.3), custom_call_target="tpu_custom_call" | custom-call | flops 1 | bytes 1 | tf_op jit(solution)/shard_map/gather_slots/pallas_call | solution.py:187
  12.1 18.5 %collective-permute-done.refs_0_.refs_1_ = bf16[128,2176]{1,0:T(8,128)(2,1)S(1)} collective-permute-done((bf16[128,2176]{1,0:T(8,128)(2,1)S(1)}, bf16[128,2176]{1,0:T(8,128)(2,1)S(1)}, u32[]{:S(2)}, u32[]{:S(2)}) %collective-permute-start) | collective-permute-done | bytes 557088 | tf_op jit(solution)/shard_map/ppermute | solution.py:23
  30.7 2.3 %collective-permute-done.2.refs_2_ = bf16[48,4096]{1,0:T(8,128)(2,1)S(1)} collective-permute-done((bf16[48,4096]{1,0:T(8,128)(2,1)S(1)}, bf16[48,4096]{1,0:T(8,128)(2,1)S(1)}, u32[]{:S(2)}, u32[]{:S(2)}) %collective-permute-start.2) | collective-permute-done | bytes 393248 | tf_op jit(solution)/shard_map/ppermute | solution.py:23
  32.9 10.0 %collective-permute-done.3.refs_1_ = bf16[48,4096]{1,0:T(8,128)(2,1)S(1)} collective-permute-done((bf16[48,4096]{1,0:T(8,128)(2,1)S(1)}, bf16[48,4096]{1,0:T(8,128)(2,1)S(1)}, u32[]{:S(2)}, u32[]{:S(2)}) %collective-permute-start.3) | collective-permute-done | bytes 393248 | tf_op jit(solution)/shard_map/ppermute | solution.py:23
  44.7 2.3 %collective-permute-start.11 = (bf16[48,2048]{1,0:T(8,128)(2,1)S(1)}, bf16[48,2048]{1,0:T(8,128)(2,1)S(1)}, u32[]{:S(2)}, u32[]{:S(2)}) collective-permute-start(bf16[48,2048]{1,0:T(8,128)(2,1)S(1)} %get-tuple-element.93), channel_id=1, source_target_pairs={{0,3},{1,2},{2,1},{3,0},{4,7},{5,6},{6,5},{7,4},{8,11},{9,10},{10,... | collective-permute-start | bytes 589832 | tf_op jit(solution)/shard_map/ppermute | solution.py:23
  47.0 9.1 %expert_both.1 = (bf16[48,4096]{1,0:T(8,128)(2,1)S(1)}, bf16[48,4096]{1,0:T(8,128)(2,1)}, bf16[48,4096]{1,0:T(8,128)(2,1)}, bf16[48,4096]{1,0:T(8,128)(2,1)S(1)}...) custom-call(bf16[48,4096]{1,0:T(8,128)(2,1)S(1)} %get-tuple-element.80.refs_0_, ...), custom_call_target="tpu_custom_call" | custom-call | flops 1 | bytes 1 | tf_op jit(solution)/shard_map/expert_both/pallas_call | solution.py:366
  56.9 1.9 %gather_slots.5 = (bf16[48,2048]{1,0:T(8,128)(2,1)S(1)}, bf16[48,2048]{1,0:T(8,128)(2,1)S(1)}, bf16[48,2048]{1,0:T(8,128)(2,1)S(1)}, bf16[48,2048]{1,0:T(8,128)(2,1)S(1)}) custom-call(bf16[128,2176]{1,0:T(8,128)(2,1)S(1)} %collective-permute-done.refs_0_.refs_1_, bf16[128,2048]{1,0:T(8,128)(2,1)} %collective-permute-done.4.refs_1_), custom_call_target="tpu_custom_call" | custom-call | flops 1 | bytes 1 | tf_op jit(solution)/shard_map/gather_slots/pallas_call | solution.py:187
  62.2 2.9 %collective-permute-start.7 = (bf16[48,2048]{1,0:T(8,128)(2,1)S(1)}, bf16[48,2048]{1,0:T(8,128)(2,1)S(1)}, u32[]{:S(2)}, u32[]{:S(2)}) collective-permute-start(bf16[48,2048]{1,0:T(8,128)(2,1)S(1)} %get-tuple-element.90), channel_id=1, source_target_pairs={{0,3},{1,2},{2,1},{3,0},{4,7},{5,6},{6,5},{7,4},{8,11},{9,10},{10,... | collective-permute-start | bytes 589832 | tf_op jit(solution)/shard_map/ppermute | solution.py:23
  65.1 5.4 %expert_forward.1 = (bf16[48,2048]{1,0:T(8,128)(2,1)S(1)}, bf16[48,2048]{1,0:T(8,128)(2,1)S(1)}, bf16[48,2048]{1,0:T(8,128)(2,1)S(1)}, bf16[48,2048]{1,0:T(8,128...) custom-call(bf16[48,2048]{1,0:T(8,128)(2,1)S(1)} %get-tuple-element., ...), custom_call_target="tpu_custom_call" | custom-call | flops 1875000064 | bytes 1 | tf_op jit(solution)/shard_map/expert_forward/pallas_call | solution.py:366
  80.9 5.2 %expert_backward.1 = (bf16[48,2048]{1,0:T(8,128)(2,1)S(1)}, bf16[48,2048]{1,0:T(8,128)(2,1)S(1)}, bf16[48,2048]{1,0:T(8,128)(2,1)S(1)}, bf16[48,2048]{1,0:T(8,12...) custom-call(bf16[48,2048]{1,0:T(8,128)(2,1)S(1)} %get-tuple-element.102.refs_0_.refs_4_, ...), custom_call_target="tpu_custom_call" | custom-call | flops 3750000128 | bytes 1 | tf_op jit(solution)/shard_map/expert_backward/pallas_call | solution.py:366
  86.7 2.7 %sum_slots.3 = bf16[128,2176]{1,0:T(8,128)(2,1)} custom-call(bf16[128,2176]{1,0:T(8,128)(2,1)S(1)} %copy-done.13, bf16[128,2048]{1,0:T(8,128)(2,1)} %collective-permute-done.4.refs_1_, bf16[48,2048]{1,0:T(8,128)(2,1)S(1)} %get-tuple-element.110.refs_2_, bf16[48,2048]{1,0:T(8,128)(2,1)S(1)} %collective-permute-done.15.refs_3_, ...), custom_call_target="tpu_custom_call" | custom-call | flops 2250000128 | bytes 1 | tf_op jit(solution)/shard_map/sum_slots/pallas_call | solution.py:268
  89.4 3.4 %collective-permute-start.25 = (bf16[128,2176]{1,0:T(8,128)(2,1)}, bf16[128,2176]{1,0:T(8,128)(2,1)}, u32[]{:S(2)}, u32[]{:S(2)}) collective-permute-start(bf16[128,2176]{1,0:T(8,128)(2,1)} %sum_slots.3), channel_id=1, source_target_pairs={{0,4},{1,5},{2,6},{3,7},{4,0},{5,1},{6,2},{7,3},{8,12},{9,13},{10,... | collective-permute-start | bytes 1671176 | tf_op jit(solution)/shard_map/ppermute | solution.py:23
  98.0 3.1 %weight_sums.5 = bf16[512,1536]{1,0:T(8,128)(2,1)} custom-call(s32[2]{0:T(128)S(1)} %get-tuple-element.127.ids_ref, bf16[48,4096]{1,0:T(8,128)(2,1)S(1)} %get-tuple-element.80.refs_0_, bf16[48,4096]{1,0:T(8,128)(2,1)S(1)} %copy-done.11, bf16[48,4096]{1,0:T(8,128)(2,1)S(1)} %copy-done.9, bf16[48,4096]{1,0:T(8,128)(2,1)S(1)} %collective-permute-done.1.refs_3_, ...), custom_call_target="tpu_custom_call" | custom-call | flops 2250000128 | bytes 1 | tf_op jit(solution)/shard_map/weight_sums/pallas_call | solution.py:481
  101.2 2.8 %collective-permute-start.26 = (bf16[512,1536]{1,0:T(8,128)(2,1)}, bf16[512,1536]{1,0:T(8,128)(2,1)S(1)}, u32[]{:S(2)}, u32[]{:S(2)}) collective-permute-start(bf16[512,1536]{1,0:T(8,128)(2,1)} %weight_sums.5), channel_id=1, source_target_pairs={{0,16},{8,24},{16,0},{24,8},{1,17},{9,25},{17,1},{25,9},{2,18},{10... | collective-permute-start | bytes 4718600 | tf_op jit(solution)/shard_map/ppermute | solution.py:23
  104.0 6.4 %collective-permute-done.22.refs_3_ = bf16[48,2048]{1,0:T(8,128)(2,1)S(1)} collective-permute-done((bf16[48,2048]{1,0:T(8,128)(2,1)S(1)}, bf16[48,2048]{1,0:T(8,128)(2,1)S(1)}, u32[]{:S(2)}, u32[]{:S(2)}) %collective-permute-start.22) | collective-permute-done | bytes 196640 | tf_op jit(solution)/shard_map/ppermute | solution.py:23
  110.3 3.3 %collective-permute-done.23.refs_4_ = bf16[48,2048]{1,0:T(8,128)(2,1)S(1)} collective-permute-done((bf16[48,2048]{1,0:T(8,128)(2,1)S(1)}, bf16[48,2048]{1,0:T(8,128)(2,1)S(1)}, u32[]{:S(2)}, u32[]{:S(2)}) %collective-permute-start.23) | collective-permute-done | bytes 196640 | tf_op jit(solution)/shard_map/ppermute | solution.py:23
  113.7 2.4 %sum_slots.4 = bf16[128,2048]{1,0:T(8,128)(2,1)} custom-call(bf16[128,2176]{1,0:T(8,128)(2,1)S(1)} %copy-done.13, bf16[128,2048]{1,0:T(8,128)(2,1)} %collective-permute-done.4.refs_1_, bf16[48,2048]{1,0:T(8,128)(2,1)S(1)} %get-tuple-element.122.refs_2_, bf16[48,2048]{1,0:T(8,128)(2,1)S(1)} %collective-permute-done.22.refs_3_, ...), custom_call_target="tpu_custom_call" | custom-call | flops 13500000256 | bytes 1 | tf_op jit(solution)/shard_map/sum_slots/pallas_call | solution.py:268
  116.1 5.8 %collective-permute-start.29 = (bf16[128,2048]{1,0:T(8,128)(2,1)}, bf16[128,2048]{1,0:T(8,128)(2,1)}, u32[]{:S(2)}, u32[]{:S(2)}) collective-permute-start(bf16[128,2048]{1,0:T(8,128)(2,1)} %sum_slots.4), channel_id=1, source_target_pairs={{0,4},{1,5},{2,6},{3,7},{4,0},{5,1},{6,2},{7,3},{8,12},{9,13},{10,... | collective-permute-start | bytes 1572872 | tf_op jit(solution)/shard_map/ppermute | solution.py:23
  121.9 4.1 %collective-permute-start.27 = (bf16[48,4096]{1,0:T(8,128)(2,1)}, bf16[48,4096]{1,0:T(8,128)(2,1)S(1)}, u32[]{:S(2)}, u32[]{:S(2)}) collective-permute-start(bf16[48,4096]{1,0:T(8,128)(2,1)} %get-tuple-element.132), channel_id=1, source_target_pairs={{0,2},{1,3},{2,0},{3,1},{4,6},{5,7},{6,4},{7,5},{8,10},{9,11},{10,... | collective-permute-start | bytes 1179656 | tf_op jit(solution)/shard_map/ppermute | solution.py:23
  126.0 2.9 %weight_sums.6.refs_0_ = f32[512,768]{1,0:T(8,128)S(1)} custom-call(s32[2]{0:T(128)S(1)} %get-tuple-element.127.ids_ref, bf16[48,4096]{1,0:T(8,128)(2,1)} %copy-done.6, bf16[48,4096]{1,0:T(8,128)(2,1)} %copy-done.10, bf16[48,4096]{1,0:T(8,128)(2,1)} %copy-done.8, bf16[48,4096]{1,0:T(8,128)(2,1)} %copy-done.7, bf16[48,2048]{1,0:T(8,128)(2,1)} %copy-done.34, ...), custom_call_target="tpu_custom_call" | custom-call | flops 2624999936 | bytes 1 | tf_op jit(solution)/shard_map/weight_sums/pallas_call | solution.py:481
  131.8 3.9 %weight_sums.7.refs_0_.refs_1_ = f32[512,1536]{1,0:T(8,128)S(1)} custom-call(s32[2]{0:T(128)S(1)} %get-tuple-element.127.ids_ref, bf16[48,4096]{1,0:T(8,128)(2,1)} %copy-done.6, bf16[48,4096]{1,0:T(8,128)(2,1)} %copy-done.10, bf16[48,4096]{1,0:T(8,128)(2,1)} %copy-done.8, bf16[48,4096]{1,0:T(8,128)(2,1)} %copy-done.7, bf16[48,2048]{1,0:T(8,128)(2,1)} %copy-done.16, ...), custom_call_target="tpu_custom_call" | custom-call | flops 1500000000 | bytes 1 | tf_op jit(solution)/shard_map/weight_sums/pallas_call | solution.py:481
  138.4 2.9 %sum_slots.5 = (bf16[128,2048]{1,0:T(8,128)(2,1)}, f32[2,128]{1,0:T(2,128)}, f32[128,2048]{1,0:T(8,128)S(1)}) custom-call(s32[2,128]{1,0:T(2,128)S(1)} %bitcast.11, f32[2,128]{1,0:T(2,128)S(1)} %bitcast.8, f32[128,2]{1,0:T(8,128)S(1)} %copy-done.33, bf16[128,2048]{1,0:T(8,128)(2,1)S(1)} %copy-done.15, bf16[48,4096]{1,0:T(8,128)(2,1)S(1)} %copy-done.28, ...), custom_call_target="tpu_custom_call" | custom-call | flops 1 | bytes 1 | tf_op jit(solution)/shard_map/sum_slots/pallas_call | solution.py:268
  141.9 1.8 %add_halves.1 = bf16[128,2048]{1,0:T(8,128)(2,1)} custom-call(f32[128,2048]{1,0:T(8,128)S(1)} %get-tuple-element.135.a_ref, bf16[128,2048]{1,0:T(8,128)(2,1)} %collective-permute-done.29.b_ref), custom_call_target="tpu_custom_call" | custom-call | flops 1 | bytes 1 | tf_op jit(solution)/shard_map/add_halves/pallas_call | solution.py:503
  (139 shorter events, 32.5 us)
Async XLA Ops:
  1.9 28.8 %collective-permute-start = (bf16[128,2176]{1,0:T(8,128)(2,1)S(1)}, bf16[128,2176]{1,0:T(8,128)(2,1)S(1)}, u32[]{:S(2)}, u32[]{:S(2)}) collective-permute-start(bf16[128,2176]{1,0:T(8,128)(2,1)S(1)} %message.1), channel_id=1, source_target_pairs={{0,4},{1,5},{2,6},{3,7},{4,0},{5,1},{6,2},{7,3},{8,12},{9,13},{10,... | collective-permute-start | bytes 1671176 | tf_op jit(solution)/shard_map/ppermute | solution.py:23
  8.6 22.0 %collective-permute-start.1 = (bf16[48,4096]{1,0:T(8,128)(2,1)}, bf16[48,4096]{1,0:T(8,128)(2,1)S(1)}, u32[]{:S(2)}, u32[]{:S(2)}) collective-permute-start(bf16[48,4096]{1,0:T(8,128)(2,1)} %get-tuple-element.75), channel_id=1, source_target_pairs={{0,1},{1,0},{2,3},{3,2},{4,5},{5,4},{6,7},{7,6},{8,9},{9,8},{10,11... | collective-permute-start | bytes 1179656 | tf_op jit(solution)/shard_map/ppermute | solution.py:23
  10.1 22.8 %collective-permute-start.2 = (bf16[48,4096]{1,0:T(8,128)(2,1)S(1)}, bf16[48,4096]{1,0:T(8,128)(2,1)S(1)}, u32[]{:S(2)}, u32[]{:S(2)}) collective-permute-start(bf16[48,4096]{1,0:T(8,128)(2,1)S(1)} %get-tuple-element.76), channel_id=1, source_target_pairs={{0,2},{1,3},{2,0},{3,1},{4,6},{5,7},{6,4},{7,5},{8,10},{9,11},{10,... | collective-permute-start | bytes 1179656 | tf_op jit(solution)/shard_map/ppermute | solution.py:23
  11.7 31.2 %collective-permute-start.3 = (bf16[48,4096]{1,0:T(8,128)(2,1)S(1)}, bf16[48,4096]{1,0:T(8,128)(2,1)S(1)}, u32[]{:S(2)}, u32[]{:S(2)}) collective-permute-start(bf16[48,4096]{1,0:T(8,128)(2,1)S(1)} %get-tuple-element.77), channel_id=1, source_target_pairs={{0,3},{1,2},{2,1},{3,0},{4,7},{5,6},{6,5},{7,4},{8,11},{9,10},{10,... | collective-permute-start | bytes 1179656 | tf_op jit(solution)/shard_map/ppermute | solution.py:23
  30.6 26.3 %collective-permute-start.4 = (bf16[128,2048]{1,0:T(8,128)(2,1)}, bf16[128,2048]{1,0:T(8,128)(2,1)}, u32[]{:S(2)}, u32[]{:S(2)}) collective-permute-start(bf16[128,2048]{1,0:T(8,128)(2,1)} %refs_3_.3), channel_id=1, source_target_pairs={{0,4},{1,5},{2,6},{3,7},{4,0},{5,1},{6,2},{7,3},{8,12},{9,13},{10,... | collective-permute-start | bytes 1572872 | tf_op jit(solution)/shard_map/ppermute | solution.py:23
  43.5 16.6 %collective-permute-start.9 = (bf16[48,2048]{1,0:T(8,128)(2,1)S(1)}, bf16[48,2048]{1,0:T(8,128)(2,1)S(1)}, u32[]{:S(2)}, u32[]{:S(2)}) collective-permute-start(bf16[48,2048]{1,0:T(8,128)(2,1)S(1)} %get-tuple-element.91), channel_id=1, source_target_pairs={{0,1},{1,0},{2,3},{3,2},{4,5},{5,4},{6,7},{7,6},{8,9},{9,8},{10,11... | collective-permute-start | bytes 589832 | tf_op jit(solution)/shard_map/ppermute | solution.py:23
  44.7 15.9 %collective-permute-start.10 = (bf16[48,2048]{1,0:T(8,128)(2,1)S(1)}, bf16[48,2048]{1,0:T(8,128)(2,1)S(1)}, u32[]{:S(2)}, u32[]{:S(2)}) collective-permute-start(bf16[48,2048]{1,0:T(8,128)(2,1)S(1)} %get-tuple-element.92), channel_id=1, source_target_pairs={{0,2},{1,3},{2,0},{3,1},{4,6},{5,7},{6,4},{7,5},{8,10},{9,11},{10,... | collective-permute-start | bytes 589832 | tf_op jit(solution)/shard_map/ppermute | solution.py:23
  44.7 17.5 %collective-permute-start.11 = (bf16[48,2048]{1,0:T(8,128)(2,1)S(1)}, bf16[48,2048]{1,0:T(8,128)(2,1)S(1)}, u32[]{:S(2)}, u32[]{:S(2)}) collective-permute-start(bf16[48,2048]{1,0:T(8,128)(2,1)S(1)} %get-tuple-element.93), channel_id=1, source_target_pairs={{0,3},{1,2},{2,1},{3,0},{4,7},{5,6},{6,5},{7,4},{8,11},{9,10},{10,... | collective-permute-start | bytes 589832 | tf_op jit(solution)/shard_map/ppermute | solution.py:23
  58.9 11.8 %collective-permute-start.5 = (bf16[48,2048]{1,0:T(8,128)(2,1)S(1)}, bf16[48,2048]{1,0:T(8,128)(2,1)S(1)}, u32[]{:S(2)}, u32[]{:S(2)}) collective-permute-start(bf16[48,2048]{1,0:T(8,128)(2,1)S(1)} %get-tuple-element.88), channel_id=1, source_target_pairs={{0,1},{1,0},{2,3},{3,2},{4,5},{5,4},{6,7},{7,6},{8,9},{9,8},{10,11... | collective-permute-start | bytes 589832 | tf_op jit(solution)/shard_map/ppermute | solution.py:23
  60.1 16.3 %collective-permute-start.13 = (bf16[192,2304]{1,0:T(8,128)(2,1)S(1)}, bf16[192,2304]{1,0:T(8,128)(2,1)S(1)}, u32[]{:S(2)}, u32[]{:S(2)}) collective-permute-start(bf16[192,2304]{1,0:T(8,128)(2,1)S(1)} %get-tuple-element.100.refs_10_.refs_14_), channel_id=1, source_target_pairs={{0,8},{8,0},{16,24},{24,16},{1,9},{9,1},{17,25},{25,17},{2,10},{10... | collective-permute-start | bytes 2654216 | tf_op jit(solution)/shard_map/ppermute | solution.py:23
  60.1 15.4 %collective-permute-start.8 = (bf16[192,2048]{1,0:T(8,128)(2,1)S(1)}, bf16[192,2048]{1,0:T(8,128)(2,1)S(1)}, u32[]{:S(2)}, u32[]{:S(2)}) collective-permute-start(bf16[192,2048]{1,0:T(8,128)(2,1)S(1)} %get-tuple-element.84), channel_id=1, source_target_pairs={{0,8},{8,0},{16,24},{24,16},{1,9},{9,1},{17,25},{25,17},{2,10},{10... | collective-permute-start | bytes 2359304 | tf_op jit(solution)/shard_map/ppermute | solution.py:23
  72.7 13.4 %collective-permute-start.15 = (bf16[48,2048]{1,0:T(8,128)(2,1)S(1)}, bf16[48,2048]{1,0:T(8,128)(2,1)S(1)}, u32[]{:S(2)}, u32[]{:S(2)}) collective-permute-start(bf16[48,2048]{1,0:T(8,128)(2,1)S(1)} %get-tuple-element.111), channel_id=1, source_target_pairs={{0,3},{1,2},{2,1},{3,0},{4,7},{5,6},{6,5},{7,4},{8,11},{9,10},{10,... | collective-permute-start | bytes 589832 | tf_op jit(solution)/shard_map/ppermute | solution.py:23
  74.1 12.1 %collective-permute-start.16 = (bf16[48,2048]{1,0:T(8,128)(2,1)S(1)}, bf16[48,2048]{1,0:T(8,128)(2,1)S(1)}, u32[]{:S(2)}, u32[]{:S(2)}) collective-permute-start(bf16[48,2048]{1,0:T(8,128)(2,1)S(1)} %get-tuple-element.112), channel_id=1, source_target_pairs={{0,2},{1,3},{2,0},{3,1},{4,6},{5,7},{6,4},{7,5},{8,10},{9,11},{10,... | collective-permute-start | bytes 589832 | tf_op jit(solution)/shard_map/ppermute | solution.py:23
  75.5 11.2 %collective-permute-start.17 = (bf16[48,2048]{1,0:T(8,128)(2,1)S(1)}, bf16[48,2048]{1,0:T(8,128)(2,1)S(1)}, u32[]{:S(2)}, u32[]{:S(2)}) collective-permute-start(bf16[48,2048]{1,0:T(8,128)(2,1)S(1)} %get-tuple-element.113), channel_id=1, source_target_pairs={{0,1},{1,0},{2,3},{3,2},{4,5},{5,4},{6,7},{7,6},{8,9},{9,8},{10,11... | collective-permute-start | bytes 589832 | tf_op jit(solution)/shard_map/ppermute | solution.py:23
  76.4 17.2 %collective-permute-start.18 = (bf16[48,4096]{1,0:T(8,128)(2,1)S(1)}, bf16[48,4096]{1,0:T(8,128)(2,1)S(1)}, u32[]{:S(2)}, u32[]{:S(2)}) collective-permute-start(bf16[48,4096]{1,0:T(8,128)(2,1)S(1)} %get-tuple-element.118), channel_id=1, source_target_pairs={{0,3},{1,2},{2,1},{3,0},{4,7},{5,6},{6,5},{7,4},{8,11},{9,10},{10,... | collective-permute-start | bytes 1179656 | tf_op jit(solution)/shard_map/ppermute | solution.py:23
  79.2 21.9 %collective-permute-start.21 = (bf16[512,768]{1,0:T(8,128)(2,1)S(1)}, bf16[512,768]{1,0:T(8,128)(2,1)S(1)}, u32[]{:S(2)}, u32[]{:S(2)}) collective-permute-start(bf16[512,768]{1,0:T(8,128)(2,1)S(1)} %weight_sums.4), channel_id=1, source_target_pairs={{0,16},{8,24},{16,0},{24,8},{1,17},{9,25},{17,1},{25,9},{2,18},{10... | collective-permute-start | bytes 2359304 | tf_op jit(solution)/shard_map/ppermute | solution.py:23
  89.4 42.4 %collective-permute-start.25 = (bf16[128,2176]{1,0:T(8,128)(2,1)}, bf16[128,2176]{1,0:T(8,128)(2,1)}, u32[]{:S(2)}, u32[]{:S(2)}) collective-permute-start(bf16[128,2176]{1,0:T(8,128)(2,1)} %sum_slots.3), channel_id=1, source_target_pairs={{0,4},{1,5},{2,6},{3,7},{4,0},{5,1},{6,2},{7,3},{8,12},{9,13},{10,... | collective-permute-start | bytes 1671176 | tf_op jit(solution)/shard_map/ppermute | solution.py:23
  94.4 15.9 %collective-permute-start.22 = (bf16[48,2048]{1,0:T(8,128)(2,1)S(1)}, bf16[48,2048]{1,0:T(8,128)(2,1)S(1)}, u32[]{:S(2)}, u32[]{:S(2)}) collective-permute-start(bf16[48,2048]{1,0:T(8,128)(2,1)S(1)} %get-tuple-element.123), channel_id=1, source_target_pairs={{0,3},{1,2},{2,1},{3,0},{4,7},{5,6},{6,5},{7,4},{8,11},{9,10},{10,... | collective-permute-start | bytes 589832 | tf_op jit(solution)/shard_map/ppermute | solution.py:23
  95.7 18.0 %collective-permute-start.23 = (bf16[48,2048]{1,0:T(8,128)(2,1)S(1)}, bf16[48,2048]{1,0:T(8,128)(2,1)S(1)}, u32[]{:S(2)}, u32[]{:S(2)}) collective-permute-start(bf16[48,2048]{1,0:T(8,128)(2,1)S(1)} %get-tuple-element.124), channel_id=1, source_target_pairs={{0,2},{1,3},{2,0},{3,1},{4,6},{5,7},{6,4},{7,5},{8,10},{9,11},{10,... | collective-permute-start | bytes 589832 | tf_op jit(solution)/shard_map/ppermute | solution.py:23
  97.1 16.6 %collective-permute-start.24 = (bf16[48,2048]{1,0:T(8,128)(2,1)S(1)}, bf16[48,2048]{1,0:T(8,128)(2,1)S(1)}, u32[]{:S(2)}, u32[]{:S(2)}) collective-permute-start(bf16[48,2048]{1,0:T(8,128)(2,1)S(1)} %get-tuple-element.125), channel_id=1, source_target_pairs={{0,1},{1,0},{2,3},{3,2},{4,5},{5,4},{6,7},{7,6},{8,9},{9,8},{10,11... | collective-permute-start | bytes 589832 | tf_op jit(solution)/shard_map/ppermute | solution.py:23
  101.2 35.4 %collective-permute-start.26 = (bf16[512,1536]{1,0:T(8,128)(2,1)}, bf16[512,1536]{1,0:T(8,128)(2,1)S(1)}, u32[]{:S(2)}, u32[]{:S(2)}) collective-permute-start(bf16[512,1536]{1,0:T(8,128)(2,1)} %weight_sums.5), channel_id=1, source_target_pairs={{0,16},{8,24},{16,0},{24,8},{1,17},{9,25},{17,1},{25,9},{2,18},{10... | collective-permute-start | bytes 4718600 | tf_op jit(solution)/shard_map/ppermute | solution.py:23
  116.1 25.8 %collective-permute-start.29 = (bf16[128,2048]{1,0:T(8,128)(2,1)}, bf16[128,2048]{1,0:T(8,128)(2,1)}, u32[]{:S(2)}, u32[]{:S(2)}) collective-permute-start(bf16[128,2048]{1,0:T(8,128)(2,1)} %sum_slots.4), channel_id=1, source_target_pairs={{0,4},{1,5},{2,6},{3,7},{4,0},{5,1},{6,2},{7,3},{8,12},{9,13},{10,... | collective-permute-start | bytes 1572872 | tf_op jit(solution)/shard_map/ppermute | solution.py:23
  121.9 16.4 %collective-permute-start.27 = (bf16[48,4096]{1,0:T(8,128)(2,1)}, bf16[48,4096]{1,0:T(8,128)(2,1)S(1)}, u32[]{:S(2)}, u32[]{:S(2)}) collective-permute-start(bf16[48,4096]{1,0:T(8,128)(2,1)} %get-tuple-element.132), channel_id=1, source_target_pairs={{0,2},{1,3},{2,0},{3,1},{4,6},{5,7},{6,4},{7,5},{8,10},{9,11},{10,... | collective-permute-start | bytes 1179656 | tf_op jit(solution)/shard_map/ppermute | solution.py:23
  126.0 12.4 %collective-permute-start.28 = (bf16[48,4096]{1,0:T(8,128)(2,1)}, bf16[48,4096]{1,0:T(8,128)(2,1)}, u32[]{:S(2)}, u32[]{:S(2)}) collective-permute-start(bf16[48,4096]{1,0:T(8,128)(2,1)} %get-tuple-element.133), channel_id=1, source_target_pairs={{0,1},{1,0},{2,3},{3,2},{4,5},{5,4},{6,7},{7,6},{8,9},{9,8},{10,11... | collective-permute-start | bytes 1179656 | tf_op jit(solution)/shard_map/ppermute | solution.py:23
  (47 other events, 762.5 us)

commit v7 on v6

--- a/solution.py
+++ b/solution.py
@@ -388,15 +388,22 @@
     c_refs, active_ref, slope_ref, held = turned(refs[:count]), refs[count], refs[count + 1], refs[count + 2 : count + 5]
     in_refs = refs[count + 5 : 2 * count + 5]
     gg_ref, gu_ref, acc, gate_ref, up_ref, down_ref, sems = refs[2 * count + 5 :]
-    wait = fetch(held, (gate_ref, up_ref, down_ref), sems, tiles(gg_ref.shape[1]))
+    weight_refs = (gate_ref, up_ref, down_ref)
+    copies = [pltpu.make_async_copy(w.at[0], r, sems.at[i, 0]) for i, (w, r) in enumerate(zip(held, weight_refs))]
+    for i in (2, 0, 1):
+        copies[i].start()
     c = join(c_refs)
     for step, inner in enumerate(tiles(gg_ref.shape[1])):
-        wait(step)
+        if step == 0:
+            copies[2].wait()
         grad_hidden = dot(c, down_ref[:, inner])
         gu = (grad_hidden * active_ref[:, inner]).astype(bf16)
         gg = (grad_hidden * slope_ref[:, inner]).astype(bf16)
         gu_ref[:, inner] = gu
         gg_ref[:, inner] = gg
+        if step == 0:
+            copies[0].wait()
+            copies[1].wait()
         for cols in chunks(acc.shape[1]):
             back = dot(gg, gate_ref[cols, inner], ((1,), (1,))) + dot(gu, up_ref[cols, inner], ((1,), (1,)))
             add_to(acc, step == 0, cols, back)

time: 145 us -> 146 us (level)
  transfers between devices with their start and end apart: 30 -> 30, of which waited for: 11 -> 9; matrix products, arithmetic and copies ran while one was open for 1% -> 1% of each run, Pallas kernels for 33% -> 32%
where the time goes in v7:
time: 146 us; the launch traced here: 145 us
  Pallas kernels  49.6 us (34%)
  waiting for transfers between devices  46.9 us (32%)
  starting transfers between devices  43.9 us (30%)
  local copies, waits for them, and re-layouts  3.56 us (2%)
    ppermute x30, waiting for transfers between devices, exchange(): return lax.ppermute(x, axis, [(i, i ^ bit) for i in range(size)])  46.9 us
    ppermute x30, starting transfers between devices, exchange(): return lax.ppermute(x, axis, [(i, i ^ bit) for i in range(size)])  43.9 us
    pallas_call x3, Pallas kernels, expert_call(): pl.pallas_call(functools.partial(kernel, form.count), out_shape=out_shape...  19 us
    pallas_call x4, Pallas kernels, weight_sums(): pl.pallas_call(functools.partial(weight_kernel, [len(g[0]) for g in left]...  11.3 us
    pallas_call x3, Pallas kernels, back(): pl.pallas_call(functools.partial(back_kernel, form, offsets, combine is n...  8.02 us
    pallas_call x3, Pallas kernels, gather(): pl.pallas_call(functools.partial(gather_kernel, form, scaled, width, plai...  5.09 us
    unnamed x83, local copies, waits for them, and re-layouts  3.54 us
  transfers between devices with their start and end apart: 30, of which 9 were waited for; matrix products, arithmetic and copies ran while one was open for 1% of the time, Pallas kernels for 32%

profile of v7, /device:TPU:0, one launch (start us, length us, event | category | flops | bytes accessed | tf_op | source)
XLA Modules:
  0.0 145.1 jit_solution(10392737620099847690)
XLA Ops:
  1.9 4.1 %collective-permute-start = (bf16[128,2176]{1,0:T(8,128)(2,1)S(1)}, bf16[128,2176]{1,0:T(8,128)(2,1)S(1)}, u32[]{:S(2)}, u32[]{:S(2)}) collective-permute-start(bf16[128,2176]{1,0:T(8,128)(2,1)S(1)} %message.1), channel_id=1, source_target_pairs={{0,4},{1,5},{2,6},{3,7},{4,0},{5,1},{6,2},{7,3},{8,12},{9,13},{10,... | collective-permute-start | bytes 1671176 | tf_op jit(solution)/shard_map/ppermute | solution.py:23
  6.0 2.6 %gather_slots.3 = (bf16[48,4096]{1,0:T(8,128)(2,1)S(1)}, bf16[48,4096]{1,0:T(8,128)(2,1)}, bf16[48,4096]{1,0:T(8,128)(2,1)S(1)}, bf16[48,4096]{1,0:T(8,128)(2,1)S(1)}) custom-call(s32[2,128]{1,0:T(2,128)} %bitcast.10, f32[2,128]{1,0:T(2,128)} %bitcast.7, bf16[128,2048]{1,0:T(8,128)(2,1)} %refs_2_.2, bf16[128,2048]{1,0:T(8,128)(2,1)} %refs_3_.3), custom_call_target="tpu_custom_call" | custom-call | flops 1 | bytes 1 | tf_op jit(solution)/shard_map/gather_slots/pallas_call | solution.py:187
  12.1 18.5 %collective-permute-done.refs_0_.refs_1_ = bf16[128,2176]{1,0:T(8,128)(2,1)S(1)} collective-permute-done((bf16[128,2176]{1,0:T(8,128)(2,1)S(1)}, bf16[128,2176]{1,0:T(8,128)(2,1)S(1)}, u32[]{:S(2)}, u32[]{:S(2)}) %collective-permute-start) | collective-permute-done | bytes 557088 | tf_op jit(solution)/shard_map/ppermute | solution.py:23
  30.7 2.3 %collective-permute-done.2.refs_2_ = bf16[48,4096]{1,0:T(8,128)(2,1)S(1)} collective-permute-done((bf16[48,4096]{1,0:T(8,128)(2,1)S(1)}, bf16[48,4096]{1,0:T(8,128)(2,1)S(1)}, u32[]{:S(2)}, u32[]{:S(2)}) %collective-permute-start.2) | collective-permute-done | bytes 393248 | tf_op jit(solution)/shard_map/ppermute | solution.py:23
  32.9 10.0 %collective-permute-done.3.refs_1_ = bf16[48,4096]{1,0:T(8,128)(2,1)S(1)} collective-permute-done((bf16[48,4096]{1,0:T(8,128)(2,1)S(1)}, bf16[48,4096]{1,0:T(8,128)(2,1)S(1)}, u32[]{:S(2)}, u32[]{:S(2)}) %collective-permute-start.3) | collective-permute-done | bytes 393248 | tf_op jit(solution)/shard_map/ppermute | solution.py:23
  44.7 2.3 %collective-permute-start.11 = (bf16[48,2048]{1,0:T(8,128)(2,1)S(1)}, bf16[48,2048]{1,0:T(8,128)(2,1)S(1)}, u32[]{:S(2)}, u32[]{:S(2)}) collective-permute-start(bf16[48,2048]{1,0:T(8,128)(2,1)S(1)} %get-tuple-element.93), channel_id=1, source_target_pairs={{0,3},{1,2},{2,1},{3,0},{4,7},{5,6},{6,5},{7,4},{8,11},{9,10},{10,... | collective-permute-start | bytes 589832 | tf_op jit(solution)/shard_map/ppermute | solution.py:23
  47.0 9.1 %expert_both.1 = (bf16[48,4096]{1,0:T(8,128)(2,1)S(1)}, bf16[48,4096]{1,0:T(8,128)(2,1)}, bf16[48,4096]{1,0:T(8,128)(2,1)}, bf16[48,4096]{1,0:T(8,128)(2,1)S(1)}...) custom-call(bf16[48,4096]{1,0:T(8,128)(2,1)S(1)} %get-tuple-element.80.refs_0_, ...), custom_call_target="tpu_custom_call" | custom-call | flops 1 | bytes 1 | tf_op jit(solution)/shard_map/expert_both/pallas_call | solution.py:366
  62.2 2.9 %collective-permute-start.7 = (bf16[48,2048]{1,0:T(8,128)(2,1)S(1)}, bf16[48,2048]{1,0:T(8,128)(2,1)S(1)}, u32[]{:S(2)}, u32[]{:S(2)}) collective-permute-start(bf16[48,2048]{1,0:T(8,128)(2,1)S(1)} %get-tuple-element.90), channel_id=1, source_target_pairs={{0,3},{1,2},{2,1},{3,0},{4,7},{5,6},{6,5},{7,4},{8,11},{9,10},{10,... | collective-permute-start | bytes 589832 | tf_op jit(solution)/shard_map/ppermute | solution.py:23
  65.1 5.4 %expert_forward.1 = (bf16[48,2048]{1,0:T(8,128)(2,1)S(1)}, bf16[48,2048]{1,0:T(8,128)(2,1)S(1)}, bf16[48,2048]{1,0:T(8,128)(2,1)S(1)}, bf16[48,2048]{1,0:T(8,128...) custom-call(bf16[48,2048]{1,0:T(8,128)(2,1)S(1)} %get-tuple-element., ...), custom_call_target="tpu_custom_call" | custom-call | flops 1875000064 | bytes 1 | tf_op jit(solution)/shard_map/expert_forward/pallas_call | solution.py:366
  80.9 4.4 %expert_backward.1 = (bf16[48,2048]{1,0:T(8,128)(2,1)S(1)}, bf16[48,2048]{1,0:T(8,128)(2,1)S(1)}, bf16[48,2048]{1,0:T(8,128)(2,1)S(1)}, bf16[48,2048]{1,0:T(8,12...) custom-call(bf16[48,2048]{1,0:T(8,128)(2,1)S(1)} %get-tuple-element.102.refs_0_.refs_4_, ...), custom_call_target="tpu_custom_call" | custom-call | flops 3750000128 | bytes 1 | tf_op jit(solution)/shard_map/expert_backward/pallas_call | solution.py:366
  85.9 2.7 %sum_slots.3 = bf16[128,2176]{1,0:T(8,128)(2,1)} custom-call(bf16[128,2176]{1,0:T(8,128)(2,1)S(1)} %copy-done.13, bf16[128,2048]{1,0:T(8,128)(2,1)} %collective-permute-done.4.refs_1_, bf16[48,2048]{1,0:T(8,128)(2,1)S(1)} %get-tuple-element.110.refs_2_, bf16[48,2048]{1,0:T(8,128)(2,1)S(1)} %collective-permute-done.15.refs_3_, ...), custom_call_target="tpu_custom_call" | custom-call | flops 2250000128 | bytes 1 | tf_op jit(solution)/shard_map/sum_slots/pallas_call | solution.py:268
  88.7 3.4 %collective-permute-start.25 = (bf16[128,2176]{1,0:T(8,128)(2,1)}, bf16[128,2176]{1,0:T(8,128)(2,1)}, u32[]{:S(2)}, u32[]{:S(2)}) collective-permute-start(bf16[128,2176]{1,0:T(8,128)(2,1)} %sum_slots.3), channel_id=1, source_target_pairs={{0,4},{1,5},{2,6},{3,7},{4,0},{5,1},{6,2},{7,3},{8,12},{9,13},{10,... | collective-permute-start | bytes 1671176 | tf_op jit(solution)/shard_map/ppermute | solution.py:23
  92.1 3.4 %collective-permute-done.18.refs_5_ = bf16[48,4096]{1,0:T(8,128)(2,1)S(1)} collective-permute-done((bf16[48,4096]{1,0:T(8,128)(2,1)S(1)}, bf16[48,4096]{1,0:T(8,128)(2,1)S(1)}, u32[]{:S(2)}, u32[]{:S(2)}) %collective-permute-start.18) | collective-permute-done | bytes 393248 | tf_op jit(solution)/shard_map/ppermute | solution.py:23
  97.1 2.7 %collective-permute-start.24 = (bf16[48,2048]{1,0:T(8,128)(2,1)S(1)}, bf16[48,2048]{1,0:T(8,128)(2,1)S(1)}, u32[]{:S(2)}, u32[]{:S(2)}) collective-permute-start(bf16[48,2048]{1,0:T(8,128)(2,1)S(1)} %get-tuple-element.125), channel_id=1, source_target_pairs={{0,1},{1,0},{2,3},{3,2},{4,5},{5,4},{6,7},{7,6},{8,9},{9,8},{10,11... | collective-permute-start | bytes 589832 | tf_op jit(solution)/shard_map/ppermute | solution.py:23
  99.8 3.1 %weight_sums.5 = bf16[512,1536]{1,0:T(8,128)(2,1)} custom-call(s32[2]{0:T(128)S(1)} %get-tuple-element.127.ids_ref, bf16[48,4096]{1,0:T(8,128)(2,1)S(1)} %get-tuple-element.80.refs_0_, bf16[48,4096]{1,0:T(8,128)(2,1)S(1)} %copy-done.11, bf16[48,4096]{1,0:T(8,128)(2,1)S(1)} %copy-done.9, bf16[48,4096]{1,0:T(8,128)(2,1)S(1)} %collective-permute-done.1.refs_3_, ...), custom_call_target="tpu_custom_call" | custom-call | flops 2250000128 | bytes 1 | tf_op jit(solution)/shard_map/weight_sums/pallas_call | solution.py:488
  105.2 4.4 %collective-permute-done.22.refs_3_ = bf16[48,2048]{1,0:T(8,128)(2,1)S(1)} collective-permute-done((bf16[48,2048]{1,0:T(8,128)(2,1)S(1)}, bf16[48,2048]{1,0:T(8,128)(2,1)S(1)}, u32[]{:S(2)}, u32[]{:S(2)}) %collective-permute-start.22) | collective-permute-done | bytes 196640 | tf_op jit(solution)/shard_map/ppermute | solution.py:23
  109.6 3.3 %collective-permute-done.23.refs_4_ = bf16[48,2048]{1,0:T(8,128)(2,1)S(1)} collective-permute-done((bf16[48,2048]{1,0:T(8,128)(2,1)S(1)}, bf16[48,2048]{1,0:T(8,128)(2,1)S(1)}, u32[]{:S(2)}, u32[]{:S(2)}) %collective-permute-start.23) | collective-permute-done | bytes 196640 | tf_op jit(solution)/shard_map/ppermute | solution.py:23
  112.9 2.4 %sum_slots.4 = bf16[128,2048]{1,0:T(8,128)(2,1)} custom-call(bf16[128,2176]{1,0:T(8,128)(2,1)S(1)} %copy-done.13, bf16[128,2048]{1,0:T(8,128)(2,1)} %collective-permute-done.4.refs_1_, bf16[48,2048]{1,0:T(8,128)(2,1)S(1)} %get-tuple-element.122.refs_2_, bf16[48,2048]{1,0:T(8,128)(2,1)S(1)} %collective-permute-done.22.refs_3_, ...), custom_call_target="tpu_custom_call" | custom-call | flops 13500000256 | bytes 1 | tf_op jit(solution)/shard_map/sum_slots/pallas_call | solution.py:268
  115.3 6.4 %collective-permute-start.29 = (bf16[128,2048]{1,0:T(8,128)(2,1)}, bf16[128,2048]{1,0:T(8,128)(2,1)}, u32[]{:S(2)}, u32[]{:S(2)}) collective-permute-start(bf16[128,2048]{1,0:T(8,128)(2,1)} %sum_slots.4), channel_id=1, source_target_pairs={{0,4},{1,5},{2,6},{3,7},{4,0},{5,1},{6,2},{7,3},{8,12},{9,13},{10,... | collective-permute-start | bytes 1572872 | tf_op jit(solution)/shard_map/ppermute | solution.py:23
  121.8 2.5 %collective-permute-start.27 = (bf16[48,4096]{1,0:T(8,128)(2,1)}, bf16[48,4096]{1,0:T(8,128)(2,1)S(1)}, u32[]{:S(2)}, u32[]{:S(2)}) collective-permute-start(bf16[48,4096]{1,0:T(8,128)(2,1)} %get-tuple-element.132), channel_id=1, source_target_pairs={{0,2},{1,3},{2,0},{3,1},{4,6},{5,7},{6,4},{7,5},{8,10},{9,11},{10,... | collective-permute-start | bytes 1179656 | tf_op jit(solution)/shard_map/ppermute | solution.py:23
  124.2 2.8 %collective-permute-start.28 = (bf16[48,4096]{1,0:T(8,128)(2,1)}, bf16[48,4096]{1,0:T(8,128)(2,1)}, u32[]{:S(2)}, u32[]{:S(2)}) collective-permute-start(bf16[48,4096]{1,0:T(8,128)(2,1)} %get-tuple-element.133), channel_id=1, source_target_pairs={{0,1},{1,0},{2,3},{3,2},{4,5},{5,4},{6,7},{7,6},{8,9},{9,8},{10,11... | collective-permute-start | bytes 1179656 | tf_op jit(solution)/shard_map/ppermute | solution.py:23
  127.0 2.9 %weight_sums.6.refs_0_ = f32[512,768]{1,0:T(8,128)S(1)} custom-call(s32[2]{0:T(128)S(1)} %get-tuple-element.127.ids_ref, bf16[48,4096]{1,0:T(8,128)(2,1)} %copy-done.6, bf16[48,4096]{1,0:T(8,128)(2,1)} %copy-done.10, bf16[48,4096]{1,0:T(8,128)(2,1)} %copy-done.8, bf16[48,4096]{1,0:T(8,128)(2,1)} %copy-done.7, bf16[48,2048]{1,0:T(8,128)(2,1)} %copy-done.34, ...), custom_call_target="tpu_custom_call" | custom-call | flops 2624999936 | bytes 1 | tf_op jit(solution)/shard_map/weight_sums/pallas_call | solution.py:488
  132.8 3.9 %weight_sums.7.refs_0_.refs_1_ = f32[512,1536]{1,0:T(8,128)S(1)} custom-call(s32[2]{0:T(128)S(1)} %get-tuple-element.127.ids_ref, bf16[48,4096]{1,0:T(8,128)(2,1)} %copy-done.6, bf16[48,4096]{1,0:T(8,128)(2,1)} %copy-done.10, bf16[48,4096]{1,0:T(8,128)(2,1)} %copy-done.8, bf16[48,4096]{1,0:T(8,128)(2,1)} %copy-done.7, bf16[48,2048]{1,0:T(8,128)(2,1)} %copy-done.16, ...), custom_call_target="tpu_custom_call" | custom-call | flops 1500000000 | bytes 1 | tf_op jit(solution)/shard_map/weight_sums/pallas_call | solution.py:488
  140.4 2.9 %sum_slots.5 = (bf16[128,2048]{1,0:T(8,128)(2,1)}, f32[2,128]{1,0:T(2,128)}, f32[128,2048]{1,0:T(8,128)S(1)}) custom-call(s32[2,128]{1,0:T(2,128)S(1)} %bitcast.11, f32[2,128]{1,0:T(2,128)S(1)} %bitcast.8, f32[128,2]{1,0:T(8,128)S(1)} %copy-done.33, bf16[128,2048]{1,0:T(8,128)(2,1)S(1)} %copy-done.15, bf16[48,4096]{1,0:T(8,128)(2,1)S(1)} %copy-done.28, ...), custom_call_target="tpu_custom_call" | custom-call | flops 1 | bytes 1 | tf_op jit(solution)/shard_map/sum_slots/pallas_call | solution.py:268
  (139 shorter events, 35.4 us)
Async XLA Ops:
  1.9 28.8 %collective-permute-start = (bf16[128,2176]{1,0:T(8,128)(2,1)S(1)}, bf16[128,2176]{1,0:T(8,128)(2,1)S(1)}, u32[]{:S(2)}, u32[]{:S(2)}) collective-permute-start(bf16[128,2176]{1,0:T(8,128)(2,1)S(1)} %message.1), channel_id=1, source_target_pairs={{0,4},{1,5},{2,6},{3,7},{4,0},{5,1},{6,2},{7,3},{8,12},{9,13},{10,... | collective-permute-start | bytes 1671176 | tf_op jit(solution)/shard_map/ppermute | solution.py:23
  8.6 22.0 %collective-permute-start.1 = (bf16[48,4096]{1,0:T(8,128)(2,1)}, bf16[48,4096]{1,0:T(8,128)(2,1)S(1)}, u32[]{:S(2)}, u32[]{:S(2)}) collective-permute-start(bf16[48,4096]{1,0:T(8,128)(2,1)} %get-tuple-element.75), channel_id=1, source_target_pairs={{0,1},{1,0},{2,3},{3,2},{4,5},{5,4},{6,7},{7,6},{8,9},{9,8},{10,11... | collective-permute-start | bytes 1179656 | tf_op jit(solution)/shard_map/ppermute | solution.py:23
  10.1 22.8 %collective-permute-start.2 = (bf16[48,4096]{1,0:T(8,128)(2,1)S(1)}, bf16[48,4096]{1,0:T(8,128)(2,1)S(1)}, u32[]{:S(2)}, u32[]{:S(2)}) collective-permute-start(bf16[48,4096]{1,0:T(8,128)(2,1)S(1)} %get-tuple-element.76), channel_id=1, source_target_pairs={{0,2},{1,3},{2,0},{3,1},{4,6},{5,7},{6,4},{7,5},{8,10},{9,11},{10,... | collective-permute-start | bytes 1179656 | tf_op jit(solution)/shard_map/ppermute | solution.py:23
  11.7 31.2 %collective-permute-start.3 = (bf16[48,4096]{1,0:T(8,128)(2,1)S(1)}, bf16[48,4096]{1,0:T(8,128)(2,1)S(1)}, u32[]{:S(2)}, u32[]{:S(2)}) collective-permute-start(bf16[48,4096]{1,0:T(8,128)(2,1)S(1)} %get-tuple-element.77), channel_id=1, source_target_pairs={{0,3},{1,2},{2,1},{3,0},{4,7},{5,6},{6,5},{7,4},{8,11},{9,10},{10,... | collective-permute-start | bytes 1179656 | tf_op jit(solution)/shard_map/ppermute | solution.py:23
  30.6 26.3 %collective-permute-start.4 = (bf16[128,2048]{1,0:T(8,128)(2,1)}, bf16[128,2048]{1,0:T(8,128)(2,1)}, u32[]{:S(2)}, u32[]{:S(2)}) collective-permute-start(bf16[128,2048]{1,0:T(8,128)(2,1)} %refs_3_.3), channel_id=1, source_target_pairs={{0,4},{1,5},{2,6},{3,7},{4,0},{5,1},{6,2},{7,3},{8,12},{9,13},{10,... | collective-permute-start | bytes 1572872 | tf_op jit(solution)/shard_map/ppermute | solution.py:23
  43.5 16.6 %collective-permute-start.9 = (bf16[48,2048]{1,0:T(8,128)(2,1)S(1)}, bf16[48,2048]{1,0:T(8,128)(2,1)S(1)}, u32[]{:S(2)}, u32[]{:S(2)}) collective-permute-start(bf16[48,2048]{1,0:T(8,128)(2,1)S(1)} %get-tuple-element.91), channel_id=1, source_target_pairs={{0,1},{1,0},{2,3},{3,2},{4,5},{5,4},{6,7},{7,6},{8,9},{9,8},{10,11... | collective-permute-start | bytes 589832 | tf_op jit(solution)/shard_map/ppermute | solution.py:23
  44.7 15.9 %collective-permute-start.10 = (bf16[48,2048]{1,0:T(8,128)(2,1)S(1)}, bf16[48,2048]{1,0:T(8,128)(2,1)S(1)}, u32[]{:S(2)}, u32[]{:S(2)}) collective-permute-start(bf16[48,2048]{1,0:T(8,128)(2,1)S(1)} %get-tuple-element.92), channel_id=1, source_target_pairs={{0,2},{1,3},{2,0},{3,1},{4,6},{5,7},{6,4},{7,5},{8,10},{9,11},{10,... | collective-permute-start | bytes 589832 | tf_op jit(solution)/shard_map/ppermute | solution.py:23
  44.7 17.5 %collective-permute-start.11 = (bf16[48,2048]{1,0:T(8,128)(2,1)S(1)}, bf16[48,2048]{1,0:T(8,128)(2,1)S(1)}, u32[]{:S(2)}, u32[]{:S(2)}) collective-permute-start(bf16[48,2048]{1,0:T(8,128)(2,1)S(1)} %get-tuple-element.93), channel_id=1, source_target_pairs={{0,3},{1,2},{2,1},{3,0},{4,7},{5,6},{6,5},{7,4},{8,11},{9,10},{10,... | collective-permute-start | bytes 589832 | tf_op jit(solution)/shard_map/ppermute | solution.py:23
  58.9 11.8 %collective-permute-start.5 = (bf16[48,2048]{1,0:T(8,128)(2,1)S(1)}, bf16[48,2048]{1,0:T(8,128)(2,1)S(1)}, u32[]{:S(2)}, u32[]{:S(2)}) collective-permute-start(bf16[48,2048]{1,0:T(8,128)(2,1)S(1)} %get-tuple-element.88), channel_id=1, source_target_pairs={{0,1},{1,0},{2,3},{3,2},{4,5},{5,4},{6,7},{7,6},{8,9},{9,8},{10,11... | collective-permute-start | bytes 589832 | tf_op jit(solution)/shard_map/ppermute | solution.py:23
  60.1 16.3 %collective-permute-start.13 = (bf16[192,2304]{1,0:T(8,128)(2,1)S(1)}, bf16[192,2304]{1,0:T(8,128)(2,1)S(1)}, u32[]{:S(2)}, u32[]{:S(2)}) collective-permute-start(bf16[192,2304]{1,0:T(8,128)(2,1)S(1)} %get-tuple-element.100.refs_10_.refs_14_), channel_id=1, source_target_pairs={{0,8},{8,0},{16,24},{24,16},{1,9},{9,1},{17,25},{25,17},{2,10},{10... | collective-permute-start | bytes 2654216 | tf_op jit(solution)/shard_map/ppermute | solution.py:23
  60.1 15.4 %collective-permute-start.8 = (bf16[192,2048]{1,0:T(8,128)(2,1)S(1)}, bf16[192,2048]{1,0:T(8,128)(2,1)S(1)}, u32[]{:S(2)}, u32[]{:S(2)}) collective-permute-start(bf16[192,2048]{1,0:T(8,128)(2,1)S(1)} %get-tuple-element.84), channel_id=1, source_target_pairs={{0,8},{8,0},{16,24},{24,16},{1,9},{9,1},{17,25},{25,17},{2,10},{10... | collective-permute-start | bytes 2359304 | tf_op jit(solution)/shard_map/ppermute | solution.py:23
  72.7 12.6 %collective-permute-start.15 = (bf16[48,2048]{1,0:T(8,128)(2,1)S(1)}, bf16[48,2048]{1,0:T(8,128)(2,1)S(1)}, u32[]{:S(2)}, u32[]{:S(2)}) collective-permute-start(bf16[48,2048]{1,0:T(8,128)(2,1)S(1)} %get-tuple-element.111), channel_id=1, source_target_pairs={{0,3},{1,2},{2,1},{3,0},{4,7},{5,6},{6,5},{7,4},{8,11},{9,10},{10,... | collective-permute-start | bytes 589832 | tf_op jit(solution)/shard_map/ppermute | solution.py:23
  74.1 11.3 %collective-permute-start.16 = (bf16[48,2048]{1,0:T(8,128)(2,1)S(1)}, bf16[48,2048]{1,0:T(8,128)(2,1)S(1)}, u32[]{:S(2)}, u32[]{:S(2)}) collective-permute-start(bf16[48,2048]{1,0:T(8,128)(2,1)S(1)} %get-tuple-element.112), channel_id=1, source_target_pairs={{0,2},{1,3},{2,0},{3,1},{4,6},{5,7},{6,4},{7,5},{8,10},{9,11},{10,... | collective-permute-start | bytes 589832 | tf_op jit(solution)/shard_map/ppermute | solution.py:23
  76.4 19.0 %collective-permute-start.18 = (bf16[48,4096]{1,0:T(8,128)(2,1)S(1)}, bf16[48,4096]{1,0:T(8,128)(2,1)S(1)}, u32[]{:S(2)}, u32[]{:S(2)}) collective-permute-start(bf16[48,4096]{1,0:T(8,128)(2,1)S(1)} %get-tuple-element.118), channel_id=1, source_target_pairs={{0,3},{1,2},{2,1},{3,0},{4,7},{5,6},{6,5},{7,4},{8,11},{9,10},{10,... | collective-permute-start | bytes 1179656 | tf_op jit(solution)/shard_map/ppermute | solution.py:23
  79.2 23.7 %collective-permute-start.21 = (bf16[512,768]{1,0:T(8,128)(2,1)S(1)}, bf16[512,768]{1,0:T(8,128)(2,1)S(1)}, u32[]{:S(2)}, u32[]{:S(2)}) collective-permute-start(bf16[512,768]{1,0:T(8,128)(2,1)S(1)} %weight_sums.4), channel_id=1, source_target_pairs={{0,16},{8,24},{16,0},{24,8},{1,17},{9,25},{17,1},{25,9},{2,18},{10... | collective-permute-start | bytes 2359304 | tf_op jit(solution)/shard_map/ppermute | solution.py:23
  85.4 11.6 %collective-permute-start.19 = (bf16[192,768]{1,0:T(8,128)(2,1)S(1)}, bf16[192,768]{1,0:T(8,128)(2,1)S(1)}, u32[]{:S(2)}, u32[]{:S(2)}) collective-permute-start(bf16[192,768]{1,0:T(8,128)(2,1)S(1)} %get-tuple-element.108.refs_11_), channel_id=1, source_target_pairs={{0,8},{8,0},{16,24},{24,16},{1,9},{9,1},{17,25},{25,17},{2,10},{10... | collective-permute-start | bytes 884744 | tf_op jit(solution)/shard_map/ppermute | solution.py:23
  88.7 44.1 %collective-permute-start.25 = (bf16[128,2176]{1,0:T(8,128)(2,1)}, bf16[128,2176]{1,0:T(8,128)(2,1)}, u32[]{:S(2)}, u32[]{:S(2)}) collective-permute-start(bf16[128,2176]{1,0:T(8,128)(2,1)} %sum_slots.3), channel_id=1, source_target_pairs={{0,4},{1,5},{2,6},{3,7},{4,0},{5,1},{6,2},{7,3},{8,12},{9,13},{10,... | collective-permute-start | bytes 1671176 | tf_op jit(solution)/shard_map/ppermute | solution.py:23
  96.2 13.4 %collective-permute-start.22 = (bf16[48,2048]{1,0:T(8,128)(2,1)S(1)}, bf16[48,2048]{1,0:T(8,128)(2,1)S(1)}, u32[]{:S(2)}, u32[]{:S(2)}) collective-permute-start(bf16[48,2048]{1,0:T(8,128)(2,1)S(1)} %get-tuple-element.123), channel_id=1, source_target_pairs={{0,3},{1,2},{2,1},{3,0},{4,7},{5,6},{6,5},{7,4},{8,11},{9,10},{10,... | collective-permute-start | bytes 589832 | tf_op jit(solution)/shard_map/ppermute | solution.py:23
  96.2 16.7 %collective-permute-start.23 = (bf16[48,2048]{1,0:T(8,128)(2,1)S(1)}, bf16[48,2048]{1,0:T(8,128)(2,1)S(1)}, u32[]{:S(2)}, u32[]{:S(2)}) collective-permute-start(bf16[48,2048]{1,0:T(8,128)(2,1)S(1)} %get-tuple-element.124), channel_id=1, source_target_pairs={{0,2},{1,3},{2,0},{3,1},{4,6},{5,7},{6,4},{7,5},{8,10},{9,11},{10,... | collective-permute-start | bytes 589832 | tf_op jit(solution)/shard_map/ppermute | solution.py:23
  97.1 15.9 %collective-permute-start.24 = (bf16[48,2048]{1,0:T(8,128)(2,1)S(1)}, bf16[48,2048]{1,0:T(8,128)(2,1)S(1)}, u32[]{:S(2)}, u32[]{:S(2)}) collective-permute-start(bf16[48,2048]{1,0:T(8,128)(2,1)S(1)} %get-tuple-element.125), channel_id=1, source_target_pairs={{0,1},{1,0},{2,3},{3,2},{4,5},{5,4},{6,7},{7,6},{8,9},{9,8},{10,11... | collective-permute-start | bytes 589832 | tf_op jit(solution)/shard_map/ppermute | solution.py:23
  103.0 35.8 %collective-permute-start.26 = (bf16[512,1536]{1,0:T(8,128)(2,1)}, bf16[512,1536]{1,0:T(8,128)(2,1)S(1)}, u32[]{:S(2)}, u32[]{:S(2)}) collective-permute-start(bf16[512,1536]{1,0:T(8,128)(2,1)} %weight_sums.5), channel_id=1, source_target_pairs={{0,16},{8,24},{16,0},{24,8},{1,17},{9,25},{17,1},{25,9},{2,18},{10... | collective-permute-start | bytes 4718600 | tf_op jit(solution)/shard_map/ppermute | solution.py:23
  115.3 27.9 %collective-permute-start.29 = (bf16[128,2048]{1,0:T(8,128)(2,1)}, bf16[128,2048]{1,0:T(8,128)(2,1)}, u32[]{:S(2)}, u32[]{:S(2)}) collective-permute-start(bf16[128,2048]{1,0:T(8,128)(2,1)} %sum_slots.4), channel_id=1, source_target_pairs={{0,4},{1,5},{2,6},{3,7},{4,0},{5,1},{6,2},{7,3},{8,12},{9,13},{10,... | collective-permute-start | bytes 1572872 | tf_op jit(solution)/shard_map/ppermute | solution.py:23
  121.8 18.6 %collective-permute-start.27 = (bf16[48,4096]{1,0:T(8,128)(2,1)}, bf16[48,4096]{1,0:T(8,128)(2,1)S(1)}, u32[]{:S(2)}, u32[]{:S(2)}) collective-permute-start(bf16[48,4096]{1,0:T(8,128)(2,1)} %get-tuple-element.132), channel_id=1, source_target_pairs={{0,2},{1,3},{2,0},{3,1},{4,6},{5,7},{6,4},{7,5},{8,10},{9,11},{10,... | collective-permute-start | bytes 1179656 | tf_op jit(solution)/shard_map/ppermute | solution.py:23
  124.2 16.1 %collective-permute-start.28 = (bf16[48,4096]{1,0:T(8,128)(2,1)}, bf16[48,4096]{1,0:T(8,128)(2,1)}, u32[]{:S(2)}, u32[]{:S(2)}) collective-permute-start(bf16[48,4096]{1,0:T(8,128)(2,1)} %get-tuple-element.133), channel_id=1, source_target_pairs={{0,1},{1,0},{2,3},{3,2},{4,5},{5,4},{6,7},{7,6},{8,9},{9,8},{10,11... | collective-permute-start | bytes 1179656 | tf_op jit(solution)/shard_map/ppermute | solution.py:23
  (47 other events, 793.3 us)
